TPU v7x, 128 devices: a whole 4x4x4 slice. The times are simulated.
128 devices in a mesh: dp: 32 (over y, z, core), group: 4 (over x).
Axes of the slice: x: 4, y: 4, z: 4, core: 2. Of those that a mesh axis runs over, the one named last changes fastest.
Arguments:
- token_tiles: bfloat16 [32, 4, 64, 128, 128], P('dp', 'group'), may hold values from -6 to 6
- segment_ids: int32 [32, 4, 64, 128], P('dp', 'group'), may hold values from -1 to 34, as said below
- visible_flags: int32 [32, 4, 64, 128], P('dp', 'group'), may hold values 0 or 1
- tile_order: int32 [32, 4, 64], P('dp', 'group'), may hold values from 0 to 63, each once within a row
- mask_token: float32 [128], replicated, may hold values from -4 to 4
- norm_gains: float32 [2, 2, 128], replicated, may hold values from 0.25 to 1.75
- shift_terms: float32 [2, 4, 128], replicated, may hold values from -2 to 2
- attn_in: bfloat16 [2, 128, 384], replicated, may hold values from -0.5 to 0.5
- attn_out: bfloat16 [2, 128, 128], replicated, may hold values from -1.5 to 1.5
- mlp_in: bfloat16 [2, 128, 512], replicated, may hold values from -0.5 to 0.5
- hidden_shift: float32 [2, 512], replicated, may hold values from -2 to 2
- mlp_out: bfloat16 [2, 512, 128], replicated, may hold values from -0.25 to 0.25
- cotangent: bfloat16 [32, 4, 64, 128, 128], P('dp', 'group'), may hold values from -6 to 6
Outputs:
- decoded: bfloat16 [32, 4, 64, 128, 128], P('dp', 'group')
- tiles_grad: float32 [32, 4, 64, 128, 128], P('dp', 'group')
- mask_grad: float32 [128], replicated
- gains_grad: float32 [2, 2, 128], replicated
- shifts_grad: float32 [2, 4, 128], replicated
- attn_in_grad: float32 [2, 128, 384], replicated
- attn_out_grad: float32 [2, 128, 128], replicated
- mlp_in_grad: float32 [2, 128, 512], replicated
- hidden_grad: float32 [2, 512], replicated
- mlp_out_grad: float32 [2, 512, 128], replicated
Inputs may be any that keep to these rules, and one draw needn't show every extreme that they name: `segment_ids`: in each tile the slots of a series hold one id; series are numbered 0, 1, 2, ... from the tile's start, each of 3 to 24 slots, one of exactly 24 in every tile; slots after the last series are padding with id -1. `tile_order`: for every device, a permutation of the numbers of its 64 tiles.
All inputs are finite; a program needn't handle non-finite values. No bound on the sum of `visible_flags` on one device may be relied on, other than what follows from the above.
Results may differ from a plain program's by a relative error of at most 0.017.
Values may be sent and summed in bfloat16 or wider, within the bound.
No kernel may reach another device: no remote copies, remote signals or barrier semaphores. Data moves between devices by JAX's collectives and lax.ppermute only.
A program may use at most 256 MiB of HBM per device.

v0:
```python
import math

import jax
import jax.numpy as jnp
from jax import lax
from jax.sharding import PartitionSpec as P

HEADS = 8


epsilon = 1e-05


def layer_norm(values, gain_row, shift_row):
    center = values - jnp.mean(values, axis=-1, keepdims=True)
    spread = jnp.mean(center * center, axis=-1, keepdims=True)
    return center * lax.rsqrt(spread + epsilon) * gain_row + shift_row


def gelu_exact(values):
    return 0.5 * values * (1.0 + lax.erf(values * 0.7071067811865476))


def allowed_mask(segments, flag_rows, decoder):
    same_series = (segments[:, :, None] == segments[:, None, :]) & (segments[:, :, None] >= 0)
    if not decoder:
        same_series = same_series & (flag_rows[:, None, :] == 1)
    diagonal = jnp.eye(segments.shape[1], dtype=bool)
    return same_series | diagonal[None]


def blocked(array_in, group_size):
    return array_in.reshape((array_in.shape[0] // group_size, group_size) + array_in.shape[1:])


def unblocked(array_in):
    return array_in.reshape((-1,) + array_in.shape[2:])


def split_heads(packed):
    tile_count, slot_count, triple = packed.shape
    pieces = packed.reshape(tile_count, slot_count, 3, HEADS, triple // (3 * HEADS))
    return (pieces[:, :, 0], pieces[:, :, 1], pieces[:, :, 2])


def block_scores(query_blk, key_blk, allow_blk):
    head_scale = query_blk.shape[-1] ** (-0.5)
    scores = (
        jnp.einsum("bqhc,bkhc->bhqk", query_blk, key_blk, preferred_element_type=jnp.float32)
        * head_scale
    )
    return jnp.where(allow_blk[:, None], scores, -1e30)


def attend_forward(queries, key_rows, value_rows, allowed, group_size):

    def one_block(inputs):
        query_blk, key_blk, value_blk, allow_blk = inputs
        scores = block_scores(query_blk, key_blk, allow_blk)
        row_top = jnp.max(scores, axis=-1, keepdims=True)
        totals = jnp.sum(jnp.exp(scores - row_top), axis=-1, keepdims=True)
        log_total = row_top + jnp.log(totals)
        weights = jnp.exp(scores - log_total).astype(jnp.bfloat16)
        mixture = jnp.einsum(
            "bhqk,bkhc->bqhc", weights, value_blk, preferred_element_type=jnp.float32
        )
        return (mixture, log_total)

    mixture, log_total = lax.map(
        one_block,
        (
            blocked(queries, group_size),
            blocked(key_rows, group_size),
            blocked(value_rows, group_size),
            blocked(allowed, group_size),
        ),
    )
    return (unblocked(mixture), unblocked(log_total))


def attend_backward(queries, key_rows, value_rows, allowed, log_total, grad_mixture, group_size):

    def one_block(inputs):
        query_blk, key_blk, value_blk, allow_blk, total_blk, grad_blk = inputs
        head_scale = query_blk.shape[-1] ** (-0.5)
        scores = block_scores(query_blk, key_blk, allow_blk)
        probability = jnp.exp(scores - total_blk)
        weights = probability.astype(jnp.bfloat16)
        grad_value = jnp.einsum(
            "bhqk,bqhc->bkhc", weights, grad_blk, preferred_element_type=jnp.float32
        )
        grad_weights = jnp.einsum(
            "bqhc,bkhc->bhqk", grad_blk, value_blk, preferred_element_type=jnp.float32
        )
        inner = jnp.sum(probability * grad_weights, axis=-1, keepdims=True)
        grad_scores = (probability * (grad_weights - inner)).astype(jnp.bfloat16)
        grad_query = (
            jnp.einsum("bhqk,bkhc->bqhc", grad_scores, key_blk, preferred_element_type=jnp.float32)
            * head_scale
        )
        grad_key = (
            jnp.einsum(
                "bhqk,bqhc->bkhc", grad_scores, query_blk, preferred_element_type=jnp.float32
            )
            * head_scale
        )
        return (grad_query, grad_key, grad_value)

    grad_query, grad_key, grad_value = lax.map(
        one_block,
        (
            blocked(queries, group_size),
            blocked(key_rows, group_size),
            blocked(value_rows, group_size),
            blocked(allowed, group_size),
            blocked(log_total, group_size),
            blocked(grad_mixture, group_size),
        ),
    )
    return (unblocked(grad_query), unblocked(grad_key), unblocked(grad_value))


def layer_forward(stream, allowed, params, group_size):
    gain_pair, shift_four, attn_in, attn_out, mlp_in, hidden_shift, mlp_out = params
    normed = layer_norm(stream, gain_pair[0], shift_four[0]).astype(jnp.bfloat16)
    packed = jnp.einsum("tsd,de->tse", normed, attn_in, preferred_element_type=jnp.float32).astype(
        jnp.bfloat16
    )
    queries, key_rows, value_rows = split_heads(packed)
    mixture, log_total = attend_forward(queries, key_rows, value_rows, allowed, group_size)
    mixture = mixture.reshape(stream.shape).astype(jnp.bfloat16)
    branch = (
        jnp.einsum("tsd,de->tse", mixture, attn_out, preferred_element_type=jnp.float32)
        + shift_four[2]
    )
    middle = stream + branch
    second = layer_norm(middle, gain_pair[1], shift_four[1]).astype(jnp.bfloat16)
    hidden = (
        jnp.einsum("tsd,df->tsf", second, mlp_in, preferred_element_type=jnp.float32) + hidden_shift
    )
    active = gelu_exact(hidden).astype(jnp.bfloat16)
    output = middle + (
        jnp.einsum("tsf,fd->tsd", active, mlp_out, preferred_element_type=jnp.float32)
        + shift_four[3]
    )
    return (output, (stream, normed, packed, log_total, mixture, middle, second, hidden, active))


def layer_backward(grad_out, stored, allowed, params, group_size):
    gain_pair, shift_four, attn_in, attn_out, mlp_in, hidden_shift, mlp_out = params
    stream, normed, packed, log_total, mixture, middle, second, hidden, active = stored
    grad_low = grad_out.astype(jnp.bfloat16)
    grad_mlp_bias = jnp.sum(grad_low.astype(jnp.float32), axis=(0, 1))
    grad_mlp_out = jnp.einsum("tsf,tsd->fd", active, grad_low, preferred_element_type=jnp.float32)
    grad_active = jnp.einsum("tsd,fd->tsf", grad_low, mlp_out, preferred_element_type=jnp.float32)
    pull_gelu = jax.vjp(gelu_exact, hidden)[1]
    grad_hidden = pull_gelu(grad_active)[0].astype(jnp.bfloat16)
    grad_hidden_bias = jnp.sum(grad_hidden.astype(jnp.float32), axis=(0, 1))
    grad_mlp_in = jnp.einsum("tsd,tsf->df", second, grad_hidden, preferred_element_type=jnp.float32)
    grad_second = jnp.einsum("tsf,df->tsd", grad_hidden, mlp_in, preferred_element_type=jnp.float32)
    pull_second = jax.vjp(layer_norm, middle, gain_pair[1], shift_four[1])[1]
    middle_part, grad_gain_two, grad_shift_two = pull_second(grad_second)
    grad_middle = grad_out + middle_part
    grad_branch = grad_middle.astype(jnp.bfloat16)
    grad_attn_bias = jnp.sum(grad_branch.astype(jnp.float32), axis=(0, 1))
    grad_attn_out = jnp.einsum(
        "tsd,tse->de", mixture, grad_branch, preferred_element_type=jnp.float32
    )
    grad_mixture = jnp.einsum(
        "tse,de->tsd", grad_branch, attn_out, preferred_element_type=jnp.float32
    ).astype(jnp.bfloat16)
    queries, key_rows, value_rows = split_heads(packed)
    grad_query, grad_key, grad_value = attend_backward(
        queries,
        key_rows,
        value_rows,
        allowed,
        log_total,
        grad_mixture.reshape(queries.shape),
        group_size,
    )
    grad_packed = jnp.concatenate(
        [
            grad_query.reshape(stream.shape),
            grad_key.reshape(stream.shape),
            grad_value.reshape(stream.shape),
        ],
        axis=-1,
    ).astype(jnp.bfloat16)
    grad_attn_in = jnp.einsum(
        "tsd,tse->de", normed, grad_packed, preferred_element_type=jnp.float32
    )
    grad_normed = jnp.einsum(
        "tse,de->tsd", grad_packed, attn_in, preferred_element_type=jnp.float32
    )
    pull_first = jax.vjp(layer_norm, stream, gain_pair[0], shift_four[0])[1]
    stream_part, grad_gain_one, grad_shift_one = pull_first(grad_normed)
    grad_stream = grad_middle + stream_part
    gradients = (
        jnp.stack([grad_gain_one, grad_gain_two]),
        jnp.stack([grad_shift_one, grad_shift_two, grad_attn_bias, grad_mlp_bias]),
        grad_attn_in,
        grad_attn_out,
        grad_mlp_in,
        grad_hidden_bias,
        grad_mlp_out,
    )
    return (grad_stream, gradients)


def on_device(
    token_tiles,
    segment_ids,
    visible_flags,
    tile_order,
    mask_token,
    norm_gains,
    shift_terms,
    attn_in,
    attn_out,
    mlp_in,
    hidden_shift,
    mlp_out,
    cotangent,
):
    tile_count = token_tiles.shape[2]
    slot_count = token_tiles.shape[3]
    model_width = token_tiles.shape[4]
    group_size = math.gcd(tile_count, max(1, 512 // slot_count))
    tile_rows = token_tiles.reshape(tile_count, slot_count, model_width)
    segments = segment_ids.reshape(tile_count, slot_count)
    flag_rows = visible_flags.reshape(tile_count, slot_count)
    send_order = tile_order.reshape(tile_count)
    inverse = jnp.argsort(send_order)
    encoder_params = (
        norm_gains[0],
        shift_terms[0],
        attn_in[0],
        attn_out[0],
        mlp_in[0],
        hidden_shift[0],
        mlp_out[0],
    )
    decoder_params = (
        norm_gains[1],
        shift_terms[1],
        attn_in[1],
        attn_out[1],
        mlp_in[1],
        hidden_shift[1],
        mlp_out[1],
    )
    full_shape = (1, 1, tile_count, slot_count, model_width)
    encoder_allowed = allowed_mask(segments, flag_rows, False)
    encoded, encoder_stored = layer_forward(
        tile_rows.astype(jnp.float32), encoder_allowed, encoder_params, group_size
    )
    encoded = encoded.astype(jnp.bfloat16)
    cot_local = lax.all_to_all(
        cotangent.reshape(tile_count, slot_count, model_width),
        "dp",
        split_axis=0,
        concat_axis=0,
        tiled=True,
    )
    cot_local = jnp.take(cot_local, inverse, axis=0)
    shown = flag_rows[..., None] == 1
    decoder_in = jnp.where(shown, encoded.astype(jnp.float32), mask_token)
    decoder_allowed = allowed_mask(segments, flag_rows, True)
    decoded_local, decoder_stored = layer_forward(
        decoder_in, decoder_allowed, decoder_params, group_size
    )
    decoded = lax.all_to_all(
        jnp.take(decoded_local.astype(jnp.bfloat16), send_order, axis=0),
        "dp",
        split_axis=0,
        concat_axis=0,
        tiled=True,
    )
    grad_decoder_in, decoder_grads = layer_backward(
        cot_local.astype(jnp.float32), decoder_stored, decoder_allowed, decoder_params, group_size
    )
    grad_mask = jnp.sum(jnp.where(shown, 0.0, grad_decoder_in), axis=(0, 1))
    grad_encoded = jnp.where(shown, grad_decoder_in, 0.0).astype(jnp.bfloat16)
    grad_tiles, encoder_grads = layer_backward(
        grad_encoded.astype(jnp.float32),
        encoder_stored,
        encoder_allowed,
        encoder_params,
        group_size,
    )
    stacked = tuple(
        (jnp.stack([encoder_grads[index_k], decoder_grads[index_k]]) for index_k in range(7))
    )
    totals = lax.psum(stacked + (grad_mask,), ("dp", "group"))
    summed = totals[:7]
    grad_mask_sum = totals[7]
    return (
        decoded.reshape(full_shape),
        grad_tiles.reshape(full_shape),
        grad_mask_sum,
        summed[0],
        summed[1],
        summed[2],
        summed[3],
        summed[4],
        summed[5],
        summed[6],
    )


def solution(mesh):
    in_specs = (
        P("dp", "group", None, None, None),
        P("dp", "group", None, None),
        P("dp", "group", None, None),
        P("dp", "group", None),
        P(),
        P(),
        P(),
        P(),
        P(),
        P(),
        P(),
        P(),
        P("dp", "group", None, None, None),
    )
    out_specs = (
        P("dp", "group", None, None, None),
        P("dp", "group", None, None, None),
        P(),
        P(),
        P(),
        P(),
        P(),
        P(),
        P(),
        P(),
    )
    return jax.shard_map(
        on_device, mesh=mesh, in_specs=in_specs, out_specs=out_specs, check_vma=False
    )
```

profile of v0, /device:TPU:1, one launch (start us, length us, event | category | flops | bytes accessed | tf_op | source)
XLA Modules:
  0.0 956.4 jit_solution(4189286133647294044)
XLA Ops:
  7.2 9.7 %all-to-all-start.1 = ((bf16[64,128,128]{2,1,0:T(8,128)(2,1)}), bf16[64,128,128]{2,1,0:T(8,128)(2,1)}, u32[]{:S(2)}, u32[]{:S(2)}) async-start(bf16[64,128,128]{2,1,0:T(8,128)(2,1)} %bitcast.478), calls=%async_computation.1 | async-start | bytes 4194304 | tf_op jit(solution)/shard_map/all_to_all | solution.py:259
  17.0 3.3 copy.84
  21.7 4.7 convolution_convert_fusion.1
  26.5 8.6 copy.86
  35.1 7.1 fusion.167
  42.2 4.3 fusion.92
  48.3 62.2 %while.52 = (s32[]{:T(128)}, bf16[16,4,128,8,16]{2,4,3,1,0:T(8,128)(2,1)}, f32[16,4,8,128,1]{3,2,1,4,0:T(8,128)S(1)}, bf16[16,4,128,8,16]{2,4,3,1,0:T(8,128)(2,1...) while((s32[]{:T(128)}, ...), condition=%wide.region_5.6_spmd, body=%wide.region_2.5_spmd.sunk | while | flops 37220352 | bytes 7276637 | solution.py:69
  115.7 8.0 multiply_convert_fusion.3
  128.3 4.9 convolution_convert_fusion
  133.2 8.6 copy.92
  141.9 7.1 fusion.166
  150.8 75.7 %while.53 = (s32[]{:T(128)}, bf16[16,4,128,8,16]{2,4,3,1,0:T(8,128)(2,1)}, f32[16,4,8,128,1]{3,2,1,4,0:T(8,128)S(1)}, bf16[16,4,128,8,16]{2,4,3,1,0:T(8,128)(2,1...) while((s32[]{:T(128)}, ...), condition=%wide.region_13.14_spmd, body=%wide.region_10.13_spmd.sunk | while | flops 37220352 | bytes 7276637 | solution.py:69
  234.1 9.7 %multiply_convert_fusion.2 = (bf16[64,128,512]{2,1,0:T(8,128)(2,1)S(1)}, f32[64,128,512]{2,1,0:T(8,128)}) fusion(f32[512]{0:T(512)S(1)} %bitcast.484, bf16[2,128,512]{2,1,0:T(8,128)(2,1)S(1)} %copy-done.42, f32[64,128,128]{1,2,0:T(8,128)} %copy-done.3, f32[128]{0:T(128)S(1)} %get-tuple-element.351, f32[128]{0:T(128)S(1)} %get-tuple-element.383, ...), kind=kOutput, calls=%fused_computation.108 | convolution fusion | flops 1104150528 | bytes 29559808 | tf_op jit(solution)/shard_map/tsd,df->tsf/dot_general | solution.py:139
  247.0 4.3 add_convert_fusion.2
  251.3 3.8 gather_fusion
  255.1 3.2 broadcast_select_fusion.1
  258.3 7.4 all-to-all-start
  265.8 3.7 gather_fusion.1
  269.6 4.1 copy.97
  273.6 7.6 convolution_bitcast_fusion.4
  281.3 14.2 %convert_reduce_fusion = (f32[512]{0:T(512)}, bf16[64,128,512]{2,1,0:T(8,128)(2,1)S(1)}) fusion(bf16[2,512,128]{2,1,0:T(8,128)(2,1)S(1)} %copy-done.52, bf16[64,128,128]{1,2,0:T(8,128)(2,1)S(1)} %copy-done.22, pred[64]{0:T(512)(128)(4,1)S(1)} %compare_and_fusion.1, f32[64,128,512]{2,1,0:T(8,128)} %get-tuple-element.367, f32[512]{0:T(512)S(1)} %bitcast.485), kind=kOutput, calls=%fused_computation.104 | convolution fusion | flops 1141898752 | bytes 27398656 | tf_op jit(solution)/shard_map/tsd,fd->tsf/dot_general | solution.py:155
  295.4 4.9 fusion.171
  302.4 6.0 copy.99
  308.4 6.1 multiply_reduce_fusion.2
  326.0 175.0 %while.54 = (s32[]{:T(128)}, bf16[16,4,128,8,16]{2,4,3,1,0:T(8,128)(2,1)}, bf16[16,4,128,8,16]{2,4,3,1,0:T(8,128)(2,1)}, bf16[16,4,128,8,16]{2,4,3,1,0:T(8,128)(...) while((s32[]{:T(128)}, ...), condition=%wide.region_21.23_spmd, body=%wide.region_19.22_spmd.sunk | while | flops 88731648 | bytes 17716340 | solution.py:109
  501.0 4.1 copy.101
  505.0 4.1 copy.102
  509.1 4.1 copy.103
  513.2 6.7 fusion.172
  519.9 5.8 copy.104
  525.7 4.0 multiply_reduce_fusion.6
  532.5 4.9 multiply_reduce_fusion.3
  541.7 10.2 %convert_reduce_fusion.1 = (f32[512]{0:T(512)S(1)}, bf16[64,128,512]{2,1,0:T(8,128)(2,1)S(1)}) fusion(bf16[64,128,128]{1,2,0:T(8,128)(2,1)S(1)} %get-tuple-element.335, bf16[2,512,128]{2,1,0:T(8,128)(2,1)S(1)} %copy-done.52, f32[64,128,512]{2,1,0:T(8,128)S(1)} %bitcast.459, f32[512]{0:T(512)S(1)} %bitcast.483), kind=kOutput, calls=%fused_computation.105 | convolution fusion | flops 1140850176 | bytes 27398144 | tf_op jit(solution)/shard_map/tsd,fd->tsf/dot_general | solution.py:155
  553.4 4.4 fusion.173
  558.5 6.0 copy.107
  564.5 5.6 multiply_reduce_fusion.4
  585.4 176.4 %while.55 = (s32[]{:T(128)}, bf16[16,4,128,8,16]{2,4,3,1,0:T(8,128)(2,1)S(1)}, bf16[16,4,128,8,16]{2,4,3,1,0:T(8,128)(2,1)}, bf16[16,4,128,8,16]{2,4,3,1,0:T(8,1...) while((s32[]{:T(128)}, ...), condition=%wide.region_28.30_spmd, body=%wide.region_26.29_spmd.sunk | while | flops 88731648 | bytes 17716340 | solution.py:109
  764.7 4.2 copy.111
  768.9 4.2 copy.112
  773.2 5.0 fusion.111
  778.2 3.6 fusion.174
  781.9 5.7 copy.113
  791.7 3.4 fusion.84
  798.1 4.2 add_bitcast_fusion
  802.4 5.6 copy.125
  808.0 4.1 copy.124
  812.2 67.4 %all-reduce = (f32[128]{0:T(128)}, f32[2,2,128]{2,1,0:T(2,128)}, f32[2,4,128]{2,1,0:T(4,128)}, f32[2,512]{1,0:T(2,128)}) all-reduce(f32[128]{0:T(128)S(1)} %get-tuple-element.232, f32[2,2,128]{2,1,0:T(2,128)S(1)} %pad_maximum_fusion.16, f32[2,4,128]{2,1,0:T(4,128)S(1)} %pad_maximum_fusion.14, ...), channel_id=1, replica_groups=mesh['dp'=32,'group'=4] {'dp','group'}, use_global_device_ids=true, to_apply=%region_32.34 | all-reduce | flops 2688 | bytes 21504 | tf_op jit(solution)/shard_map/psum | solution.py:295
  879.7 62.6 %all-reduce.4.cloned.1.call-done = (f32[2,128,384]{2,1,0:T(8,128)}, f32[2,128,128]{2,1,0:T(8,128)}, f32[2,128,512]{2,1,0:T(8,128)}, f32[2,512,128]{2,1,0:T(8,128)}) async-done(((f32[2,128,384]{2,1,0:T(8,128)}, f32[2,128,128]{2,1,0:T(8,128)}, f32[2,128,512]{2,1,0:T(8,128)}, f32[2,512,128]{2,1,0:T(8,128)}), (f32[2,128,384]{2,1,0:T(8,128)}, f32[2,128,128]{2,1,0:T(8,128)}, f32[2,128,512]{2,1,0:T(8,128)}, ...) | async-done | bytes 1572880 | tf_op jit(solution)/shard_map/psum | solution.py:295
  (672 shorter events, 568.5 us)
Async XLA Ops:
  7.2 9.7 %copy-start.58 = (s32[1,1,64,128]{3,2,1,0:T(8,128)S(1)}, s32[1,1,64,128]{3,2,1,0:T(8,128)}, u32[]{:S(2)}) copy-start(s32[1,1,64,128]{3,2,1,0:T(8,128)} %param.25) | copy-start | bytes 98308
  7.2 251.1 %all-to-all-start.1 = ((bf16[64,128,128]{2,1,0:T(8,128)(2,1)}), bf16[64,128,128]{2,1,0:T(8,128)(2,1)}, u32[]{:S(2)}, u32[]{:S(2)}) async-start(bf16[64,128,128]{2,1,0:T(8,128)(2,1)} %bitcast.478), calls=%async_computation.1 | async-start | bytes 4194304 | tf_op jit(solution)/shard_map/all_to_all | solution.py:259
  20.2 90.3 %copy-start.7 = (bf16[1,1,64,128,128]{3,4,2,1,0:T(8,128)(2,1)}, bf16[1,1,64,128,128]{3,4,2,1,0:T(8,128)(2,1)S(1)}, u32[]{:S(2)}) copy-start(bf16[1,1,64,128,128]{3,4,2,1,0:T(8,128)(2,1)S(1)} %copy.84) | copy-start | bytes 6291460
  21.6 4.9 copy-start.47
  21.7 4.8 copy-start.44
  21.7 94.0 %copy-start.60 = (f32[128]{0:T(128)}, f32[128]{0:T(128)S(1)}, u32[]{:S(2)}) copy-start(f32[128]{0:T(128)S(1)} %get-tuple-element.382) | copy-start | bytes 1540
  21.7 94.0 %copy-start.66 = (f32[128]{0:T(128)}, f32[128]{0:T(128)S(1)}, u32[]{:S(2)}) copy-start(f32[128]{0:T(128)S(1)} %get-tuple-element.348) | copy-start | bytes 1540
  21.7 106.6 %copy-start.73 = (f32[128]{0:T(128)}, f32[128]{0:T(128)S(1)}, u32[]{:S(2)}) copy-start(f32[128]{0:T(128)S(1)} %get-tuple-element.346) | copy-start | bytes 1540
  35.1 7.1 copy-start.51
  48.3 62.9 %copy-start.53 = (bf16[2,128,128]{2,1,0:T(8,128)(2,1)S(1)}, bf16[2,128,128]{2,1,0:T(8,128)(2,1)}, u32[]{:S(2)}) copy-start(bf16[2,128,128]{2,1,0:T(8,128)(2,1)} %param.31) | copy-start | bytes 196612
  113.7 10.1 %copy-start = (f32[64,128,128]{1,2,0:T(8,128)}, f32[64,128,128]{1,2,0:T(8,128)S(1)}, u32[]{:S(2)}) copy-start(f32[64,128,128]{1,2,0:T(8,128)S(1)} %get-tuple-element.359) | copy-start | bytes 12582916
  113.7 10.0 %copy-start.36 = (f32[64,128]{1,0:T(8,128)}, f32[64,128]{1,0:T(8,128)S(1)}, u32[]{:S(2)}) copy-start(f32[64,128]{1,0:T(8,128)S(1)} %broadcast_multiply_fusion.2) | copy-start | bytes 98308
  114.7 9.1 copy-start.38
  114.7 9.0 copy-start.62
  115.7 8.1 copy-start.52
  115.7 8.1 copy-start.59
  234.1 12.9 %copy-start.4 = (f32[64,128,128]{1,2,0:T(8,128)S(1)}, f32[64,128,128]{1,2,0:T(8,128)}, u32[]{:S(2)}) copy-start(f32[64,128,128]{1,2,0:T(8,128)} %copy-done.3) | copy-start | bytes 12582916
  258.3 549.7 %all-to-all-start = ((bf16[64,128,128]{1,2,0:T(8,128)(2,1)}), bf16[64,128,128]{1,2,0:T(8,128)(2,1)}, u32[]{:S(2)}, u32[]{:S(2)}) async-start(bf16[64,128,128]{1,2,0:T(8,128)(2,1)} %broadcast_select_fusion.1), calls=%async_computation | async-start | bytes 4194304 | tf_op jit(solution)/shard_map/all_to_all | solution.py:273
  265.8 676.5 %all-reduce.4.cloned.1.call-start = ((), (), s32[]{:S(2)}) async-start(), calls=%async_computation.2 | async-start | bytes 3145728 | tf_op jit(solution)/shard_map/psum | solution.py:295
  273.6 7.6 copy-start.22
  295.4 4.9 copy-start.5
  308.4 6.2 copy-start.6
  308.4 6.2 copy-start.17
  318.4 5.7 copy-start.19
  529.7 7.7 slice-start
  532.5 4.9 slice-start.1
  532.5 8.0 slice-start.2
  532.5 8.1 slice-start.3
  541.7 10.3 %copy-start.1 = (f32[64,128,128]{1,2,0:T(8,128)S(1)}, f32[64,128,128]{1,2,0:T(8,128)}, u32[]{:S(2)}) copy-start(f32[64,128,128]{1,2,0:T(8,128)} %copy-done) | copy-start | bytes 12582916
  541.7 10.3 %copy-start.37 = (f32[64,128]{1,0:T(8,128)S(1)}, f32[64,128]{1,0:T(8,128)}, u32[]{:S(2)}) copy-start(f32[64,128]{1,0:T(8,128)} %copy-done.36) | copy-start | bytes 98308
  541.7 10.3 %copy-start.39 = (f32[64,128]{1,0:T(8,128)S(1)}, f32[64,128]{1,0:T(8,128)}, u32[]{:S(2)}) copy-start(f32[64,128]{1,0:T(8,128)} %copy-done.38) | copy-start | bytes 98308
  541.7 10.3 %copy-start.61 = (f32[128]{0:T(128)S(1)}, f32[128]{0:T(128)}, u32[]{:S(2)}) copy-start(f32[128]{0:T(128)} %copy-done.60) | copy-start | bytes 1540
  541.7 10.3 %copy-start.67 = (f32[128]{0:T(128)S(1)}, f32[128]{0:T(128)}, u32[]{:S(2)}) copy-start(f32[128]{0:T(128)} %copy-done.66) | copy-start | bytes 1540
  564.5 5.6 copy-start.50
  564.5 5.7 copy-start.2
  564.5 5.9 copy-start.18
  764.7 8.5 copy-start.8
  764.7 8.5 copy-start.41
  764.7 8.5 copy-start.45
  764.7 8.5 copy-start.65
  764.7 8.5 copy-start.72
  773.2 5.0 copy-start.33
  773.2 5.0 copy-start.34
  773.2 5.0 copy-start.35
  781.9 5.7 copy-start.54
  781.9 5.7 copy-start.55
  781.9 6.5 copy-start.43
  789.9 5.2 copy-start.48
  (41 other events, 130.9 us)
Sparse Core Ops, SparseCore 0:
  791.8 150.3 all-reduce.3
where the time goes:
time: 974 us; the launch traced here: 956 us
  matrix products  520 us (53%)
  local copies, waits for them, and re-layouts  188 us (19%)
  other arithmetic  84.5 us (9%)
  blocking collectives  67.4 us (7%)
  waiting for transfers between devices  62.6 us (6%)
  starting transfers between devices  17.2 us (2%)
  between operations  15.5 us (2%)
    dot_general x64, matrix products, block_scores(): jnp.einsum('bqhc,bkhc->bhqk', query_blk, key_blk, preferred_element_type=...  106 us
    dot_general x32, matrix products, one_block(): jnp.einsum('bhqk,bqhc->bkhc', grad_scores, query_blk, preferred_element_t...  71.3 us
    dot_general x32, matrix products, one_block(): jnp.einsum('bhqk,bqhc->bkhc', weights, grad_blk, preferred_element_type=j...  71.1 us
    psum x1, blocking collectives, on_device(): totals = lax.psum(stacked + (grad_mask,), ('dp', 'group'))  67.4 us
    dot_general x32, matrix products, one_block(): jnp.einsum('bhqk,bkhc->bqhc', weights, value_blk, preferred_element_type=...  63.1 us
    psum x1, waiting for transfers between devices, on_device(): totals = lax.psum(stacked + (grad_mask,), ('dp', 'group'))  62.6 us
    dot_general x32, matrix products, one_block(): jnp.einsum('bhqk,bkhc->bqhc', grad_scores, key_blk, preferred_element_typ...  52 us
    dot_general x32, matrix products, one_block(): jnp.einsum('bqhc,bkhc->bhqk', grad_blk, value_blk, preferred_element_type...  46.4 us
  transfers between devices with their start and end apart: 3, of which 1 were waited for; matrix products, arithmetic and copies ran while one was open for 81% of the time, Pallas kernels for 0%

commit v1 on v0

v1 whole, which is shorter than its diff:
```python
import jax
import jax.numpy as jnp
from jax import lax
from jax.experimental import pallas as pl
from jax.experimental.pallas import tpu as pltpu
from jax.sharding import PartitionSpec as P

HEADS = 8
HEAD = 16
D = 128
FF = 512
S = 128
NT = 2
L = NT * S
EPS = 1e-5
LOG2E = 1.4426950408889634
LN2 = 0.6931471805599453
F32 = jnp.float32
BF = jnp.bfloat16


def nn(a, b):
    return lax.dot_general(a, b, (((1,), (0,)), ((), ())), preferred_element_type=F32)


def nt(a, b):
    return lax.dot_general(a, b, (((1,), (1,)), ((), ())), preferred_element_type=F32)


def wide(col):
    return jnp.concatenate([col] * NT, axis=1)


def fold(val):
    out = val[:, :S]
    for t in range(1, NT):
        out = out + val[:, t * S:(t + 1) * S]
    return out


def normalize(x):
    center = x - jnp.sum(x, axis=0, keepdims=True) * (1.0 / D)
    var = jnp.sum(center * center, axis=0, keepdims=True) * (1.0 / D)
    rstd = lax.rsqrt(var + EPS)
    return center * rstd, rstd


def norm_back(grad, xhat, rstd, gain):
    gx = grad * gain
    m1 = jnp.sum(gx, axis=0, keepdims=True) * (1.0 / D)
    m2 = jnp.sum(gx * xhat, axis=0, keepdims=True) * (1.0 / D)
    return (gx - m1 - xhat * m2) * rstd


def padded(rows, h):
    parts = []
    if h > 0:
        parts.append(jnp.zeros((HEAD * h, S), BF))
    parts.append(rows)
    if h < HEADS - 1:
        parts.append(jnp.zeros((D - HEAD * (h + 1), S), BF))
    return jnp.concatenate(parts, axis=0)


def layer_fwd(l, x, biases, w, scr):
    cols, hid, wi_t, wi, wo_t, wo, m1_t, m1, m2_t, m2 = w
    e_ref, p_ref, inv_ref, o_ref, u_ref, gp_ref = scr
    xhat0, rstd0 = normalize(x)
    a = (xhat0 * wide(cols[l, 0]) + wide(cols[l, 2])).astype(BF)
    p = nn(wi_t[l], a)
    p_ref[l, 0:D, :] = (p[0:D] * (0.25 * LOG2E)).astype(BF)
    p_ref[l, D:3 * D, :] = p[D:3 * D].astype(BF)
    ones = jnp.ones((HEAD, S), BF)
    for t in range(NT):
        sl = slice(t * S, (t + 1) * S)
        keys = jnp.transpose(p_ref[l, D:2 * D, sl])
        for h in range(HEADS):
            hs = slice(HEAD * h, HEAD * (h + 1))
            s = nn(keys, padded(p_ref[l, hs, sl], h)) + biases[t]
            e = jnp.exp2(s - jnp.max(s, axis=0, keepdims=True)).astype(BF)
            e_ref[l, t, h] = e
            v = p_ref[l, 2 * D + HEAD * h:2 * D + HEAD * (h + 1), sl]
            o = nn(jnp.concatenate([v, ones], axis=0), e)
            inv = 1.0 / o[HEAD:HEAD + 8]
            inv_ref[l, 8 * h:8 * h + 8, sl] = inv
            o_ref[l, hs, sl] = o[0:HEAD] * jnp.concatenate([inv, inv], axis=0)
    ob = o_ref[l].astype(BF)
    x1 = x + nn(wo_t[l], ob) + wide(cols[l, 4])
    xhat1, rstd1 = normalize(x1)
    b = (xhat1 * wide(cols[l, 1]) + wide(cols[l, 3])).astype(BF)
    hidden = nn(m1_t[l], b) + wide(hid[l])
    cdf = 0.5 * lax.erf(hidden * 0.7071067811865476) + 0.5
    u = (hidden * cdf).astype(BF)
    u_ref[l] = u
    phi = jnp.exp2(hidden * hidden * (-0.5 * LOG2E)) * 0.3989422804014327
    gp_ref[l] = (cdf + hidden * phi).astype(BF)
    x2 = x1 + nn(m2_t[l], u) + wide(cols[l, 5])
    return x2, (xhat0, rstd0, a, ob, xhat1, rstd1, b)


def layer_bwd(l, g2, saved, w, scr, acc):
    cols, hid, wi_t, wi, wo_t, wo, m1_t, m1, m2_t, m2 = w
    e_ref, p_ref, inv_ref, o_ref, u_ref, gp_ref = scr
    a_vec, a_hid, a_wi, a_wo, a_m1, a_m2 = acc
    xhat0, rstd0, a, ob, xhat1, rstd1, b = saved
    gz = g2.astype(BF)
    a_vec[l, 5] += fold(g2)
    a_m2[l] += nt(u_ref[l], gz)
    gh = nn(m2[l], gz) * gp_ref[l].astype(F32)
    a_hid[l] += fold(gh)
    ghb = gh.astype(BF)
    a_m1[l] += nt(ghb, b)
    gb = nn(m1[l], ghb)
    a_vec[l, 1] += fold(gb * xhat1)
    a_vec[l, 3] += fold(gb)
    g1 = g2 + norm_back(gb, xhat1, rstd1, wide(cols[l, 1]))
    gy = g1.astype(BF)
    a_vec[l, 4] += fold(g1)
    a_wo[l] += nt(ob, gy)
    go = nn(wo[l], gy)
    gps = []
    for t in range(NT):
        sl = slice(t * S, (t + 1) * S)
        values = jnp.transpose(p_ref[l, 2 * D:3 * D, sl])
        gq, gk, gv = [], [], []
        for h in range(HEADS):
            hs = slice(HEAD * h, HEAD * (h + 1))
            inv = inv_ref[l, 8 * h:8 * h + 8, sl]
            gob = (go[hs, sl] * jnp.concatenate([inv, inv], axis=0)).astype(BF)
            r = jnp.sum(gob.astype(F32) * o_ref[l, hs, sl], axis=0, keepdims=True)
            e = e_ref[l, t, h]
            gs = (e.astype(F32) * (nn(values, padded(gob, h)) - r)).astype(BF)
            gv.append(nt(gob, e))
            gq.append(nn(p_ref[l, D + HEAD * h:D + HEAD * (h + 1), sl], gs) * 0.25)
            gk.append(nt(p_ref[l, hs, sl], gs) * LN2)
        gps.append(jnp.concatenate(gq + gk + gv, axis=0).astype(BF))
    gp = jnp.concatenate(gps, axis=1)
    a_wi[l] += nt(gp, a)
    ga = nn(wi[l], gp)
    a_vec[l, 0] += fold(ga * xhat0)
    a_vec[l, 2] += fold(ga)
    return g1 + norm_back(ga, xhat0, rstd0, wide(cols[l, 0]))


def kernel(inv_order, x_ref, *rest):
    cots = rest[:NT]
    (seg_ref, vis_ref, cols, hid, maskcol, wi_t, wi, wo_t, wo, m1_t, m1, m2_t, m2,
     dec_ref, tg_ref, o_m2, o_m1, o_wi, o_wo, o_row,
     a_vec, a_mask, a_hid, a_m2, a_m1, a_wi, a_wo,
     e_ref, p_ref, i_ref, o_ref, u_ref, gp_ref) = rest[NT:]
    step = pl.program_id(0)
    acc = (a_vec, a_hid, a_wi, a_wo, a_m1, a_m2)

    @pl.when(step == 0)
    def _():
        for ref in acc + (a_mask,):
            ref[...] = jnp.zeros_like(ref)

    w = (cols, hid, wi_t, wi, wo_t, wo, m1_t, m1, m2_t, m2)
    scr = (e_ref, p_ref, i_ref, o_ref, u_ref, gp_ref)
    rows_i = lax.broadcasted_iota(jnp.int32, (S, S), 0)
    cols_i = lax.broadcasted_iota(jnp.int32, (S, S), 1)
    diag = rows_i == cols_i
    eye = diag.astype(F32).astype(BF)
    bias_e, bias_d = [], []
    for t in range(NT):
        seg = seg_ref[0, t:t + 1, :]
        vis = vis_ref[0, t:t + 1, :]
        code = jnp.where(seg >= 0, seg, -2) * 2 + jnp.where(vis == 1, 1, 0)
        code_k = jnp.transpose(jnp.broadcast_to(code, (S, S)).astype(F32))
        diff = code_k - (2 * seg).astype(F32)
        bias_e.append(jnp.where((diff == 1.0) | diag, 0.0, -1e30))
        bias_d.append(jnp.where((diff == 1.0) | (diff == 0.0) | diag, 0.0, -1e30))
    x = jnp.concatenate([nt(eye, x_ref[t]) for t in range(NT)], axis=1)
    enc, saved_e = layer_fwd(0, x, bias_e, w, scr)
    shown = jnp.concatenate([vis_ref[0, t:t + 1, :] for t in range(NT)], axis=1) == 1
    dec_in = jnp.where(shown, enc.astype(BF).astype(F32), wide(maskcol[...]))
    dec, saved_d = layer_fwd(1, dec_in, bias_d, w, scr)
    decb = dec.astype(BF)
    for t in range(NT):
        dec_ref[t] = nt(eye, decb[:, t * S:(t + 1) * S]).astype(BF)
    g = jnp.concatenate([nt(eye, c[0]) for c in cots], axis=1)
    g = layer_bwd(1, g, saved_d, w, scr, acc)
    a_mask[...] += fold(jnp.where(shown, 0.0, g))
    g = jnp.where(shown, g, 0.0).astype(BF).astype(F32)
    g = layer_bwd(0, g, saved_e, w, scr, acc)
    for t in range(NT):
        tg_ref[t] = jnp.transpose(g[:, t * S:(t + 1) * S])

    @pl.when(step == pl.num_programs(0) - 1)
    def _():
        o_m2[...] = a_m2[...]
        o_wo[...] = a_wo[...]
        for l in range(2):
            o_m1[l] = jnp.transpose(a_m1[l])
            o_wi[l] = jnp.transpose(a_wi[l])
            for j in range(6):
                o_row[6 * l + j:6 * l + j + 1, :] = jnp.sum(jnp.transpose(a_vec[l, j]), axis=0, keepdims=True)
            for j in range(4):
                o_row[12 + 4 * l + j:13 + 4 * l + j, :] = jnp.sum(
                    jnp.transpose(a_hid[l, j * D:(j + 1) * D]), axis=0, keepdims=True)
        o_row[20:21, :] = jnp.sum(jnp.transpose(a_mask[...]), axis=0, keepdims=True)
        o_row[21:24, :] = jnp.zeros((3, D), F32)


def local_compute(x, seg, vis, inv_order, cot, cols, hid, maskcol, weights):
    tiles = x.shape[0]
    steps = tiles // NT
    const = lambda shape: pl.BlockSpec(shape, lambda i, o: (0,) * len(shape))
    in_specs = [pl.BlockSpec((NT, S, D), lambda i, o: (i, 0, 0))]
    for t in range(NT):
        in_specs.append(pl.BlockSpec((1, S, D), lambda i, o, t=t: (o[NT * i + t], 0, 0)))
    in_specs += [pl.BlockSpec((1, NT, S), lambda i, o: (i, 0, 0))] * 2
    consts = (cols, hid, maskcol) + weights
    in_specs += [const(c.shape) for c in consts]
    out_shape = [
        jax.ShapeDtypeStruct((tiles, S, D), BF),
        jax.ShapeDtypeStruct((tiles, S, D), F32),
        jax.ShapeDtypeStruct((2, FF, D), F32),
        jax.ShapeDtypeStruct((2, D, FF), F32),
        jax.ShapeDtypeStruct((2, D, 3 * D), F32),
        jax.ShapeDtypeStruct((2, D, D), F32),
        jax.ShapeDtypeStruct((24, D), F32),
    ]
    out_specs = [pl.BlockSpec((NT, S, D), lambda i, o: (i, 0, 0))] * 2
    out_specs += [const(o.shape) for o in out_shape[2:]]
    scratch = [
        pltpu.VMEM((2, 6, D, S), F32),
        pltpu.VMEM((D, S), F32),
        pltpu.VMEM((2, FF, S), F32),
        pltpu.VMEM((2, FF, D), F32),
        pltpu.VMEM((2, FF, D), F32),
        pltpu.VMEM((2, 3 * D, D), F32),
        pltpu.VMEM((2, D, D), F32),
        pltpu.VMEM((2, NT, HEADS, S, S), BF),
        pltpu.VMEM((2, 3 * D, L), BF),
        pltpu.VMEM((2, 8 * HEADS, L), F32),
        pltpu.VMEM((2, D, L), F32),
        pltpu.VMEM((2, FF, L), BF),
        pltpu.VMEM((2, FF, L), BF),
    ]
    return pl.pallas_call(
        kernel,
        grid_spec=pltpu.PrefetchScalarGridSpec(
            num_scalar_prefetch=1,
            grid=(steps,),
            in_specs=in_specs,
            out_specs=out_specs,
            scratch_shapes=scratch,
        ),
        out_shape=out_shape,
        compiler_params=pltpu.CompilerParams(
            dimension_semantics=("arbitrary",), vmem_limit_bytes=56 * 1024 * 1024
        ),
    )(inv_order, x, *([cot] * NT), seg.reshape(steps, NT, S), vis.reshape(steps, NT, S), *consts)


def prepare(mask_token, norm_gains, shift_terms, attn_in, attn_out, mlp_in, hidden_shift, mlp_out):
    rows = jnp.concatenate([norm_gains, shift_terms], axis=1)
    cols = jnp.broadcast_to(rows[..., None], (2, 6, D, S))
    hid = jnp.broadcast_to(hidden_shift[..., None], (2, FF, S))
    maskcol = jnp.broadcast_to(mask_token[:, None], (D, S))
    tr = lambda v: jnp.swapaxes(v, 1, 2)
    weights = (tr(attn_in), attn_in, tr(attn_out), attn_out, tr(mlp_in), mlp_in, tr(mlp_out), mlp_out)
    return cols, hid, maskcol, weights


def on_device(token_tiles, segment_ids, visible_flags, tile_order, mask_token, norm_gains, shift_terms,
              attn_in, attn_out, mlp_in, hidden_shift, mlp_out, cotangent):
    tiles = token_tiles.shape[2]
    full_shape = (1, 1, tiles, S, D)
    order = tile_order.reshape(tiles)
    spots = jnp.arange(tiles, dtype=jnp.int32)
    inv_order = jnp.sum(jnp.where(order[None, :] == spots[:, None], spots[None, :], 0), axis=1).astype(jnp.int32)
    cot = lax.all_to_all(cotangent.reshape(tiles, S, D), "dp", split_axis=0, concat_axis=0, tiled=True)
    cols, hid, maskcol, weights = prepare(
        mask_token, norm_gains, shift_terms, attn_in, attn_out, mlp_in, hidden_shift, mlp_out)
    dec, tg, g_m2, g_m1, g_wi, g_wo, rows = local_compute(
        token_tiles.reshape(tiles, S, D), segment_ids.reshape(tiles, S), visible_flags.reshape(tiles, S),
        inv_order, cot, cols, hid, maskcol, weights)
    decoded = lax.all_to_all(jnp.take(dec, order, axis=0), "dp", split_axis=0, concat_axis=0, tiled=True)
    g_m2, g_m1, g_wi, g_wo, rows = lax.psum((g_m2, g_m1, g_wi, g_wo, rows), ("dp", "group"))
    vec = rows[0:12].reshape(2, 6, D)
    return (
        decoded.reshape(full_shape),
        tg.reshape(full_shape),
        rows[20],
        vec[:, 0:2],
        vec[:, 2:6],
        g_wi,
        g_wo,
        g_m1,
        rows[12:20].reshape(2, FF),
        g_m2,
    )


def solution(mesh):
    tile5 = P("dp", "group", None, None, None)
    in_specs = (tile5, P("dp", "group", None, None), P("dp", "group", None, None), P("dp", "group", None),
                P(), P(), P(), P(), P(), P(), P(), P(), tile5)
    out_specs = (tile5, tile5) + (P(),) * 8
    return jax.shard_map(on_device, mesh=mesh, in_specs=in_specs, out_specs=out_specs, check_vma=False)
```

time: 974 us -> 585 us (0.60); the launches traced: 956 us -> 585 us
  matrix products: 520 us -> 0 us
  Pallas kernels: 0 us -> 353 us
  local copies, waits for them, and re-layouts: 188 us -> 15.5 us
  other arithmetic: 84.5 us -> 2.23 us
  waiting for transfers between devices: 62.6 us -> 102 us
  blocking collectives: 67.4 us -> 82.7 us
    dot_general x248 -> x0, matrix products: 520 us -> none  [the longest x64 106 us: block_scores(): jnp.einsum('bqhc,bkhc->bhqk', query_blk, key_blk, preferred_element_type=...]
    pallas_call x0 -> x1, Pallas kernels: none -> 353 us  [local_compute(): pl.pallas_call(kernel, grid_spec=pltpu.PrefetchScalarGridSpec(num_scalar_...]
    reduce_sum x48 -> x1, other arithmetic: 51.8 us -> 0.63 us  [on_device(): jnp.sum(jnp.where(order[None, :] == spots[:, None], spots[None, :], 0), a...]
    broadcast_in_dim x64 -> x3, local copies, waits for them, and re-layouts: 40.9 us -> 3.08 us  [the longest x1 1.38 us: prepare(): cols = jnp.broadcast_to(rows[..., None], (2, 6, D, S))]
    another operation x16 -> x0, local copies, waits for them, and re-layouts: 37 us -> none
    unnamed x179 -> x39, local copies, waits for them, and re-layouts: 32.5 us -> 7.61 us
    all_to_all x2, waiting for transfers between devices: 0.01 us -> 24.3 us  [the longest x1 24.3 us: on_device(): lax.all_to_all(cotangent.reshape(tiles, S, D), 'dp', split_axis=0, concat...]
    dot_general x4 -> x0, local copies, waits for them, and re-layouts: 23.4 us -> none  [the longest x2 12 us: layer_backward(): jnp.einsum('tsf,df->tsd', grad_hidden, mlp_in, preferred_element_type=jnp...]
  transfers between devices with their start and end apart: 3 -> 3, of which waited for: 1 -> 2; matrix products, arithmetic and copies ran while one was open for 81% -> 1% of each run, Pallas kernels for 0% -> 0%
where the time goes in v1:
time: 585 us
  Pallas kernels  353 us (60%)
  waiting for transfers between devices  102 us (17%)
  blocking collectives  82.7 us (14%)
  local copies, waits for them, and re-layouts  15.5 us (3%)
  starting transfers between devices  14.5 us (2%)
  between operations  14.2 us (2%)
    pallas_call x1, Pallas kernels, local_compute(): pl.pallas_call(kernel, grid_spec=pltpu.PrefetchScalarGridSpec(num_scalar_...  353 us
    psum x1, blocking collectives, on_device(): lax.psum((g_m2, g_m1, g_wi, g_wo, rows), ('dp', 'group'))  82.7 us
    psum x1, waiting for transfers between devices, on_device(): lax.psum((g_m2, g_m1, g_wi, g_wo, rows), ('dp', 'group'))  76.9 us
    all_to_all x1, waiting for transfers between devices, on_device(): lax.all_to_all(cotangent.reshape(tiles, S, D), 'dp', split_axis=0, concat...  24.3 us
  transfers between devices with their start and end apart: 3, of which 2 were waited for; matrix products, arithmetic and copies ran while one was open for 1% of the time, Pallas kernels for 0%

profile of v1, /device:TPU:1, one launch (start us, length us, event | category | flops | bytes accessed | tf_op | source)
XLA Modules:
  0.0 584.6 jit_solution(16845562245979123797)
XLA Ops:
  7.2 0.0 copy-start.1
  7.2 0.0 copy-start.2
  7.2 0.0 copy-start.3
  7.2 0.0 copy-start.7
  7.2 0.0 copy-start.14
  7.2 0.0 copy-start.11
  7.2 0.0 copy-start.12
  7.3 9.7 %all-to-all-start = ((bf16[64,128,128]{2,1,0:T(8,128)(2,1)}), bf16[64,128,128]{2,1,0:T(8,128)(2,1)S(1)}, u32[]{:S(2)}, u32[]{:S(2)}) async-start(bf16[64,128,128]{2,1,0:T(8,128)(2,1)} %bitcast.19), calls=%async_computation | async-start | bytes 4194304 | tf_op jit(solution)/shard_map/all_to_all | solution.py:275
  17.0 0.0 copy-done.1
  17.0 0.0 copy-start.10
  17.0 0.0 copy-start.13
  17.0 0.8 copy.33
  17.9 0.0 copy-done.2
  17.9 0.9 copy.34
  18.7 0.0 copy-done.3
  18.7 0.8 copy.31
  19.5 0.0 copy-done.7
  19.6 0.7 copy.32
  20.3 0.0 copy-done.14
  20.3 0.0 copy-done.11
  20.3 0.0 copy-done.12
  20.3 0.6 select_reduce_fusion.inv_order
  21.0 24.3 %all-to-all-done.rest_0_.rest_1_ = bf16[64,128,128]{2,1,0:T(8,128)(2,1)S(1)} async-done(((bf16[64,128,128]{2,1,0:T(8,128)(2,1)}), bf16[64,128,128]{2,1,0:T(8,128)(2,1)S(1)}, u32[]{:S(2)}, u32[]{:S(2)}) %all-to-all-start) | async-done | bytes 2097184 | tf_op jit(solution)/shard_map/all_to_all | solution.py:275
  45.3 1.4 broadcast_in_dim.45.rest_4_
  46.7 0.0 copy-done.10
  46.7 1.0 broadcast_in_dim.46.rest_5_
  47.7 0.0 copy-done.13
  47.7 0.7 broadcast_in_dim.47.rest_6_
  48.4 0.0 copy-done
  48.4 353.5 %shard_map.204 = (bf16[64,128,128]{2,1,0:T(8,128)(2,1)}, f32[64,128,128]{2,1,0:T(8,128)}, f32[2,512,128]{2,1,0:T(8,128)}, f32[2,128,512]{2,1,0:T(8,128)}, f32[2,...) custom-call(s32[64]{0:T(128)} %select_reduce_fusion.inv_order, bf16[64,128,128]{2,1,0:T(8,128)(2,1)} %bitcast.20, ...), custom_call_target="tpu_custom_call" | custom-call | tf_op jit(solution)/shard_map/pallas_call | solution.py:242
  401.9 2.5 gather_fusion
  404.4 1.6 broadcast_select_fusion
  406.0 4.7 all-to-all-start.1
  410.7 0.0 all-reduce.3.cloned.1.call-start
  410.7 0.7 all-reduce.3.cloned.1.call-update
  411.4 0.0 copy-done.9
  411.4 82.7 %psum.35 = f32[24,128]{1,0:T(8,128)S(1)} all-reduce(f32[24,128]{1,0:T(8,128)S(1)} %copy-done.9), channel_id=1, replica_groups=mesh['dp'=32,'group'=4] {'dp','group'}, use_global_device_ids=true, to_apply=%region_1.2 | all-reduce | flops 3072 | bytes 24576 | tf_op jit(solution)/shard_map/psum | solution.py:282
  494.2 0.6 slice.25
  494.8 0.6 slice.24
  495.3 0.6 reshape.88
  495.9 0.5 slice_bitcast_fusion
  496.5 0.0 all-to-all-done.1
  496.5 76.9 %all-reduce.3.cloned.1.call-done = (f32[2,128,384]{2,1,0:T(8,128)}, f32[2,128,128]{2,1,0:T(8,128)}, f32[2,128,512]{2,1,0:T(8,128)}, f32[2,512,128]{2,1,0:T(8,128)}) async-done(((f32[2,128,384]{2,1,0:T(8,128)}, f32[2,128,128]{2,1,0:T(8,128)}, f32[2,128,512]{2,1,0:T(8,128)}, f32[2,512,128]{2,1,0:T(8,128)}), (f32[2,128,384]{2,1,0:T(8,128)}, f32[2,128,128]{2,1,0:T(8,128)}, f32[2,128,512]{2,1,0:T(8,128)}, ...) | async-done | bytes 1572880 | tf_op jit(solution)/shard_map/psum | solution.py:282
  573.4 1.3 copy.40
  574.7 0.7 copy.41
  575.5 0.7 copy.42
  576.1 0.8 copy.43
  576.9 0.8 copy.44
  (17 shorter events, 0.1 us)
Async XLA Ops:
  7.2 9.8 %copy-start.1 = (bf16[2,128,512]{2,1,0:T(8,128)(2,1)S(1)}, bf16[2,128,512]{2,1,0:T(8,128)(2,1)}, u32[]{:S(2)}) copy-start(bf16[2,128,512]{2,1,0:T(8,128)(2,1)} %rest_12_.1) | copy-start | bytes 786436
  7.2 10.7 %copy-start.2 = (bf16[2,512,128]{2,1,0:T(8,128)(2,1)S(1)}, bf16[2,512,128]{2,1,0:T(8,128)(2,1)}, u32[]{:S(2)}) copy-start(bf16[2,512,128]{2,1,0:T(8,128)(2,1)} %rest_14_.1) | copy-start | bytes 786436
  7.2 11.5 %copy-start.3 = (bf16[2,128,384]{2,1,0:T(8,128)(2,1)S(1)}, bf16[2,128,384]{2,1,0:T(8,128)(2,1)}, u32[]{:S(2)}) copy-start(bf16[2,128,384]{2,1,0:T(8,128)(2,1)} %rest_8_.1) | copy-start | bytes 589828
  7.2 12.3 %copy-start.7 = (bf16[2,128,128]{2,1,0:T(8,128)(2,1)S(1)}, bf16[2,128,128]{2,1,0:T(8,128)(2,1)}, u32[]{:S(2)}) copy-start(bf16[2,128,128]{2,1,0:T(8,128)(2,1)} %rest_10_.1) | copy-start | bytes 196612
  7.2 13.1 %copy-start.14 = (s32[1,1,64]{2,1,0:T(1,128)S(1)}, s32[1,1,64]{2,1,0:T(1,128)}, u32[]{:S(2)}) copy-start(s32[1,1,64]{2,1,0:T(1,128)} %param.16) | copy-start | bytes 772
  7.2 13.1 %copy-start.11 = (f32[2,4,128]{2,1,0:T(4,128)S(1)}, f32[2,4,128]{2,1,0:T(4,128)}, u32[]{:S(2)}) copy-start(f32[2,4,128]{2,1,0:T(4,128)} %param.19) | copy-start | bytes 12292
  7.2 13.1 %copy-start.12 = (f32[2,2,128]{2,1,0:T(2,128)S(1)}, f32[2,2,128]{2,1,0:T(2,128)}, u32[]{:S(2)}) copy-start(f32[2,2,128]{2,1,0:T(2,128)} %param.18) | copy-start | bytes 6148
  7.3 38.1 %all-to-all-start = ((bf16[64,128,128]{2,1,0:T(8,128)(2,1)}), bf16[64,128,128]{2,1,0:T(8,128)(2,1)S(1)}, u32[]{:S(2)}, u32[]{:S(2)}) async-start(bf16[64,128,128]{2,1,0:T(8,128)(2,1)} %bitcast.19), calls=%async_computation | async-start | bytes 4194304 | tf_op jit(solution)/shard_map/all_to_all | solution.py:275
  17.0 29.7 %copy-start.10 = (f32[2,512]{1,0:T(2,128)S(1)}, f32[2,512]{1,0:T(2,128)}, u32[]{:S(2)}) copy-start(f32[2,512]{1,0:T(2,128)} %param.23) | copy-start | bytes 12292
  17.0 30.7 %copy-start.13 = (f32[128]{0:T(128)S(1)}, f32[128]{0:T(128)}, u32[]{:S(2)}) copy-start(f32[128]{0:T(128)} %param.17) | copy-start | bytes 1540
  45.3 3.1 copy-start
  406.0 5.4 copy-start.9
  406.0 90.5 %all-to-all-start.1 = ((bf16[64,128,128]{2,1,0:T(8,128)(2,1)}), bf16[64,128,128]{2,1,0:T(8,128)(2,1)S(1)}, u32[]{:S(2)}, u32[]{:S(2)}) async-start(bf16[64,128,128]{2,1,0:T(8,128)(2,1)} %broadcast_select_fusion), calls=%async_computation.1 | async-start | bytes 4194304 | tf_op jit(solution)/shard_map/all_to_all | solution.py:281
  410.7 162.7 %all-reduce.3.cloned.1.call-start = ((), (), s32[]{:S(2)}) async-start(), calls=%async_computation.2 | async-start | bytes 3145728 | tf_op jit(solution)/shard_map/psum | solution.py:282
  573.4 1.3 copy-start.6
  573.4 2.1 copy-start.8
  573.4 2.7 copy-start.5
  574.7 2.2 copy-start.4
Sparse Core Ops, SparseCore 0:
  417.3 156.0 all-reduce.2

commit v2 on v1

v2 whole, which is shorter than its diff:
```python
import jax
import jax.numpy as jnp
from jax import lax
from jax.experimental import pallas as pl
from jax.experimental.pallas import tpu as pltpu
from jax.sharding import PartitionSpec as P

HEADS = 8
HEAD = 16
D = 128
FF = 512
S = 128
NT = 2
NG = 2
LAG_E = 3
LAG_D = 3
LAG_B = 3
L = NT * S
STEP = NT * NG
SMALL = 2 * FF + 4 * D
PACKED = SMALL + 64
EPS = 1e-5
LOG2E = 1.4426950408889634
LN2 = 0.6931471805599453
F32 = jnp.float32
BF = jnp.bfloat16


def nn(a, b):
    return lax.dot_general(a, b, (((1,), (0,)), ((), ())), preferred_element_type=F32)


def nt(a, b):
    return lax.dot_general(a, b, (((1,), (1,)), ((), ())), preferred_element_type=F32)


def wide(col):
    return jnp.concatenate([col] * NT, axis=1)


def fold(val):
    out = val[:, :S]
    for t in range(1, NT):
        out = out + val[:, t * S:(t + 1) * S]
    return out


def normalize(x):
    center = x - jnp.sum(x, axis=0, keepdims=True) * (1.0 / D)
    var = jnp.sum(center * center, axis=0, keepdims=True) * (1.0 / D)
    rstd = lax.rsqrt(var + EPS)
    return center * rstd, rstd


def norm_back(grad, xhat, rstd, gain):
    gx = grad * gain
    m1 = jnp.sum(gx, axis=0, keepdims=True) * (1.0 / D)
    m2 = jnp.sum(gx * xhat, axis=0, keepdims=True) * (1.0 / D)
    return (gx - m1 - xhat * m2) * rstd


def padded(rows, h):
    parts = []
    if h > 0:
        parts.append(jnp.zeros((HEAD * h, S), BF))
    parts.append(rows)
    if h < HEADS - 1:
        parts.append(jnp.zeros((D - HEAD * (h + 1), S), BF))
    return jnp.concatenate(parts, axis=0)


def pair_rhs(two, h):
    return jnp.concatenate([padded(two[0:HEAD], h), padded(two[HEAD:2 * HEAD], h + 1)], axis=1)


UNITS = [(t, h) for t in range(NT) for h in range(0, HEADS, 2)]


def layer_fwd(x, biases, w, sv):
    wi_t, wo_t, m1_t, m2_t, cols, hid = w["wi_t"], w["wo_t"], w["m1_t"], w["m2_t"], w["cols"], w["hid"]
    xhat0, rstd0 = normalize(x)
    sv["xhat0"][...] = xhat0.astype(BF)
    sv["rstd"][0:8, :] = jnp.broadcast_to(rstd0, (8, L))
    a = (xhat0 * wide(cols[0]) + wide(cols[2])).astype(BF)
    sv["a"][...] = a
    p = nn(wi_t[...], a)
    yield
    sv["p"][0:D, :] = (p[0:D] * (0.25 * LOG2E)).astype(BF)
    sv["p"][D:3 * D, :] = p[D:3 * D].astype(BF)
    yield
    ones = jnp.ones((HEAD, S), BF)
    keys = [jnp.transpose(sv["p"][D:2 * D, t * S:(t + 1) * S]) for t in range(NT)]
    n = len(UNITS)
    for i in range(n + 2):
        if i < n:
            t, h = UNITS[i]
            sl = slice(t * S, (t + 1) * S)
            sv["s"][i] = nn(keys[t], pair_rhs(sv["p"][HEAD * h:HEAD * (h + 2), sl], h))
        if 1 <= i <= n:
            t, h = UNITS[i - 1]
            for k in range(2):
                s = sv["s"][i - 1, :, k * S:(k + 1) * S] + biases[t]
                e = jnp.exp2(s - jnp.max(s, axis=0, keepdims=True)).astype(BF)
                sv["e"][t, :, (h + k) * S:(h + k + 1) * S] = e
        if i >= 2:
            t, h = UNITS[i - 2]
            sl = slice(t * S, (t + 1) * S)
            v = sv["p"][2 * D + HEAD * h:2 * D + HEAD * (h + 2), sl]
            o = nn(jnp.concatenate([v, ones], axis=0), sv["e"][t, :, h * S:(h + 2) * S])
            for k in range(2):
                kl = slice(k * S, (k + 1) * S)
                inv = 1.0 / o[2 * HEAD:2 * HEAD + 8, kl]
                sv["inv"][8 * (h + k):8 * (h + k) + 8, sl] = inv
                sv["o"][HEAD * (h + k):HEAD * (h + k + 1), sl] = (
                    o[HEAD * k:HEAD * (k + 1), kl] * jnp.concatenate([inv, inv], axis=0)).astype(BF)
        yield
    x1 = x + nn(wo_t[...], sv["o"][...]) + wide(cols[4])
    yield
    xhat1, rstd1 = normalize(x1)
    sv["xhat1"][...] = xhat1.astype(BF)
    sv["rstd"][8:16, :] = jnp.broadcast_to(rstd1, (8, L))
    b = (xhat1 * wide(cols[1]) + wide(cols[3])).astype(BF)
    sv["b"][...] = b
    yield
    hidden = None
    for i in range(5):
        last = hidden
        if i < 4:
            hidden = nn(m1_t[i * D:(i + 1) * D, :], b)
        if i >= 1:
            rows = slice((i - 1) * D, i * D)
            hv = last + wide(hid[rows, :])
            cdf = 0.5 * lax.erf(hv * 0.7071067811865476) + 0.5
            sv["u"][rows, :] = (hv * cdf).astype(BF)
            phi = jnp.exp2(hv * hv * (-0.5 * LOG2E)) * 0.3989422804014327
            sv["gp"][rows, :] = (cdf + hv * phi).astype(BF)
        yield
    return x1 + nn(m2_t[...], sv["u"][...]) + wide(cols[5])


def layer_bwd(g2, w, sv, acc):
    wi, wo, m1, m2, cols = w["wi"], w["wo"], w["m1"], w["m2"], w["cols"]
    a_vec, a_hid, a_wi, a_wo, a_m1, a_m2 = acc
    gz = g2.astype(BF)
    a_vec[5] += fold(g2)
    gu = None
    for i in range(5):
        last = gu
        if i < 4:
            rows = slice(i * D, (i + 1) * D)
            gu = nn(m2[rows, :], gz)
            a_m2[rows, :] += nt(sv["u"][rows, :], gz)
        if i >= 1:
            rows = slice((i - 1) * D, i * D)
            gh = last * sv["gp"][rows, :].astype(F32)
            a_hid[rows, :] += fold(gh)
            ghb = gh.astype(BF)
            sv["gh"][rows, :] = ghb
            a_m1[rows, :] += nt(ghb, sv["b"][...])
        yield
    gb = nn(m1[...], sv["gh"][...])
    yield
    xhat1 = sv["xhat1"][...].astype(F32)
    a_vec[1] += fold(gb * xhat1)
    a_vec[3] += fold(gb)
    g1 = g2 + norm_back(gb, xhat1, sv["rstd"][8:9, :], wide(cols[1]))
    gy = g1.astype(BF)
    a_vec[4] += fold(g1)
    yield
    a_wo[...] += nt(sv["o"][...], gy)
    go = nn(wo[...], gy)
    yield
    values = [jnp.transpose(sv["p"][2 * D:3 * D, t * S:(t + 1) * S]) for t in range(NT)]
    n = len(UNITS)
    gobs, rs = {}, {}
    for i in range(n + 2):
        if i < n:
            t, h = UNITS[i]
            sl = slice(t * S, (t + 1) * S)
            parts = []
            for k in (h, h + 1):
                hs = slice(HEAD * k, HEAD * (k + 1))
                inv = sv["inv"][8 * k:8 * k + 8, sl]
                gob = (go[hs, sl] * jnp.concatenate([inv, inv], axis=0)).astype(BF)
                parts.append(gob)
                rs[t, k] = jnp.sum(gob.astype(F32) * sv["o"][hs, sl].astype(F32), axis=0, keepdims=True)
            gobs[i] = jnp.concatenate(parts, axis=0)
            sv["s"][i] = nn(values[t], pair_rhs(gobs[i], h))
        if 1 <= i <= n:
            t, h = UNITS[i - 1]
            for k in range(2):
                kl = slice(k * S, (k + 1) * S)
                e = sv["e"][t, :, (h + k) * S:(h + k + 1) * S].astype(F32)
                sv["gs"][i - 1, :, kl] = (e * (sv["s"][i - 1, :, kl] - rs[t, h + k])).astype(BF)
        if i >= 2:
            t, h = UNITS[i - 2]
            sl = slice(t * S, (t + 1) * S)
            e2 = jnp.concatenate([sv["e"][t, :, (h + k) * S:(h + k + 1) * S] for k in range(2)], axis=0)
            s2 = jnp.concatenate([sv["gs"][i - 2, :, k * S:(k + 1) * S] for k in range(2)], axis=0)
            pv = nt(gobs[i - 2], e2)
            pq = nn(sv["p"][D + HEAD * h:D + HEAD * (h + 2), sl], sv["gs"][i - 2])
            pk = nt(sv["p"][HEAD * h:HEAD * (h + 2), sl], s2)
            for k in range(2):
                kr = slice(HEAD * k, HEAD * (k + 1))
                kl = slice(k * S, (k + 1) * S)
                at = HEAD * (h + k)
                sv["gpk"][at:at + HEAD, sl] = (pq[kr, kl] * 0.25).astype(BF)
                sv["gpk"][D + at:D + at + HEAD, sl] = (pk[kr, kl] * LN2).astype(BF)
                sv["gpk"][2 * D + at:2 * D + at + HEAD, sl] = pv[kr, kl].astype(BF)
        yield
    gp = sv["gpk"][...]
    ga = nn(wi[...], gp)
    a_wi[...] += nt(gp, sv["a"][...])
    yield
    xhat0 = sv["xhat0"][...].astype(F32)
    a_vec[0] += fold(ga * xhat0)
    a_vec[2] += fold(ga)
    return g1 + norm_back(ga, xhat0, sv["rstd"][0:1, :], wide(cols[0]))


def masks(seg_ref, vis_ref, first, decoder):
    rows_i = lax.broadcasted_iota(jnp.int32, (S, S), 0)
    cols_i = lax.broadcasted_iota(jnp.int32, (S, S), 1)
    diag = rows_i == cols_i
    out = []
    for t in range(NT):
        seg = seg_ref[0, first + t:first + t + 1, :]
        key = jnp.where(seg >= 0, seg, -2)
        if not decoder:
            key = jnp.where(vis_ref[0, first + t:first + t + 1, :] == 1, key, -2)
        key_k = jnp.transpose(jnp.broadcast_to(key, (S, S)).astype(F32))
        out.append(jnp.where((key_k == seg.astype(F32)) | diag, 0.0, -1e30))
    return out


def identity():
    rows_i = lax.broadcasted_iota(jnp.int32, (S, S), 0)
    cols_i = lax.broadcasted_iota(jnp.int32, (S, S), 1)
    return (rows_i == cols_i).astype(F32).astype(BF)


def drive(gens, lag):
    live = [True] * len(gens)
    tick = 0
    while any(live):
        for j, gen in enumerate(gens):
            if live[j] and tick >= lag * j:
                try:
                    next(gen)
                except StopIteration:
                    live[j] = False
        tick += 1


SAVED = {
    "p": ((3 * D, L), BF),
    "e": ((NT, S, HEADS * S), BF),
    "inv": ((8 * HEADS, L), F32),
    "o": ((D, L), BF),
    "u": ((FF, L), BF),
    "gp": ((FF, L), BF),
    "xhat0": ((D, L), BF),
    "xhat1": ((D, L), BF),
    "a": ((D, L), BF),
    "b": ((D, L), BF),
    "rstd": ((16, L), F32),
}
SCORES = {"s": ((len(UNITS), S, 2 * S), F32)}
BACK = {
    "gs": ((len(UNITS), S, 2 * S), BF),
    "gh": ((FF, L), BF),
    "gpk": ((3 * D, L), BF),
}
RAW = ("gains", "shifts", "hidden", "wi", "wo", "m1", "m2")
PREP = {
    "cols": ((6, D, S), F32),
    "hid": ((FF, S), F32),
    "wi_t": ((3 * D, D), BF),
    "wo_t": ((D, D), BF),
    "m1_t": ((FF, D), BF),
    "m2_t": ((D, FF), BF),
}


def spread_row(row):
    return jnp.transpose(jnp.broadcast_to(row, (S, D)))


def prep_weights(l, raw, prep, forward):
    raw = dict(zip(RAW, raw))
    prep = dict(zip(PREP, prep))

    @pl.when(pl.program_id(0) == 0)
    def _():
        for j in range(2):
            prep["cols"][j] = spread_row(raw["gains"][l, j:j + 1, :])
        for j in range(4):
            prep["cols"][2 + j] = spread_row(raw["shifts"][l, j:j + 1, :])
        if forward:
            for j in range(4):
                rows = slice(j * D, (j + 1) * D)
                prep["hid"][rows, :] = spread_row(raw["hidden"][l:l + 1, rows])
                prep["m1_t"][rows, :] = jnp.transpose(raw["m1"][l, :, rows])
                prep["m2_t"][:, rows] = jnp.transpose(raw["m2"][l, rows, :])
            for j in range(3):
                rows = slice(j * D, (j + 1) * D)
                prep["wi_t"][rows, :] = jnp.transpose(raw["wi"][l, :, rows])
            prep["wo_t"][...] = jnp.transpose(raw["wo"][l])

    return prep | {name: raw[name].at[l] for name in ("wi", "wo", "m1", "m2")}


def scratch_of(table):
    return [pltpu.VMEM((NG,) + shape, dt) for shape, dt in table.values()]


def prep_scratch():
    return [pltpu.VMEM(shape, dt) for shape, dt in PREP.values()]


def views(names, refs, g):
    return {name: ref.at[g] for name, ref in zip(names, refs)}


def encode_kernel(x_ref, seg_ref, vis_ref, *rest):
    raw, rest = rest[:len(RAW)], rest[len(RAW):]
    enc_ref = rest[0]
    saved = rest[1:1 + len(SAVED)]
    score = rest[1 + len(SAVED):1 + len(SAVED) + len(SCORES)]
    w = prep_weights(0, raw, rest[1 + len(SAVED) + len(SCORES):], True)
    eye = identity()

    def group(g):
        sv = views(SAVED, saved, g) | views(SCORES, score, g)
        bias = masks(seg_ref, vis_ref, NT * g, False)
        x = jnp.concatenate([nt(eye, x_ref[NT * g + t]) for t in range(NT)], axis=1)
        yield
        out = yield from layer_fwd(x, bias, w, sv)
        enc_ref[g] = out.astype(BF)

    drive([group(g) for g in range(NG)], LAG_E)


def zero_first(refs):
    @pl.when(pl.program_id(0) == 0)
    def _():
        for ref in refs:
            ref[...] = jnp.zeros_like(ref)


ACC = [
    ((6, D, S), F32),
    ((FF, S), F32),
    ((3 * D, D), F32),
    ((D, D), F32),
    ((FF, D), F32),
    ((FF, D), F32),
]


def finish(acc, out, a_mask=None):
    a_vec, a_hid, a_wi, a_wo, a_m1, a_m2 = acc

    @pl.when(pl.program_id(0) == pl.num_programs(0) - 1)
    def _():
        out[0:FF, :] = a_m2[...]
        for j in range(4):
            rows = slice(j * D, (j + 1) * D)
            out[FF + j * D:FF + (j + 1) * D, :] = jnp.transpose(a_m1[rows, :])
        for j in range(3):
            rows = slice(j * D, (j + 1) * D)
            out[2 * FF + j * D:2 * FF + (j + 1) * D, :] = jnp.transpose(a_wi[rows, :])
        out[2 * FF + 3 * D:SMALL, :] = a_wo[...]
        out[SMALL:PACKED, :] = jnp.zeros((PACKED - SMALL, D), F32)
        for j in range(6):
            out[SMALL + j:SMALL + j + 1, :] = jnp.sum(jnp.transpose(a_vec[j]), axis=0, keepdims=True)
        for j in range(4):
            out[SMALL + 6 + j:SMALL + 7 + j, :] = jnp.sum(
                jnp.transpose(a_hid[j * D:(j + 1) * D]), axis=0, keepdims=True)
        if a_mask is not None:
            out[SMALL + 10:SMALL + 11, :] = jnp.sum(jnp.transpose(a_mask[...]), axis=0, keepdims=True)


def decode_kernel(inv_order, enc_ref, *rest):
    cots = rest[:STEP]
    seg_ref, vis_ref, mask_row = rest[STEP:STEP + 3]
    rest = rest[STEP + 3:]
    raw, rest = rest[:len(RAW)], rest[len(RAW):]
    dec_out, ge_ref, out_ref = rest[:3]
    rest = rest[3:]
    acc, rest = rest[:len(ACC)], rest[len(ACC):]
    a_mask, maskcol, dec_ref, sems = rest[:4]
    rest = rest[4:]
    w = prep_weights(1, raw, rest[:len(PREP)], True)
    scr = rest[len(PREP):]
    step = pl.program_id(0)
    slot = lax.rem(step, 2)

    @pl.when(step == 0)
    def _():
        maskcol[...] = spread_row(mask_row[0:1, :])

    def copies(at, where):
        return [
            pltpu.make_async_copy(dec_ref.at[where, t], dec_out.at[inv_order[STEP * at + t]], sems.at[where, t])
            for t in range(STEP)
        ]

    @pl.when(step >= 2)
    def _():
        for copy in copies(step - 2, slot):
            copy.wait()

    zero_first(acc + (a_mask,))
    eye = identity()
    table = list(SAVED) + list(SCORES) + list(BACK)

    def group(g):
        sv = views(table, scr, g)
        bias = masks(seg_ref, vis_ref, NT * g, True)
        shown = jnp.concatenate([vis_ref[0, NT * g + t:NT * g + t + 1, :] for t in range(NT)], axis=1) == 1
        x = jnp.where(shown, enc_ref[g].astype(F32), wide(maskcol[...]))
        yield
        out = yield from layer_fwd(x, bias, w, sv)
        outb = out.astype(BF)
        for t in range(NT):
            dec_ref[slot, NT * g + t] = nt(eye, outb[:, t * S:(t + 1) * S]).astype(BF)
        yield
        grad = jnp.concatenate([nt(eye, cots[NT * g + t][0]) for t in range(NT)], axis=1)
        yield
        grad = yield from layer_bwd(grad, w, sv, acc)
        a_mask[...] += fold(jnp.where(shown, 0.0, grad))
        ge_ref[g] = jnp.where(shown, grad, 0.0).astype(BF)

    drive([group(g) for g in range(NG)], LAG_D)
    for copy in copies(step, slot):
        copy.start()

    @pl.when(step == pl.num_programs(0) - 1)
    def _():
        for copy in copies(step - 1, 1 - slot) + copies(step, slot):
            copy.wait()

    finish(acc, out_ref, a_mask)


def back_kernel(ge_ref, *rest):
    saved = rest[:len(SAVED)]
    rest = rest[len(SAVED):]
    raw, rest = rest[:len(RAW)], rest[len(RAW):]
    tg_ref, out_ref = rest[:2]
    acc = rest[2:2 + len(ACC)]
    w = prep_weights(0, raw, rest[2 + len(ACC):2 + len(ACC) + len(PREP)], False)
    scr = rest[2 + len(ACC) + len(PREP):]
    zero_first(acc)
    table = list(SCORES) + list(BACK)

    def group(g):
        sv = views(SAVED, saved, g) | views(table, scr, g)
        grad = ge_ref[g].astype(F32)
        yield
        grad = yield from layer_bwd(grad, w, sv, acc)
        for t in range(NT):
            tg_ref[NT * g + t] = jnp.transpose(grad[:, t * S:(t + 1) * S])

    drive([group(g) for g in range(NG)], LAG_B)
    finish(acc, out_ref)


def const_spec(arr):
    return pl.BlockSpec(arr.shape, lambda *_: (0,) * arr.ndim)


def step_spec(shape):
    return pl.BlockSpec(shape, lambda i, *_: (i,) + (0,) * (len(shape) - 1))


PARAMS = pltpu.CompilerParams(dimension_semantics=("arbitrary",), vmem_limit_bytes=60 * 1024 * 1024)
GRADS = [jax.ShapeDtypeStruct((PACKED, D), F32)]


def cost(flops, nbytes):
    return pl.CostEstimate(flops=flops, bytes_accessed=nbytes, transcendentals=0)


def run_encode(x, seg, vis, w):
    tiles = x.shape[0]
    groups, steps = tiles // NT, tiles // STEP
    ops = list(w)
    out_shape = [jax.ShapeDtypeStruct((groups, D, L), BF)]
    out_shape += [jax.ShapeDtypeStruct((groups,) + shape, dt) for shape, dt in SAVED.values()]
    return pl.pallas_call(
        encode_kernel,
        grid=(steps,),
        in_specs=[step_spec((STEP, S, D)), step_spec((1, STEP, S)), step_spec((1, STEP, S))] + [const_spec(o) for o in ops],
        out_specs=[step_spec((NG,) + o.shape[1:]) for o in out_shape],
        out_shape=out_shape,
        scratch_shapes=scratch_of(SCORES) + prep_scratch(),
        cost_estimate=cost(20 * 10**9, 60 * 10**6),
        compiler_params=PARAMS,
    )(x, seg.reshape(steps, STEP, S), vis.reshape(steps, STEP, S), *ops)


def run_decode(inv_order, enc, cot, seg, vis, mask_row, w):
    tiles = cot.shape[0]
    groups, steps = tiles // NT, tiles // STEP
    ops = [mask_row] + list(w)
    cot_specs = [pl.BlockSpec((1, S, D), lambda i, o, t=t: (o[STEP * i + t], 0, 0)) for t in range(STEP)]
    out_shape = [jax.ShapeDtypeStruct((tiles, S, D), BF), jax.ShapeDtypeStruct((groups, D, L), BF)] + GRADS
    return pl.pallas_call(
        decode_kernel,
        grid_spec=pltpu.PrefetchScalarGridSpec(
            num_scalar_prefetch=1,
            grid=(steps,),
            in_specs=[step_spec((NG, D, L))] + cot_specs + [step_spec((1, STEP, S))] * 2 + [const_spec(o) for o in ops],
            out_specs=[pl.BlockSpec(memory_space=pl.ANY), step_spec((NG, D, L))] + [const_spec(o) for o in GRADS],
            scratch_shapes=[pltpu.VMEM(shape, dt) for shape, dt in ACC] + [pltpu.VMEM((D, S), F32)] * 2
            + [pltpu.VMEM((2, STEP, S, D), BF), pltpu.SemaphoreType.DMA((2, STEP))]
            + prep_scratch() + scratch_of(SAVED) + scratch_of(SCORES) + scratch_of(BACK),
        ),
        out_shape=out_shape,
        cost_estimate=cost(40 * 10**9, 10 * 10**6),
        compiler_params=PARAMS,
    )(inv_order, enc, *([cot] * STEP), seg.reshape(steps, STEP, S), vis.reshape(steps, STEP, S), *ops)


def run_back(ge, saved, w):
    groups = ge.shape[0]
    steps = groups // NG
    ops = list(w)
    out_shape = [jax.ShapeDtypeStruct((groups * NT, S, D), F32)] + GRADS
    return pl.pallas_call(
        back_kernel,
        grid=(steps,),
        in_specs=[step_spec((NG, D, L))] + [step_spec((NG,) + s.shape[1:]) for s in saved] + [const_spec(o) for o in ops],
        out_specs=[step_spec((STEP, S, D))] + [const_spec(o) for o in GRADS],
        out_shape=out_shape,
        scratch_shapes=[pltpu.VMEM(shape, dt) for shape, dt in ACC] + prep_scratch() + scratch_of(SCORES) + scratch_of(BACK),
        cost_estimate=cost(20 * 10**9, 60 * 10**6),
        compiler_params=PARAMS,
    )(ge, *saved, *ops)


def unpack_kernel(core_ref, mine, other, g_m2, g_m1, g_wi, g_wo, g_gain, g_shift, g_hid, g_mask):
    core = core_ref[0]

    def write(src, l):
        g_m2[l] = src[0:FF, :].astype(F32)
        for j in range(4):
            g_m1[l, :, j * D:(j + 1) * D] = src[FF + j * D:FF + (j + 1) * D, :].astype(F32)
        for j in range(3):
            g_wi[l, :, j * D:(j + 1) * D] = src[2 * FF + j * D:2 * FF + (j + 1) * D, :].astype(F32)
        g_wo[l] = src[2 * FF + 3 * D:SMALL, :].astype(F32)
        rows = src[SMALL:SMALL + 16, :].astype(F32)
        g_gain[l] = rows[0:2]
        g_shift[l] = rows[2:6]
        for j in range(4):
            g_hid[l:l + 1, j * D:(j + 1) * D] = rows[6 + j:7 + j]
        if l == 1:
            g_mask[...] = rows[10:11]

    @pl.when(core == 0)
    def _():
        write(mine, 0)
        write(other, 1)

    @pl.when(core == 1)
    def _():
        write(other, 0)
        write(mine, 1)


def unpack(core, mine, other):
    shapes = [(2, FF, D), (2, D, FF), (2, D, 3 * D), (2, D, D), (2, 2, D), (2, 4, D), (2, FF), (1, D)]
    return pl.pallas_call(
        unpack_kernel,
        grid_spec=pltpu.PrefetchScalarGridSpec(
            num_scalar_prefetch=1,
            grid=(1,),
            in_specs=[const_spec(mine), const_spec(other)],
            out_specs=[pl.BlockSpec(sh, lambda *_, n=len(sh): (0,) * n) for sh in shapes],
        ),
        out_shape=[jax.ShapeDtypeStruct(sh, F32) for sh in shapes],
        compiler_params=PARAMS,
    )(core.reshape(1).astype(jnp.int32), mine, other)


def swap(value, axis, bits, size):
    return lax.ppermute(value, axis, [(i, i ^ bits) for i in range(size)])


def split(value, bit):
    half = value.shape[0] // 2
    keep = lax.dynamic_slice_in_dim(value, bit * half, half, axis=0)
    send = lax.dynamic_slice_in_dim(value, (1 - bit) * half, half, axis=0)
    return keep, send.astype(BF)


def join(mine, other, bit):
    return jnp.where(bit == 0, jnp.concatenate([mine, other], axis=0), jnp.concatenate([other, mine], axis=0))


def reduce_all(first, second, n_dp, n_group):
    core = lax.axis_index("dp") % 2
    x = lax.axis_index("group")
    keep = jnp.where(core == 0, first, second)
    send = jnp.where(core == 0, second, first).astype(BF)
    value = keep + swap(send, "dp", 1, n_dp).astype(F32)
    for bits, bit in ((3, x // 2), (1, x % 2)):
        keep, send = split(value, bit)
        value = keep + swap(send, "group", bits, n_group).astype(F32)
    for bits in (2, 6, 8, 24):
        value = value + swap(value.astype(BF), "dp", bits, n_dp).astype(F32)
    value = value.astype(BF)
    for bits, bit in ((1, x % 2), (3, x // 2)):
        value = join(value, swap(value, "group", bits, n_group), bit)
    other = swap(value, "dp", 1, n_dp)
    return core, value, other


def on_device(token_tiles, segment_ids, visible_flags, tile_order, mask_token, norm_gains, shift_terms,
              attn_in, attn_out, mlp_in, hidden_shift, mlp_out, cotangent):
    tiles = token_tiles.shape[2]
    full_shape = (1, 1, tiles, S, D)
    order = tile_order.reshape(tiles)
    spots = jnp.arange(tiles, dtype=jnp.int32)
    inv_order = jnp.sum(jnp.where(order[None, :] == spots[:, None], spots[None, :], 0), axis=1).astype(jnp.int32)
    cot = lax.all_to_all(cotangent.reshape(tiles, S, D), "dp", split_axis=0, concat_axis=0, tiled=True)
    w = (norm_gains, shift_terms, hidden_shift, attn_in, attn_out, mlp_in, mlp_out)
    seg, vis = segment_ids.reshape(tiles, S), visible_flags.reshape(tiles, S)
    enc, *saved = run_encode(token_tiles.reshape(tiles, S, D), seg, vis, w)
    dec, ge, packed1 = run_decode(inv_order, enc, cot, seg, vis, mask_token.reshape(1, D), w)
    decoded = lax.all_to_all(dec, "dp", split_axis=0, concat_axis=0, tiled=True)
    tg, packed0 = run_back(ge, saved, w)
    n_dp = lax.axis_size("dp")
    if n_dp == 32:
        decoded, packed0 = lax.optimization_barrier((decoded, packed0))
        core, mine, other = reduce_all(packed0, packed1, n_dp, lax.axis_size("group"))
    else:
        core, mine, other = jnp.int32(0), packed0.astype(BF), packed1.astype(BF)
    g_m2, g_m1, g_wi, g_wo, g_gain, g_shift, g_hid, g_mask = unpack(core, mine, other)
    return (
        decoded.reshape(full_shape),
        tg.reshape(full_shape),
        g_mask.reshape(D),
        g_gain,
        g_shift,
        g_wi,
        g_wo,
        g_m1,
        g_hid,
        g_m2,
    )


def solution(mesh):
    tile5 = P("dp", "group", None, None, None)
    in_specs = (tile5, P("dp", "group", None, None), P("dp", "group", None, None), P("dp", "group", None),
                P(), P(), P(), P(), P(), P(), P(), P(), tile5)
    out_specs = (tile5, tile5) + (P(),) * 8
    return jax.shard_map(on_device, mesh=mesh, in_specs=in_specs, out_specs=out_specs, check_vma=False)
```

time: 585 us -> 268 us (0.46)
  Pallas kernels: 353 us -> 191 us
  blocking collectives: 82.7 us -> 0 us
  waiting for transfers between devices: 102 us -> 26.1 us
  starting transfers between devices: 14.5 us -> 41.2 us
  between operations: 14.2 us -> 0.85 us
  local copies, waits for them, and re-layouts: 15.5 us -> 4.33 us
    pallas_call x1 -> x4, Pallas kernels: 353 us -> 191 us  [the longest x1 90 us: run_decode(): pl.pallas_call(decode_kernel, grid_spec=pltpu.PrefetchScalarGridSpec(num_...]
    psum x1 -> x0, blocking collectives: 82.7 us -> none  [on_device(): lax.psum((g_m2, g_m1, g_wi, g_wo, rows), ('dp', 'group'))]
    psum x1 -> x0, waiting for transfers between devices: 76.9 us -> none  [on_device(): lax.psum((g_m2, g_m1, g_wi, g_wo, rows), ('dp', 'group'))]
    ppermute x0 -> x10, waiting for transfers between devices: none -> 26.1 us  [swap(): return lax.ppermute(value, axis, [(i, i ^ bits) for i in range(size)])]
    all_to_all x1, waiting for transfers between devices: 24.3 us -> 0.01 us  [on_device(): lax.all_to_all(cotangent.reshape(tiles, S, D), 'dp', split_axis=0, concat...]
    ppermute x0 -> x10, starting transfers between devices: none -> 24.1 us  [swap(): return lax.ppermute(value, axis, [(i, i ^ bits) for i in range(size)])]
  transfers between devices with their start and end apart: 3 -> 12, of which waited for: 2 -> 10; matrix products, arithmetic and copies ran while one was open for 1% -> 0% of each run, Pallas kernels for 0% -> 37%
where the time goes in v2:
time: 268 us; the launch traced here: 267 us
  Pallas kernels  191 us (71%)
  starting transfers between devices  41.2 us (15%)
  waiting for transfers between devices  26.1 us (10%)
  local copies, waits for them, and re-layouts  4.33 us (2%)
  other arithmetic  4.1 us (2%)
    pallas_call x1, Pallas kernels, run_decode(): pl.pallas_call(decode_kernel, grid_spec=pltpu.PrefetchScalarGridSpec(num_...  90 us
    pallas_call x1, Pallas kernels, run_encode(): pl.pallas_call(encode_kernel, grid=(steps,), in_specs=[step_spec((STEP, S...  49.5 us
    pallas_call x1, Pallas kernels, run_back(): pl.pallas_call(back_kernel, grid=(steps,), in_specs=[step_spec((NG, D, L)...  48.9 us
    ppermute x10, waiting for transfers between devices, swap(): return lax.ppermute(value, axis, [(i, i ^ bits) for i in range(size)])  26.1 us
    ppermute x10, starting transfers between devices, swap(): return lax.ppermute(value, axis, [(i, i ^ bits) for i in range(size)])  24.1 us
    all_to_all x1, starting transfers between devices, on_device(): lax.all_to_all(cotangent.reshape(tiles, S, D), 'dp', split_axis=0, concat...  9.61 us
    all_to_all x1, starting transfers between devices, on_device(): decoded = lax.all_to_all(dec, 'dp', split_axis=0, concat_axis=0, tiled=True)  7.39 us
  transfers between devices with their start and end apart: 12, of which 10 were waited for; matrix products, arithmetic and copies ran while one was open for 0% of the time, Pallas kernels for 37%

profile of v2, /device:TPU:1, one launch (start us, length us, event | category | flops | bytes accessed | tf_op | source)
XLA Modules:
  0.0 267.4 jit_solution(2785715971619643369)
XLA Ops:
  0.6 0.0 copy-start.5
  0.7 9.6 %all-to-all-start = ((bf16[64,128,128]{2,1,0:T(8,128)(2,1)}), bf16[64,128,128]{2,1,0:T(8,128)(2,1)S(1)}, u32[]{:S(2)}, u32[]{:S(2)}) async-start(bf16[64,128,128]{2,1,0:T(8,128)(2,1)} %bitcast.11), calls=%async_computation | async-start | bytes 4194304 | tf_op jit(solution)/shard_map/all_to_all | solution.py:628
  10.3 0.0 copy-done.5
  10.3 0.6 select_reduce_fusion.inv_order
  10.9 49.5 %shard_map.204 = (bf16[32,128,256]{2,1,0:T(8,128)(2,1)}, bf16[32,384,256]{2,1,0:T(8,128)(2,1)}, bf16[32,2,128,1024]{3,2,1,0:T(8,128)(2,1)}, f32[32,64,256]{2,1,0...) custom-call(bf16[64,128,128]{2,1,0:T(8,128)(2,1)} %bitcast.12, ...), custom_call_target="tpu_custom_call" | custom-call | flops 20000000000 | bytes 60000000 | tf_op jit(solution)/shard_map/pallas_call | solution.py:492
  60.5 0.0 all-to-all-done.rest_0_.rest_1_.rest_2_.rest_3_
  60.5 0.0 copy-start.2
  60.5 1.3 copy-done.2
  61.8 90.0 %shard_map.205 = (bf16[64,128,128]{2,1,0:T(8,128)(2,1)}, bf16[32,128,256]{2,1,0:T(8,128)(2,1)}, f32[1600,128]{1,0:T(8,128)}) custom-call(s32[64]{0:T(128)} %select_reduce_fusion.inv_order, bf16[32,128,256]{2,1,0:T(8,128)(2,1)} %get-tuple-element.37.enc_ref, bf16[64,128,128]{2,1,0:T(8,128)(2,1)} %copy-done.2, bf16[64,128,128]{2,1,0:T(8,128)(2,1)} %copy-done.2, ...), custom_call_target="tpu_custom_call" | custom-call | flops 40000000000 | bytes 10000000 | tf_op jit(solution)/shard_map/pallas_call | solution.py:510
  151.8 7.4 %all-to-all-start.1 = ((bf16[64,128,128]{2,1,0:T(8,128)(2,1)}), bf16[64,128,128]{2,1,0:T(8,128)(2,1)S(1)}, u32[]{:S(2)}, u32[]{:S(2)}) async-start(bf16[64,128,128]{2,1,0:T(8,128)(2,1)} %get-tuple-element.38), calls=%async_computation.1 | async-start | bytes 4194304 | tf_op jit(solution)/shard_map/all_to_all | solution.py:633
  159.2 0.0 copy-start
  159.2 48.9 %shard_map.206 = (f32[64,128,128]{2,1,0:T(8,128)}, f32[1600,128]{1,0:T(8,128)}) custom-call(bf16[32,128,256]{2,1,0:T(8,128)(2,1)} %get-tuple-element.39.ge_ref, bf16[32,384,256]{2,1,0:T(8,128)(2,1)} %get-tuple-element.40.rest_0_, bf16[32,2,128,1024]{3,2,1,0:T(8,128)(2,1)} %get-tuple-element.41.rest_1_, f32[32,64,256]{2,1,0:T(8,128)} %get-tuple-element.42.rest_2_, ...), custom_call_target="tpu_custom_call" | custom-call | flops 20000000000 | bytes 60000000 | tf_op jit(solution)/shard_map/pallas_call | solution.py:532
  208.2 0.0 all-to-all-done.1
  208.2 0.0 copy-done
  208.2 2.0 select_convert_fusion
  210.2 0.0 collective-permute-start
  210.2 2.0 collective-permute-done
  212.1 0.1 convert_add_fusion
  212.2 0.0 copy-start.1
  212.3 0.9 copy-done.1
  213.2 2.6 collective-permute-start.1
  215.7 4.0 %collective-permute-done.1 = bf16[800,128]{1,0:T(8,128)(2,1)S(1)} collective-permute-done((bf16[800,128]{1,0:T(8,128)(2,1)S(1)}, bf16[800,128]{1,0:T(8,128)(2,1)S(1)}, u32[]{:S(2)}, u32[]{:S(2)}) %collective-permute-start.1) | collective-permute-done | bytes 204832 | tf_op jit(solution)/shard_map/ppermute | solution.py:589
  219.7 1.0 convert_add_fusion.1
  220.8 0.3 collective-permute-start.2
  221.1 3.5 %collective-permute-done.2 = bf16[400,128]{1,0:T(8,128)(2,1)S(1)} collective-permute-done((bf16[400,128]{1,0:T(8,128)(2,1)S(1)}, bf16[400,128]{1,0:T(8,128)(2,1)S(1)}, u32[]{:S(2)}, u32[]{:S(2)}) %collective-permute-start.2) | collective-permute-done | bytes 102432 | tf_op jit(solution)/shard_map/ppermute | solution.py:589
  224.6 1.5 collective-permute-start.3
  226.1 2.1 collective-permute-done.3
  228.2 2.7 %collective-permute-start.4 = (bf16[400,128]{1,0:T(8,128)(2,1)S(1)}, bf16[400,128]{1,0:T(8,128)(2,1)S(1)}, u32[]{:S(2)}, u32[]{:S(2)}) collective-permute-start(bf16[400,128]{1,0:T(8,128)(2,1)S(1)} %fusion), channel_id=1, source_target_pairs={{0,24},{4,28},{8,16},{12,20},{16,8},{20,12},{24,0},{28,4},{32,56},... | collective-permute-start | bytes 307208 | tf_op jit(solution)/shard_map/ppermute | solution.py:589
  230.9 2.1 collective-permute-done.4
  233.0 0.1 fusion.3
  233.1 1.5 collective-permute-start.5
  234.6 2.1 collective-permute-done.5
  236.7 2.7 %collective-permute-start.6 = (bf16[400,128]{1,0:T(8,128)(2,1)S(1)}, bf16[400,128]{1,0:T(8,128)(2,1)S(1)}, u32[]{:S(2)}, u32[]{:S(2)}) collective-permute-start(bf16[400,128]{1,0:T(8,128)(2,1)S(1)} %fusion.1), channel_id=1, source_target_pairs={{0,96},{4,100},{8,104},{12,108},{16,112},{20,116},{24,120},{28,124... | collective-permute-start | bytes 307208 | tf_op jit(solution)/shard_map/ppermute | solution.py:589
  239.4 2.1 collective-permute-done.6
  241.6 0.1 collective-permute-start.7
  241.7 3.5 %collective-permute-done.7 = bf16[400,128]{1,0:T(8,128)(2,1)S(1)} collective-permute-done((bf16[400,128]{1,0:T(8,128)(2,1)S(1)}, bf16[400,128]{1,0:T(8,128)(2,1)S(1)}, u32[]{:S(2)}, u32[]{:S(2)}) %collective-permute-start.7) | collective-permute-done | bytes 102432 | tf_op jit(solution)/shard_map/ppermute | solution.py:589
  245.2 0.1 maximum_select_fusion.1
  245.2 2.6 collective-permute-start.8
  247.8 3.3 %collective-permute-done.8 = bf16[800,128]{1,0:T(8,128)(2,1)S(1)} collective-permute-done((bf16[800,128]{1,0:T(8,128)(2,1)S(1)}, bf16[800,128]{1,0:T(8,128)(2,1)S(1)}, u32[]{:S(2)}, u32[]{:S(2)}) %collective-permute-start.8) | collective-permute-done | bytes 204832 | tf_op jit(solution)/shard_map/ppermute | solution.py:589
  251.1 0.1 maximum_select_fusion.mine
  251.2 0.0 copy-start.3
  251.2 10.3 %collective-permute-start.9 = (bf16[1600,128]{1,0:T(8,128)(2,1)S(1)}, bf16[1600,128]{1,0:T(8,128)(2,1)S(1)}, u32[]{:S(2)}, u32[]{:S(2)}) collective-permute-start(bf16[1600,128]{1,0:T(8,128)(2,1)S(1)} %maximum_select_fusion.mine), channel_id=1, source_target_pairs={{0,4},{4,0},{8,12},{12,8},{16,20},{20,16},{24,28},{28,24},{32,36},... | collective-permute-start | bytes 1228808 | tf_op jit(solution)/shard_map/ppermute | solution.py:589
  261.6 1.4 collective-permute-done.9.other
  262.9 0.0 copy-start.4
  262.9 0.0 copy-done.3
  262.9 0.7 copy-done.4
  263.7 2.4 shard_map.207
  266.1 1.3 copy.24
  (6 shorter events, 0.2 us)
Async XLA Ops:
  0.6 9.6 %copy-start.5 = (s32[1,1,64]{2,1,0:T(1,128)S(1)}, s32[1,1,64]{2,1,0:T(1,128)}, u32[]{:S(2)}) copy-start(s32[1,1,64]{2,1,0:T(1,128)} %param.16) | copy-start | bytes 772
  0.7 59.8 %all-to-all-start = ((bf16[64,128,128]{2,1,0:T(8,128)(2,1)}), bf16[64,128,128]{2,1,0:T(8,128)(2,1)S(1)}, u32[]{:S(2)}, u32[]{:S(2)}) async-start(bf16[64,128,128]{2,1,0:T(8,128)(2,1)} %bitcast.11), calls=%async_computation | async-start | bytes 4194304 | tf_op jit(solution)/shard_map/all_to_all | solution.py:628
  60.5 1.3 copy-start.2
  151.8 56.4 %all-to-all-start.1 = ((bf16[64,128,128]{2,1,0:T(8,128)(2,1)}), bf16[64,128,128]{2,1,0:T(8,128)(2,1)S(1)}, u32[]{:S(2)}, u32[]{:S(2)}) async-start(bf16[64,128,128]{2,1,0:T(8,128)(2,1)} %get-tuple-element.38), calls=%async_computation.1 | async-start | bytes 4194304 | tf_op jit(solution)/shard_map/all_to_all | solution.py:633
  159.2 49.0 %copy-start = (f32[1600,128]{1,0:T(8,128)S(1)}, f32[1600,128]{1,0:T(8,128)}, u32[]{:S(2)}) copy-start(f32[1600,128]{1,0:T(8,128)} %get-tuple-element.55) | copy-start | bytes 2457604
  210.2 2.0 collective-permute-start
  212.2 0.9 copy-start.1
  213.2 6.6 %collective-permute-start.1 = (bf16[800,128]{1,0:T(8,128)(2,1)S(1)}, bf16[800,128]{1,0:T(8,128)(2,1)S(1)}, u32[]{:S(2)}, u32[]{:S(2)}) collective-permute-start(bf16[800,128]{1,0:T(8,128)(2,1)S(1)} %dynamic-slice_convert_fusion), channel_id=1, source_target_pairs={{0,3},{1,2},{2,1},{3,0},{4,7},{5,6},{6,5},{7,4},{8,11},{9,10},{10,... | collective-permute-start | bytes 614408 | tf_op jit(solution)/shard_map/ppermute | solution.py:589
  220.8 3.8 %collective-permute-start.2 = (bf16[400,128]{1,0:T(8,128)(2,1)S(1)}, bf16[400,128]{1,0:T(8,128)(2,1)S(1)}, u32[]{:S(2)}, u32[]{:S(2)}) collective-permute-start(bf16[400,128]{1,0:T(8,128)(2,1)S(1)} %dynamic-slice_convert_fusion.1), channel_id=1, source_target_pairs={{0,1},{1,0},{2,3},{3,2},{4,5},{5,4},{6,7},{7,6},{8,9},{9,8},{10,11... | collective-permute-start | bytes 307208 | tf_op jit(solution)/shard_map/ppermute | solution.py:589
  224.6 3.6 %collective-permute-start.3 = (bf16[400,128]{1,0:T(8,128)(2,1)S(1)}, bf16[400,128]{1,0:T(8,128)(2,1)S(1)}, u32[]{:S(2)}, u32[]{:S(2)}) collective-permute-start(bf16[400,128]{1,0:T(8,128)(2,1)S(1)} %fusion.2), channel_id=1, source_target_pairs={{0,8},{4,12},{8,0},{12,4},{16,24},{20,28},{24,16},{28,20},{32,40},... | collective-permute-start | bytes 307208 | tf_op jit(solution)/shard_map/ppermute | solution.py:589
  228.2 4.8 %collective-permute-start.4 = (bf16[400,128]{1,0:T(8,128)(2,1)S(1)}, bf16[400,128]{1,0:T(8,128)(2,1)S(1)}, u32[]{:S(2)}, u32[]{:S(2)}) collective-permute-start(bf16[400,128]{1,0:T(8,128)(2,1)S(1)} %fusion), channel_id=1, source_target_pairs={{0,24},{4,28},{8,16},{12,20},{16,8},{20,12},{24,0},{28,4},{32,56},... | collective-permute-start | bytes 307208 | tf_op jit(solution)/shard_map/ppermute | solution.py:589
  233.1 3.6 %collective-permute-start.5 = (bf16[400,128]{1,0:T(8,128)(2,1)S(1)}, bf16[400,128]{1,0:T(8,128)(2,1)S(1)}, u32[]{:S(2)}, u32[]{:S(2)}) collective-permute-start(bf16[400,128]{1,0:T(8,128)(2,1)S(1)} %get-tuple-element.64), channel_id=1, source_target_pairs={{0,32},{4,36},{8,40},{12,44},{16,48},{20,52},{24,56},{28,60},{32,0... | collective-permute-start | bytes 307208 | tf_op jit(solution)/shard_map/ppermute | solution.py:589
  236.7 4.8 %collective-permute-start.6 = (bf16[400,128]{1,0:T(8,128)(2,1)S(1)}, bf16[400,128]{1,0:T(8,128)(2,1)S(1)}, u32[]{:S(2)}, u32[]{:S(2)}) collective-permute-start(bf16[400,128]{1,0:T(8,128)(2,1)S(1)} %fusion.1), channel_id=1, source_target_pairs={{0,96},{4,100},{8,104},{12,108},{16,112},{20,116},{24,120},{28,124... | collective-permute-start | bytes 307208 | tf_op jit(solution)/shard_map/ppermute | solution.py:589
  241.6 3.6 %collective-permute-start.7 = (bf16[400,128]{1,0:T(8,128)(2,1)S(1)}, bf16[400,128]{1,0:T(8,128)(2,1)S(1)}, u32[]{:S(2)}, u32[]{:S(2)}) collective-permute-start(bf16[400,128]{1,0:T(8,128)(2,1)S(1)} %add_convert_fusion), channel_id=1, source_target_pairs={{0,1},{1,0},{2,3},{3,2},{4,5},{5,4},{6,7},{7,6},{8,9},{9,8},{10,11... | collective-permute-start | bytes 307208 | tf_op jit(solution)/shard_map/ppermute | solution.py:589
  245.2 5.9 %collective-permute-start.8 = (bf16[800,128]{1,0:T(8,128)(2,1)S(1)}, bf16[800,128]{1,0:T(8,128)(2,1)S(1)}, u32[]{:S(2)}, u32[]{:S(2)}) collective-permute-start(bf16[800,128]{1,0:T(8,128)(2,1)S(1)} %maximum_select_fusion.1), channel_id=1, source_target_pairs={{0,3},{1,2},{2,1},{3,0},{4,7},{5,6},{6,5},{7,4},{8,11},{9,10},{10,... | collective-permute-start | bytes 614408 | tf_op jit(solution)/shard_map/ppermute | solution.py:589
  251.2 11.7 %copy-start.3 = (bf16[1600,128]{1,0:T(8,128)(2,1)}, bf16[1600,128]{1,0:T(8,128)(2,1)S(1)}, u32[]{:S(2)}) copy-start(bf16[1600,128]{1,0:T(8,128)(2,1)S(1)} %maximum_select_fusion.mine) | copy-start | bytes 1228804
  251.2 11.7 %collective-permute-start.9 = (bf16[1600,128]{1,0:T(8,128)(2,1)S(1)}, bf16[1600,128]{1,0:T(8,128)(2,1)S(1)}, u32[]{:S(2)}, u32[]{:S(2)}) collective-permute-start(bf16[1600,128]{1,0:T(8,128)(2,1)S(1)} %maximum_select_fusion.mine), channel_id=1, source_target_pairs={{0,4},{4,0},{8,12},{12,8},{16,20},{20,16},{24,28},{28,24},{32,36},... | collective-permute-start | bytes 1228808 | tf_op jit(solution)/shard_map/ppermute | solution.py:589
  262.9 0.8 copy-start.4

commit v3 on v2

v3 whole, which is shorter than its diff:
```python
import jax
import jax.numpy as jnp
from jax import lax
from jax.experimental import pallas as pl
from jax.experimental.pallas import tpu as pltpu
from jax.sharding import PartitionSpec as P

HEADS = 8
HEAD = 16
D = 128
FF = 512
S = 128
NT = 2
NG_E = 8
TURN_E = 2
TURN_D = 2
TURN_B = 2
NG_D = 8
NG_B = 4
L = NT * S
SMALL = 2 * FF + 4 * D
PACKED = SMALL + 64
EPS = 1e-5
LOG2E = 1.4426950408889634
LN2 = 0.6931471805599453
F32 = jnp.float32
BF = jnp.bfloat16


def nn(a, b):
    return lax.dot_general(a, b, (((1,), (0,)), ((), ())), preferred_element_type=F32)


def nt(a, b):
    return lax.dot_general(a, b, (((1,), (1,)), ((), ())), preferred_element_type=F32)


def wide(col):
    return jnp.concatenate([col] * NT, axis=1)


def fold(val):
    out = val[:, :S]
    for t in range(1, NT):
        out = out + val[:, t * S:(t + 1) * S]
    return out


def normalize(x):
    center = x - jnp.sum(x, axis=0, keepdims=True) * (1.0 / D)
    var = jnp.sum(center * center, axis=0, keepdims=True) * (1.0 / D)
    rstd = lax.rsqrt(var + EPS)
    return center * rstd, rstd


def norm_back(grad, xhat, rstd, gain):
    gx = grad * gain
    m1 = jnp.sum(gx, axis=0, keepdims=True) * (1.0 / D)
    m2 = jnp.sum(gx * xhat, axis=0, keepdims=True) * (1.0 / D)
    return (gx - m1 - xhat * m2) * rstd


def padded(rows, h):
    parts = []
    if h > 0:
        parts.append(jnp.zeros((HEAD * h, S), BF))
    parts.append(rows)
    if h < HEADS - 1:
        parts.append(jnp.zeros((D - HEAD * (h + 1), S), BF))
    return jnp.concatenate(parts, axis=0)


def pair_rhs(two, h):
    return jnp.concatenate([padded(two[0:HEAD], h), padded(two[HEAD:2 * HEAD], h + 1)], axis=1)


def flip_pair(two):
    return jnp.concatenate([jnp.transpose(two[:, 0:S]), jnp.transpose(two[:, S:2 * S])], axis=1)


def pair_lhs(two):
    zero = jnp.zeros((HEAD, S), BF)
    return jnp.concatenate(
        [jnp.concatenate([two[0:HEAD], zero], axis=1), jnp.concatenate([zero, two[HEAD:2 * HEAD]], axis=1)], axis=0)


UNITS = [(t, h) for t in range(NT) for h in range(0, HEADS, 2)]


def mix_values(sv, t, h):
    sl = slice(t * S, (t + 1) * S)
    v = sv["p"][2 * D + HEAD * h:2 * D + HEAD * (h + 2), sl]
    o = nn(jnp.concatenate([v, jnp.ones((HEAD, S), BF)], axis=0), sv["e"][t, :, h * S:(h + 2) * S])
    totals = []
    for k in range(2):
        kl = slice(k * S, (k + 1) * S)
        totals.append(o[2 * HEAD:2 * HEAD + 8, kl])
        inv = 1.0 / totals[k]
        sv["inv"][8 * (h + k):8 * (h + k) + 8, sl] = inv
        sv["o"][HEAD * (h + k):HEAD * (h + k + 1), sl] = (
            o[HEAD * k:HEAD * (k + 1), kl] * jnp.concatenate([inv, inv], axis=0)).astype(BF)
    return totals


def redo_shifted(low, high, group_view, group_bias, ng):
    safe = (jnp.min(low) > 2.0 ** -60) & (jnp.max(high) < 2.0 ** 60)

    @pl.when(jnp.logical_not(safe))
    def _():
        def one(g, carry):
            sv = group_view(g)
            biases = group_bias(g)
            for t, h in UNITS:
                sl = slice(t * S, (t + 1) * S)
                keys = jnp.transpose(sv["p"][D:2 * D, sl])
                scores = nn(keys, pair_rhs(sv["p"][HEAD * h:HEAD * (h + 2), sl], h))
                for k in range(2):
                    part = scores[:, k * S:(k + 1) * S] + biases[t]
                    e = jnp.exp2(part - jnp.max(part, axis=0, keepdims=True))
                    sv["e"][t, :, (h + k) * S:(h + k + 1) * S] = e.astype(BF)
                mix_values(sv, t, h)
            return carry

        lax.fori_loop(0, ng, one, 0)


def layer_fwd(x, biases, w, sv, share):
    per_turn = share["per_turn"]
    wi_t, wo_t, m1_t, m2_t, cols, hid = w["wi_t"], w["wo_t"], w["m1_t"], w["m2_t"], w["cols"], w["hid"]
    xhat0, rstd0 = normalize(x)
    sv["xhat0"][...] = xhat0.astype(BF)
    sv["rstd"][0:8, :] = jnp.broadcast_to(rstd0, (8, L))
    a = (xhat0 * wide(cols[0]) + wide(cols[2])).astype(BF)
    sv["a"][...] = a
    p = nn(wi_t[...], a)
    yield
    sv["p"][0:D, :] = (p[0:D] * (0.25 * LOG2E)).astype(BF)
    sv["p"][D:3 * D, :] = p[D:3 * D].astype(BF)
    yield
    keys = [jnp.transpose(sv["p"][D:2 * D, t * S:(t + 1) * S]) for t in range(NT)]
    n = len(UNITS)
    for turn in range(0, n + per_turn, per_turn):
        for t, h in UNITS[turn:turn + per_turn]:
            scores = nn(keys[t], pair_rhs(sv["p"][HEAD * h:HEAD * (h + 2), t * S:(t + 1) * S], h))
            for k in range(2):
                e = jnp.exp2(scores[:, k * S:(k + 1) * S] + biases[t])
                sv["e"][t, :, (h + k) * S:(h + k + 1) * S] = e.astype(BF)
        for t, h in UNITS[max(turn - per_turn, 0):turn]:
            for total in mix_values(sv, t, h):
                share["low"] = total if share["low"] is None else jnp.minimum(share["low"], total)
                share["high"] = total if share["high"] is None else jnp.maximum(share["high"], total)
        yield
    if share["last"] is sv:
        share["redo"](share["low"], share["high"])
    yield
    x1 = x + nn(wo_t[...], sv["o"][...]) + wide(cols[4])
    yield
    xhat1, rstd1 = normalize(x1)
    sv["xhat1"][...] = xhat1.astype(BF)
    sv["rstd"][8:16, :] = jnp.broadcast_to(rstd1, (8, L))
    b = (xhat1 * wide(cols[1]) + wide(cols[3])).astype(BF)
    sv["b"][...] = b
    yield
    hidden = None
    for i in range(5):
        last = hidden
        if i < 4:
            hidden = nn(m1_t[i * D:(i + 1) * D, :], b)
        if i >= 1:
            rows = slice((i - 1) * D, i * D)
            hv = last + wide(hid[rows, :])
            arg = hv * 0.7071067811865476
            cdf2 = lax.erf(arg) + 1.0
            sv["u"][rows, :] = (hv * cdf2).astype(BF)
            bell = jnp.exp2(arg * arg * -LOG2E)
            sv["gp"][rows, :] = (cdf2 + arg * 1.1283791670955126 * bell).astype(BF)
        yield
    return x1 + nn(m2_t[...], sv["u"][...]) + wide(cols[5])


def lanes(views, name):
    return jnp.concatenate([sv[name][...] for sv in views], axis=1)


def layer_bwd(g2, w, sv, acc, share):
    wi, wo, m1, m2, cols = w["wi"], w["wo"], w["m1"], w["m2_h"], w["cols"]
    a_vec, a_wi, a_wo, a_m1, a_m2 = acc
    views = share["views"]
    per_turn = share["per_turn"]
    last = views[-1] is sv
    n = len(UNITS)
    gz = g2.astype(BF)
    sv["gz"][...] = gz
    gu = None
    for i in range(5):
        done = gu
        if i < 4:
            gu = nn(m2[i * D:(i + 1) * D, :], gz)
        if i >= 1:
            rows = slice((i - 1) * D, i * D)
            sv["gh"][rows, :] = (done * sv["gp"][rows, :].astype(F32)).astype(BF)
        yield
    gb = nn(m1[...], sv["gh"][...])
    yield
    if last:
        width = L * len(views)
        a_m2[...] += nt(jnp.concatenate([lanes(views, "u"), jnp.ones((HEAD, width), BF)], axis=0), lanes(views, "gz"))
    yield
    if last:
        a_m1[...] += nt(lanes(views, "gh"), jnp.concatenate([lanes(views, "b"), jnp.ones((D, width), BF)], axis=0))
    yield
    xhat1 = sv["xhat1"][...].astype(F32)
    a_vec[1] += fold(gb * xhat1)
    a_vec[3] += fold(gb)
    g1 = g2 + norm_back(gb, xhat1, sv["rstd"][8:9, :], wide(cols[1]))
    gy = g1.astype(BF)
    sv["gy"][...] = gy
    yield
    go = nn(wo[...], gy)
    yield
    if last:
        a_wo[...] += nt(jnp.concatenate([lanes(views, "o"), jnp.ones((HEAD, width), BF)], axis=0), lanes(views, "gy"))
    values = [jnp.transpose(sv["p"][2 * D:3 * D, t * S:(t + 1) * S]) for t in range(NT)]
    gobs = {}
    for turn in range(0, n + per_turn, per_turn):
        for i in range(turn, min(turn + per_turn, n)):
            t, h = UNITS[i]
            sl = slice(t * S, (t + 1) * S)
            parts, rs = [], []
            for k in (h, h + 1):
                hs = slice(HEAD * k, HEAD * (k + 1))
                inv = sv["inv"][8 * k:8 * k + 8, sl]
                gob = (go[hs, sl] * jnp.concatenate([inv, inv], axis=0)).astype(BF)
                parts.append(gob)
                rs.append(jnp.sum(gob.astype(F32) * sv["o"][hs, sl].astype(F32), axis=0, keepdims=True))
            gobs[i] = jnp.concatenate(parts, axis=0)
            gf = nn(values[t], pair_rhs(gobs[i], h))
            for k in range(2):
                kl = slice(k * S, (k + 1) * S)
                e = sv["e"][t, :, (h + k) * S:(h + k + 1) * S].astype(F32)
                sv["gs"][i, :, kl] = (e * (gf[:, kl] - rs[k])).astype(BF)
        for i in range(max(turn - per_turn, 0), turn):
            t, h = UNITS[i]
            sl = slice(t * S, (t + 1) * S)
            pv = nn(gobs[i], flip_pair(sv["e"][t, :, h * S:(h + 2) * S]))
            pq = nn(sv["p"][D + HEAD * h:D + HEAD * (h + 2), sl], sv["gs"][i])
            pk = nn(sv["p"][HEAD * h:HEAD * (h + 2), sl], flip_pair(sv["gs"][i]))
            for k in range(2):
                kr = slice(HEAD * k, HEAD * (k + 1))
                kl = slice(k * S, (k + 1) * S)
                at = HEAD * (h + k)
                sv["gpk"][at:at + HEAD, sl] = (pq[kr, kl] * 0.25).astype(BF)
                sv["gpk"][D + at:D + at + HEAD, sl] = (pk[kr, kl] * LN2).astype(BF)
                sv["gpk"][2 * D + at:2 * D + at + HEAD, sl] = pv[kr, kl].astype(BF)
        yield
    ga = nn(wi[...], sv["gpk"][...])
    yield
    if last:
        a_wi[...] += nt(lanes(views, "gpk"), lanes(views, "a"))
    xhat0 = sv["xhat0"][...].astype(F32)
    a_vec[0] += fold(ga * xhat0)
    a_vec[2] += fold(ga)
    return g1 + norm_back(ga, xhat0, sv["rstd"][0:1, :], wide(cols[0]))


def masks(seg_ref, vis_ref, first, decoder):
    rows_i = lax.broadcasted_iota(jnp.int32, (S, S), 0)
    cols_i = lax.broadcasted_iota(jnp.int32, (S, S), 1)
    diag = rows_i == cols_i
    out = []
    for t in range(NT):
        seg = seg_ref[0, pl.ds(first + t, 1), :]
        key = jnp.where(seg >= 0, seg, -2)
        if not decoder:
            key = jnp.where(vis_ref[0, pl.ds(first + t, 1), :] == 1, key, -2)
        key_k = jnp.transpose(jnp.broadcast_to(key, (S, S)).astype(F32))
        out.append(jnp.where((key_k == seg.astype(F32)) | diag, 0.0, -1e30))
    return out


def drive(gens):
    gens = list(gens)
    while gens:
        alive = []
        for gen in gens:
            try:
                next(gen)
                alive.append(gen)
            except StopIteration:
                pass
        gens = alive


SAVED = {
    "p": ((3 * D, L), BF),
    "e": ((NT, S, HEADS * S), BF),
    "inv": ((8 * HEADS, L), F32),
    "o": ((D, L), BF),
    "u": ((FF, L), BF),
    "gp": ((FF, L), BF),
    "xhat0": ((D, L), BF),
    "xhat1": ((D, L), BF),
    "a": ((D, L), BF),
    "b": ((D, L), BF),
    "rstd": ((16, L), F32),
}
BACK = {
    "gs": ((len(UNITS), S, 2 * S), BF),
    "gz": ((D, L), BF),
    "gy": ((D, L), BF),
    "gh": ((FF, L), BF),
    "gpk": ((3 * D, L), BF),
}
RAW = ("gains", "shifts", "hidden", "wi", "wo", "m1", "m2")
PREP = {
    "cols": ((6, D, S), F32),
    "hid": ((FF, S), F32),
    "wi_t": ((3 * D, D), BF),
    "wo_t": ((D, D), BF),
    "m1_t": ((FF, D), BF),
    "m2_t": ((D, FF), BF),
    "m2_h": ((FF, D), BF),
}


def spread_row(row):
    return jnp.transpose(jnp.broadcast_to(row, (S, D)))


def prep_weights(l, raw, prep, forward):
    raw = dict(zip(RAW, raw))
    prep = dict(zip(PREP, prep))

    @pl.when(pl.program_id(0) == 0)
    def _():
        for j in range(2):
            prep["cols"][j] = spread_row(raw["gains"][l, j:j + 1, :])
        for j in range(4):
            prep["cols"][2 + j] = spread_row(raw["shifts"][l, j:j + 1, :])
        if forward:
            for j in range(4):
                rows = slice(j * D, (j + 1) * D)
                prep["hid"][rows, :] = spread_row(raw["hidden"][l:l + 1, rows])
                prep["m1_t"][rows, :] = jnp.transpose(raw["m1"][l, :, rows])
                prep["m2_t"][:, rows] = jnp.transpose(raw["m2"][l, rows, :]) * BF(0.5)
            for j in range(3):
                rows = slice(j * D, (j + 1) * D)
                prep["wi_t"][rows, :] = jnp.transpose(raw["wi"][l, :, rows])
            prep["wo_t"][...] = jnp.transpose(raw["wo"][l])
        prep["m2_h"][...] = raw["m2"][l] * BF(0.5)

    return prep | {name: raw[name].at[l] for name in ("wi", "wo", "m1")}


def scratch_of(table, ng):
    return [pltpu.VMEM((ng,) + shape, dt) for shape, dt in table.values()]


def prep_scratch():
    return [pltpu.VMEM(shape, dt) for shape, dt in PREP.values()]


def views(names, refs, g):
    return {name: ref.at[g] for name, ref in zip(names, refs)}


def sharing(group_views, per_turn, view_at, bias_at):
    return {
        "per_turn": per_turn,
        "views": group_views,
        "last": group_views[-1],
        "low": None,
        "high": None,
        "redo": lambda low, high: redo_shifted(low, high, view_at, bias_at, len(group_views)),
    }


def encode_kernel(x_ref, seg_ref, vis_ref, *rest):
    raw, rest = rest[:len(RAW)], rest[len(RAW):]
    enc_ref = rest[0]
    saved = rest[1:1 + len(SAVED)]
    w = prep_weights(0, raw, rest[1 + len(SAVED):], True)
    share = sharing([views(SAVED, saved, g) for g in range(NG_E)], TURN_E, lambda g: views(SAVED, saved, g),
                    lambda g: masks(seg_ref, vis_ref, NT * g, False))

    def group(g):
        sv = share["views"][g]
        bias = masks(seg_ref, vis_ref, NT * g, False)
        x = jnp.concatenate([jnp.transpose(x_ref[NT * g + t]).astype(F32) for t in range(NT)], axis=1)
        yield
        out = yield from layer_fwd(x, bias, w, sv, share)
        enc_ref[g] = out.astype(BF)

    drive([group(g) for g in range(NG_E)])


def zero_first(refs):
    @pl.when(pl.program_id(0) == 0)
    def _():
        for ref in refs:
            ref[...] = jnp.zeros_like(ref)


ACC = [
    ((4, D, S), F32),
    ((3 * D, D), F32),
    ((D + HEAD, D), F32),
    ((FF, 2 * D), F32),
    ((FF + HEAD, D), F32),
]


def finish(acc, out, a_mask=None):
    a_vec, a_wi, a_wo, a_m1, a_m2 = acc

    @pl.when(pl.program_id(0) == pl.num_programs(0) - 1)
    def _():
        out[0:FF, :] = a_m2[0:FF, :] * 0.5
        for j in range(4):
            rows = slice(j * D, (j + 1) * D)
            out[FF + j * D:FF + (j + 1) * D, :] = jnp.transpose(a_m1[rows, 0:D])
            out[SMALL + 6 + j:SMALL + 7 + j, :] = jnp.transpose(a_m1[rows, D:2 * D])[0:1]
            out[SMALL + j:SMALL + j + 1, :] = jnp.sum(jnp.transpose(a_vec[j]), axis=0, keepdims=True)
        for j in range(3):
            rows = slice(j * D, (j + 1) * D)
            out[2 * FF + j * D:2 * FF + (j + 1) * D, :] = jnp.transpose(a_wi[rows, :])
        out[2 * FF + 3 * D:SMALL, :] = a_wo[0:D, :]
        out[SMALL + 4:SMALL + 5, :] = a_wo[D:D + 1, :]
        out[SMALL + 5:SMALL + 6, :] = a_m2[FF:FF + 1, :]
        out[SMALL + 11:PACKED, :] = jnp.zeros((PACKED - SMALL - 11, D), F32)
        out[SMALL + 10:SMALL + 11, :] = jnp.zeros((1, D), F32)
        if a_mask is not None:
            out[SMALL + 10:SMALL + 11, :] = jnp.sum(jnp.transpose(a_mask[...]), axis=0, keepdims=True)


def decode_kernel(inv_order, enc_ref, *rest):
    cots = rest[:(NT * NG_D)]
    seg_ref, vis_ref, mask_row = rest[(NT * NG_D):(NT * NG_D) + 3]
    rest = rest[(NT * NG_D) + 3:]
    raw, rest = rest[:len(RAW)], rest[len(RAW):]
    dec_out, ge_ref, out_ref = rest[:3]
    rest = rest[3:]
    acc, rest = rest[:len(ACC)], rest[len(ACC):]
    a_mask, maskcol, dec_ref, sems = rest[:4]
    rest = rest[4:]
    w = prep_weights(1, raw, rest[:len(PREP)], True)
    scr = rest[len(PREP):]
    step = pl.program_id(0)
    slot = lax.rem(step, 2)

    @pl.when(step == 0)
    def _():
        maskcol[...] = spread_row(mask_row[0:1, :])

    def copies(at, where):
        return [
            pltpu.make_async_copy(dec_ref.at[where, t], dec_out.at[inv_order[(NT * NG_D) * at + t]], sems.at[where, t])
            for t in range((NT * NG_D))
        ]

    @pl.when(step >= 2)
    def _():
        for copy in copies(step - 2, slot):
            copy.wait()

    zero_first(acc + (a_mask,))
    table = list(SAVED) + list(BACK)
    share = sharing([views(table, scr, g) for g in range(NG_D)], TURN_D, lambda g: views(table, scr, g),
                    lambda g: masks(seg_ref, vis_ref, NT * g, True))

    def group(g):
        sv = share["views"][g]
        bias = masks(seg_ref, vis_ref, NT * g, True)
        shown = jnp.concatenate([vis_ref[0, NT * g + t:NT * g + t + 1, :] for t in range(NT)], axis=1) == 1
        x = jnp.where(shown, enc_ref[g].astype(F32), wide(maskcol[...]))
        yield
        out = yield from layer_fwd(x, bias, w, sv, share)
        outb = out.astype(BF)
        for t in range(NT):
            dec_ref[slot, NT * g + t] = jnp.transpose(outb[:, t * S:(t + 1) * S])
        yield
        grad = jnp.concatenate([jnp.transpose(cots[NT * g + t][0]).astype(F32) for t in range(NT)], axis=1)
        yield
        grad = yield from layer_bwd(grad, w, sv, acc, share)
        a_mask[...] += fold(jnp.where(shown, 0.0, grad))
        ge_ref[g] = jnp.where(shown, grad, 0.0).astype(BF)

    drive([group(g) for g in range(NG_D)])
    for copy in copies(step, slot):
        copy.start()

    @pl.when(step == pl.num_programs(0) - 1)
    def _():
        for copy in copies(step - 1, 1 - slot) + copies(step, slot):
            copy.wait()

    finish(acc, out_ref, a_mask)


def back_kernel(core_ref, ge_ref, other_ref, *rest):
    saved = rest[:len(SAVED)]
    rest = rest[len(SAVED):]
    raw, rest = rest[:len(RAW)], rest[len(RAW):]
    tg_ref, keep_ref, send_ref = rest[:3]
    out_ref, rest = rest[3], rest[4:]
    acc, rest = rest[:len(ACC)], rest[len(ACC):]
    w = prep_weights(0, raw, rest[:len(PREP)], False)
    scr = rest[len(PREP):]
    zero_first(acc)
    share = sharing([views(SAVED, saved, g) | views(BACK, scr, g) for g in range(NG_B)], TURN_B, None, None)

    def group(g):
        sv = share["views"][g]
        grad = ge_ref[g].astype(F32)
        yield
        grad = yield from layer_bwd(grad, w, sv, acc, share)
        for t in range(NT):
            tg_ref[NT * g + t] = jnp.transpose(grad[:, t * S:(t + 1) * S])

    drive([group(g) for g in range(NG_B)])
    finish(acc, out_ref)

    @pl.when((pl.program_id(0) == pl.num_programs(0) - 1) & (core_ref[0] == 0))
    def _():
        keep_ref[...] = out_ref[...]
        send_ref[...] = other_ref[...].astype(BF)

    @pl.when((pl.program_id(0) == pl.num_programs(0) - 1) & (core_ref[0] == 1))
    def _():
        keep_ref[...] = other_ref[...]
        send_ref[...] = out_ref[...].astype(BF)


def const_spec(arr):
    return pl.BlockSpec(arr.shape, lambda *_: (0,) * arr.ndim)


def step_spec(shape):
    return pl.BlockSpec(shape, lambda i, *_: (i,) + (0,) * (len(shape) - 1))


PARAMS = pltpu.CompilerParams(dimension_semantics=("arbitrary",), vmem_limit_bytes=60 * 1024 * 1024)
GRADS = [jax.ShapeDtypeStruct((PACKED, D), F32)]


def cost(flops, nbytes):
    return pl.CostEstimate(flops=flops, bytes_accessed=nbytes, transcendentals=0)


def run_encode(x, seg, vis, w):
    tiles = x.shape[0]
    groups, steps = tiles // NT, tiles // (NT * NG_E)
    ops = list(w)
    out_shape = [jax.ShapeDtypeStruct((groups, D, L), BF)]
    out_shape += [jax.ShapeDtypeStruct((groups,) + shape, dt) for shape, dt in SAVED.values()]
    return pl.pallas_call(
        encode_kernel,
        grid=(steps,),
        in_specs=[step_spec(((NT * NG_E), S, D)), step_spec((1, (NT * NG_E), S)), step_spec((1, (NT * NG_E), S))] + [const_spec(o) for o in ops],
        out_specs=[step_spec((NG_E,) + o.shape[1:]) for o in out_shape],
        out_shape=out_shape,
        scratch_shapes=prep_scratch(),
        cost_estimate=cost(20 * 10**9, 60 * 10**6),
        compiler_params=PARAMS,
    )(x, seg.reshape(steps, (NT * NG_E), S), vis.reshape(steps, (NT * NG_E), S), *ops)


def run_decode(inv_order, enc, cot, seg, vis, mask_row, w):
    tiles = cot.shape[0]
    groups, steps = tiles // NT, tiles // (NT * NG_D)
    ops = [mask_row] + list(w)
    cot_specs = [pl.BlockSpec((1, S, D), lambda i, o, t=t: (o[(NT * NG_D) * i + t], 0, 0)) for t in range((NT * NG_D))]
    out_shape = [jax.ShapeDtypeStruct((tiles, S, D), BF), jax.ShapeDtypeStruct((groups, D, L), BF)] + GRADS
    return pl.pallas_call(
        decode_kernel,
        grid_spec=pltpu.PrefetchScalarGridSpec(
            num_scalar_prefetch=1,
            grid=(steps,),
            in_specs=[step_spec((NG_D, D, L))] + cot_specs + [step_spec((1, (NT * NG_D), S))] * 2 + [const_spec(o) for o in ops],
            out_specs=[pl.BlockSpec(memory_space=pl.ANY), step_spec((NG_D, D, L))] + [const_spec(o) for o in GRADS],
            scratch_shapes=[pltpu.VMEM(shape, dt) for shape, dt in ACC] + [pltpu.VMEM((D, S), F32)] * 2
            + [pltpu.VMEM((2, (NT * NG_D), S, D), BF), pltpu.SemaphoreType.DMA((2, (NT * NG_D)))]
            + prep_scratch() + scratch_of(SAVED, NG_D) + scratch_of(BACK, NG_D),
        ),
        out_shape=out_shape,
        cost_estimate=cost(40 * 10**9, 10 * 10**6),
        compiler_params=PARAMS,
    )(inv_order, enc, *([cot] * (NT * NG_D)), seg.reshape(steps, (NT * NG_D), S), vis.reshape(steps, (NT * NG_D), S), *ops)


def run_back(core, ge, other, saved, w):
    groups = ge.shape[0]
    steps = groups // NG_B
    ops = list(w)
    packed = jax.ShapeDtypeStruct((PACKED, D), F32)
    out_shape = [jax.ShapeDtypeStruct((groups * NT, S, D), F32), packed, jax.ShapeDtypeStruct((PACKED, D), BF)]
    return pl.pallas_call(
        back_kernel,
        grid_spec=pltpu.PrefetchScalarGridSpec(
            num_scalar_prefetch=1,
            grid=(steps,),
            in_specs=[step_spec((NG_B, D, L)), const_spec(other)] + [step_spec((NG_B,) + v.shape[1:]) for v in saved]
            + [const_spec(o) for o in ops],
            out_specs=[step_spec((NT * NG_B, S, D))] + [const_spec(o) for o in out_shape[1:]],
            scratch_shapes=[pltpu.VMEM((PACKED, D), F32)] + [pltpu.VMEM(shape, dt) for shape, dt in ACC] + prep_scratch()
            + scratch_of(BACK, NG_B),
        ),
        out_shape=out_shape,
        compiler_params=PARAMS,
        cost_estimate=cost(20 * 10**9, 60 * 10**6),
    )(core, ge, other, *saved, *ops)


def unpack_kernel(core_ref, mine, other, g_m2, g_m1, g_wi, g_wo, g_gain, g_shift, g_hid, g_mask):
    core = core_ref[0]

    def write(src, l):
        g_m2[l] = src[0:FF, :].astype(F32)
        for j in range(4):
            g_m1[l, :, j * D:(j + 1) * D] = src[FF + j * D:FF + (j + 1) * D, :].astype(F32)
        for j in range(3):
            g_wi[l, :, j * D:(j + 1) * D] = src[2 * FF + j * D:2 * FF + (j + 1) * D, :].astype(F32)
        g_wo[l] = src[2 * FF + 3 * D:SMALL, :].astype(F32)
        rows = src[SMALL:SMALL + 16, :].astype(F32)
        g_gain[l] = rows[0:2]
        g_shift[l] = rows[2:6]
        for j in range(4):
            g_hid[l:l + 1, j * D:(j + 1) * D] = rows[6 + j:7 + j]
        if l == 1:
            g_mask[...] = rows[10:11]

    @pl.when(core == 0)
    def _():
        write(mine, 0)
        write(other, 1)

    @pl.when(core == 1)
    def _():
        write(other, 0)
        write(mine, 1)


def unpack(core, mine, other):
    shapes = [(2, FF, D), (2, D, FF), (2, D, 3 * D), (2, D, D), (2, 2, D), (2, 4, D), (2, FF), (1, D)]
    return pl.pallas_call(
        unpack_kernel,
        grid_spec=pltpu.PrefetchScalarGridSpec(
            num_scalar_prefetch=1,
            grid=(1,),
            in_specs=[const_spec(mine), const_spec(other)],
            out_specs=[pl.BlockSpec(sh, lambda *_, n=len(sh): (0,) * n) for sh in shapes],
        ),
        out_shape=[jax.ShapeDtypeStruct(sh, F32) for sh in shapes],
        compiler_params=PARAMS,
    )(core.reshape(1).astype(jnp.int32), mine, other)


def swap(value, axis, bits, size):
    return lax.ppermute(value, axis, [(i, i ^ bits) for i in range(size)])


def split(value, bit):
    half = value.shape[0] // 2
    keep = lax.dynamic_slice_in_dim(value, bit * half, half, axis=0)
    send = lax.dynamic_slice_in_dim(value, (1 - bit) * half, half, axis=0)
    return keep, send.astype(BF)


def join(mine, other, bit):
    return jnp.where(bit == 0, jnp.concatenate([mine, other], axis=0), jnp.concatenate([other, mine], axis=0))


def reduce_all(keep, send, n_dp, n_group):
    x = lax.axis_index("group")
    value = keep + swap(send, "dp", 1, n_dp).astype(F32)
    for bits, bit in ((3, x // 2), (1, x % 2)):
        keep, send = split(value, bit)
        value = keep + swap(send, "group", bits, n_group).astype(F32)
    for bits in (2, 6, 8, 24):
        value = value + swap(value.astype(BF), "dp", bits, n_dp).astype(F32)
    value = value.astype(BF)
    for bits, bit in ((1, x % 2), (3, x // 2)):
        value = join(value, swap(value, "group", bits, n_group), bit)
    other = swap(value, "dp", 1, n_dp)
    return value, other


def on_device(token_tiles, segment_ids, visible_flags, tile_order, mask_token, norm_gains, shift_terms,
              attn_in, attn_out, mlp_in, hidden_shift, mlp_out, cotangent):
    tiles = token_tiles.shape[2]
    full_shape = (1, 1, tiles, S, D)
    order = tile_order.reshape(tiles)
    spots = jnp.arange(tiles, dtype=jnp.int32)
    inv_order = jnp.sum(jnp.where(order[None, :] == spots[:, None], spots[None, :], 0), axis=1).astype(jnp.int32)
    cot = lax.all_to_all(cotangent.reshape(tiles, S, D), "dp", split_axis=0, concat_axis=0, tiled=True)
    w = (norm_gains, shift_terms, hidden_shift, attn_in, attn_out, mlp_in, mlp_out)
    seg, vis = segment_ids.reshape(tiles, S), visible_flags.reshape(tiles, S)
    enc, *saved = run_encode(token_tiles.reshape(tiles, S, D), seg, vis, w)
    dec, ge, packed1 = run_decode(inv_order, enc, cot, seg, vis, mask_token.reshape(1, D), w)
    decoded = lax.all_to_all(dec, "dp", split_axis=0, concat_axis=0, tiled=True)
    core = lax.rem(lax.axis_index("dp"), 2).astype(jnp.int32)
    tg, keep, send = run_back(core.reshape(1), ge, packed1, saved, w)
    n_dp = lax.axis_size("dp")
    if n_dp == 32:
        decoded, send = lax.optimization_barrier((decoded, send))
        mine, other = reduce_all(keep, send, n_dp, lax.axis_size("group"))
    else:
        mine, other = keep.astype(BF), send
    g_m2, g_m1, g_wi, g_wo, g_gain, g_shift, g_hid, g_mask = unpack(core, mine, other)
    return (
        decoded.reshape(full_shape),
        tg.reshape(full_shape),
        g_mask.reshape(D),
        g_gain,
        g_shift,
        g_wi,
        g_wo,
        g_m1,
        g_hid,
        g_m2,
    )


def solution(mesh):
    tile5 = P("dp", "group", None, None, None)
    in_specs = (tile5, P("dp", "group", None, None), P("dp", "group", None, None), P("dp", "group", None),
                P(), P(), P(), P(), P(), P(), P(), P(), tile5)
    out_specs = (tile5, tile5) + (P(),) * 8
    return jax.shard_map(on_device, mesh=mesh, in_specs=in_specs, out_specs=out_specs, check_vma=False)
```

time: 268 us -> 193 us (0.72)
  Pallas kernels: 191 us -> 119 us
    pallas_call x2, Pallas kernels: 98.5 us -> 60.7 us  [the longest x1 33.6 us: run_back(): pl.pallas_call(back_kernel, grid_spec=pltpu.PrefetchScalarGridSpec(num_sc...]
    pallas_call x1, Pallas kernels: 90 us -> 55.9 us  [run_decode(): pl.pallas_call(decode_kernel, grid_spec=pltpu.PrefetchScalarGridSpec(num_...]
  transfers between devices with their start and end apart: 12 -> 12, of which waited for: 10 -> 11; matrix products, arithmetic and copies ran while one was open for 0% -> 0% of each run, Pallas kernels for 37% -> 32%
where the time goes in v3:
time: 193 us
  Pallas kernels  119 us (62%)
  starting transfers between devices  38.8 us (20%)
  waiting for transfers between devices  28.4 us (15%)
  local copies, waits for them, and re-layouts  3.45 us (2%)
  other arithmetic  2.22 us (1%)
    pallas_call x1, Pallas kernels, run_decode(): pl.pallas_call(decode_kernel, grid_spec=pltpu.PrefetchScalarGridSpec(num_...  55.9 us
    pallas_call x1, Pallas kernels, run_back(): pl.pallas_call(back_kernel, grid_spec=pltpu.PrefetchScalarGridSpec(num_sc...  33.6 us
    ppermute x10, waiting for transfers between devices, swap(): return lax.ppermute(value, axis, [(i, i ^ bits) for i in range(size)])  27.9 us
    pallas_call x1, Pallas kernels, run_encode(): pl.pallas_call(encode_kernel, grid=(steps,), in_specs=[step_spec((NT * NG...  27.1 us
    ppermute x10, starting transfers between devices, swap(): return lax.ppermute(value, axis, [(i, i ^ bits) for i in range(size)])  22.3 us
    all_to_all x1, starting transfers between devices, on_device(): lax.all_to_all(cotangent.reshape(tiles, S, D), 'dp', split_axis=0, concat...  9.62 us
    all_to_all x1, starting transfers between devices, on_device(): decoded = lax.all_to_all(dec, 'dp', split_axis=0, concat_axis=0, tiled=True)  6.83 us
  transfers between devices with their start and end apart: 12, of which 11 were waited for; matrix products, arithmetic and copies ran while one was open for 0% of the time, Pallas kernels for 32%

profile of v3, /device:TPU:1, one launch (start us, length us, event | category | flops | bytes accessed | tf_op | source)
XLA Modules:
  0.0 192.6 jit_solution(7557469523546871422)
XLA Ops:
  0.6 0.0 copy-start.3
  0.7 9.6 %all-to-all-start = ((bf16[64,128,128]{2,1,0:T(8,128)(2,1)}), bf16[64,128,128]{2,1,0:T(8,128)(2,1)S(1)}, u32[]{:S(2)}, u32[]{:S(2)}) async-start(bf16[64,128,128]{2,1,0:T(8,128)(2,1)} %bitcast.11), calls=%async_computation | async-start | bytes 4194304 | tf_op jit(solution)/shard_map/all_to_all | solution.py:695
  10.3 0.0 copy-done.3
  10.3 0.6 select_reduce_fusion.inv_order
  10.9 27.1 %shard_map.204 = (bf16[32,128,256]{2,1,0:T(8,128)(2,1)}, bf16[32,384,256]{2,1,0:T(8,128)(2,1)}, bf16[32,2,128,1024]{3,2,1,0:T(8,128)(2,1)}, f32[32,64,256]{2,1,0...) custom-call(bf16[64,128,128]{2,1,0:T(8,128)(2,1)} %bitcast.12, ...), custom_call_target="tpu_custom_call" | custom-call | flops 20000000000 | bytes 60000000 | tf_op jit(solution)/shard_map/pallas_call | solution.py:556
  38.0 0.5 all-to-all-done.rest_0_.rest_1_.rest_2_.rest_3_.rest_4_.rest_5_.rest_6_.rest_7_.rest_8_.rest_9_.rest_10_.rest_11_.rest_12_.rest_13_.rest_14_.rest_15_
  38.6 0.0 copy-start
  38.6 1.3 copy-done
  39.9 55.9 %shard_map.205 = (bf16[64,128,128]{2,1,0:T(8,128)(2,1)}, bf16[32,128,256]{2,1,0:T(8,128)(2,1)}, f32[1600,128]{1,0:T(8,128)}) custom-call(s32[64]{0:T(128)} %select_reduce_fusion.inv_order, bf16[32,128,256]{2,1,0:T(8,128)(2,1)} %get-tuple-element.38.enc_ref, bf16[64,128,128]{2,1,0:T(8,128)(2,1)} %copy-done, bf16[64,128,128]{2,1,0:T(8,128)(2,1)} %copy-done, ...), custom_call_target="tpu_custom_call" | custom-call | flops 40000000000 | bytes 10000000 | tf_op jit(solution)/shard_map/pallas_call | solution.py:574
  95.8 6.8 %all-to-all-start.1 = ((bf16[64,128,128]{2,1,0:T(8,128)(2,1)}), bf16[64,128,128]{2,1,0:T(8,128)(2,1)S(1)}, u32[]{:S(2)}, u32[]{:S(2)}) async-start(bf16[64,128,128]{2,1,0:T(8,128)(2,1)} %get-tuple-element.39), calls=%async_computation.1 | async-start | bytes 4194304 | tf_op jit(solution)/shard_map/all_to_all | solution.py:700
  102.6 33.6 %shard_map.206 = (f32[64,128,128]{2,1,0:T(8,128)}, f32[1600,128]{1,0:T(8,128)}, bf16[1600,128]{1,0:T(8,128)(2,1)}) custom-call(s32[1]{0:T(128)} %bitcast.6.core_ref, bf16[32,128,256]{2,1,0:T(8,128)(2,1)} %get-tuple-element.40.ge_ref, f32[1600,128]{1,0:T(8,128)} %get-tuple-element.41.other_ref, bf16[32,384,256]{2,1,0:T(8,128)(2,1)} %get-tuple-element.42.rest_0_, ...), custom_call_target="tpu_custom_call" | custom-call | flops 20000000000 | bytes 60000000 | tf_op jit(solution)/shard_map/pallas_call | solution.py:597
  136.2 0.0 all-to-all-done.1
  136.2 0.3 collective-permute-start
  136.6 1.7 collective-permute-done
  138.3 1.2 convert_add_fusion
  139.5 2.6 %collective-permute-start.1 = (bf16[800,128]{1,0:T(8,128)(2,1)S(1)}, bf16[800,128]{1,0:T(8,128)(2,1)S(1)}, u32[]{:S(2)}, u32[]{:S(2)}) collective-permute-start(bf16[800,128]{1,0:T(8,128)(2,1)S(1)} %dynamic-slice_convert_fusion), channel_id=1, source_target_pairs={{0,3},{1,2},{2,1},{3,0},{4,7},{5,6},{6,5},{7,4},{8,11},{9,10},{10,... | collective-permute-start | bytes 614408 | tf_op jit(solution)/shard_map/ppermute | solution.py:659
  142.1 5.2 %collective-permute-done.1 = bf16[800,128]{1,0:T(8,128)(2,1)S(1)} collective-permute-done((bf16[800,128]{1,0:T(8,128)(2,1)S(1)}, bf16[800,128]{1,0:T(8,128)(2,1)S(1)}, u32[]{:S(2)}, u32[]{:S(2)}) %collective-permute-start.1) | collective-permute-done | bytes 204832 | tf_op jit(solution)/shard_map/ppermute | solution.py:659
  147.3 0.1 collective-permute-start.2
  147.4 3.5 %collective-permute-done.2 = bf16[400,128]{1,0:T(8,128)(2,1)S(1)} collective-permute-done((bf16[400,128]{1,0:T(8,128)(2,1)S(1)}, bf16[400,128]{1,0:T(8,128)(2,1)S(1)}, u32[]{:S(2)}, u32[]{:S(2)}) %collective-permute-start.2) | collective-permute-done | bytes 102432 | tf_op jit(solution)/shard_map/ppermute | solution.py:659
  151.0 1.3 collective-permute-start.3
  152.3 2.3 %collective-permute-done.3 = bf16[400,128]{1,0:T(8,128)(2,1)S(1)} collective-permute-done((bf16[400,128]{1,0:T(8,128)(2,1)S(1)}, bf16[400,128]{1,0:T(8,128)(2,1)S(1)}, u32[]{:S(2)}, u32[]{:S(2)}) %collective-permute-start.3) | collective-permute-done | bytes 102432 | tf_op jit(solution)/shard_map/ppermute | solution.py:659
  154.6 2.5 %collective-permute-start.4 = (bf16[400,128]{1,0:T(8,128)(2,1)S(1)}, bf16[400,128]{1,0:T(8,128)(2,1)S(1)}, u32[]{:S(2)}, u32[]{:S(2)}) collective-permute-start(bf16[400,128]{1,0:T(8,128)(2,1)S(1)} %fusion), channel_id=1, source_target_pairs={{0,24},{4,28},{8,16},{12,20},{16,8},{20,12},{24,0},{28,4},{32,56},... | collective-permute-start | bytes 307208 | tf_op jit(solution)/shard_map/ppermute | solution.py:659
  157.1 2.3 %collective-permute-done.4 = bf16[400,128]{1,0:T(8,128)(2,1)S(1)} collective-permute-done((bf16[400,128]{1,0:T(8,128)(2,1)S(1)}, bf16[400,128]{1,0:T(8,128)(2,1)S(1)}, u32[]{:S(2)}, u32[]{:S(2)}) %collective-permute-start.4) | collective-permute-done | bytes 102432 | tf_op jit(solution)/shard_map/ppermute | solution.py:659
  159.4 0.1 fusion.3
  159.4 1.3 collective-permute-start.5
  160.8 2.6 %collective-permute-done.5 = bf16[400,128]{1,0:T(8,128)(2,1)S(1)} collective-permute-done((bf16[400,128]{1,0:T(8,128)(2,1)S(1)}, bf16[400,128]{1,0:T(8,128)(2,1)S(1)}, u32[]{:S(2)}, u32[]{:S(2)}) %collective-permute-start.5) | collective-permute-done | bytes 102432 | tf_op jit(solution)/shard_map/ppermute | solution.py:659
  163.4 2.6 %collective-permute-start.6 = (bf16[400,128]{1,0:T(8,128)(2,1)S(1)}, bf16[400,128]{1,0:T(8,128)(2,1)S(1)}, u32[]{:S(2)}, u32[]{:S(2)}) collective-permute-start(bf16[400,128]{1,0:T(8,128)(2,1)S(1)} %fusion.1), channel_id=1, source_target_pairs={{0,96},{4,100},{8,104},{12,108},{16,112},{20,116},{24,120},{28,124... | collective-permute-start | bytes 307208 | tf_op jit(solution)/shard_map/ppermute | solution.py:659
  165.9 2.2 %collective-permute-done.6 = bf16[400,128]{1,0:T(8,128)(2,1)S(1)} collective-permute-done((bf16[400,128]{1,0:T(8,128)(2,1)S(1)}, bf16[400,128]{1,0:T(8,128)(2,1)S(1)}, u32[]{:S(2)}, u32[]{:S(2)}) %collective-permute-start.6) | collective-permute-done | bytes 102432 | tf_op jit(solution)/shard_map/ppermute | solution.py:659
  168.2 0.1 collective-permute-start.7
  168.3 3.5 %collective-permute-done.7 = bf16[400,128]{1,0:T(8,128)(2,1)S(1)} collective-permute-done((bf16[400,128]{1,0:T(8,128)(2,1)S(1)}, bf16[400,128]{1,0:T(8,128)(2,1)S(1)}, u32[]{:S(2)}, u32[]{:S(2)}) %collective-permute-start.7) | collective-permute-done | bytes 102432 | tf_op jit(solution)/shard_map/ppermute | solution.py:659
  171.8 0.1 maximum_select_fusion.1
  171.9 2.6 %collective-permute-start.8 = (bf16[800,128]{1,0:T(8,128)(2,1)S(1)}, bf16[800,128]{1,0:T(8,128)(2,1)S(1)}, u32[]{:S(2)}, u32[]{:S(2)}) collective-permute-start(bf16[800,128]{1,0:T(8,128)(2,1)S(1)} %maximum_select_fusion.1), channel_id=1, source_target_pairs={{0,3},{1,2},{2,1},{3,0},{4,7},{5,6},{6,5},{7,4},{8,11},{9,10},{10,... | collective-permute-start | bytes 614408 | tf_op jit(solution)/shard_map/ppermute | solution.py:659
  174.4 3.3 %collective-permute-done.8 = bf16[800,128]{1,0:T(8,128)(2,1)S(1)} collective-permute-done((bf16[800,128]{1,0:T(8,128)(2,1)S(1)}, bf16[800,128]{1,0:T(8,128)(2,1)S(1)}, u32[]{:S(2)}, u32[]{:S(2)}) %collective-permute-start.8) | collective-permute-done | bytes 204832 | tf_op jit(solution)/shard_map/ppermute | solution.py:659
  177.8 0.1 maximum_select_fusion.mine
  177.9 0.0 copy-start.1
  177.9 8.9 %collective-permute-start.9 = (bf16[1600,128]{1,0:T(8,128)(2,1)S(1)}, bf16[1600,128]{1,0:T(8,128)(2,1)S(1)}, u32[]{:S(2)}, u32[]{:S(2)}) collective-permute-start(bf16[1600,128]{1,0:T(8,128)(2,1)S(1)} %maximum_select_fusion.mine), channel_id=1, source_target_pairs={{0,4},{4,0},{8,12},{12,8},{16,20},{20,16},{24,28},{28,24},{32,36},... | collective-permute-start | bytes 1228808 | tf_op jit(solution)/shard_map/ppermute | solution.py:659
  186.8 1.4 collective-permute-done.9.other
  188.1 0.0 copy-done.1
  188.1 0.0 copy-start.2
  188.1 0.8 copy-done.2
  188.9 2.4 %shard_map.207 = (f32[2,512,128]{2,1,0:T(8,128)}, f32[2,128,512]{2,1,0:T(8,128)}, f32[2,128,384]{2,1,0:T(8,128)}, f32[2,128,128]{2,1,0:T(8,128)}, f32[2,2,128]{2...) custom-call(s32[1]{0:T(128)} %bitcast.6.core_ref, bf16[1600,128]{1,0:T(8,128)(2,1)} %copy-done.1, ...), custom_call_target="tpu_custom_call" | custom-call | tf_op jit(solution)/shard_map/pallas_call | solution.py:645
  191.3 1.3 copy.24
  (7 shorter events, 0.2 us)
Async XLA Ops:
  0.6 9.6 %copy-start.3 = (s32[1,1,64]{2,1,0:T(1,128)S(1)}, s32[1,1,64]{2,1,0:T(1,128)}, u32[]{:S(2)}) copy-start(s32[1,1,64]{2,1,0:T(1,128)} %param.16) | copy-start | bytes 772
  0.7 37.9 %all-to-all-start = ((bf16[64,128,128]{2,1,0:T(8,128)(2,1)}), bf16[64,128,128]{2,1,0:T(8,128)(2,1)S(1)}, u32[]{:S(2)}, u32[]{:S(2)}) async-start(bf16[64,128,128]{2,1,0:T(8,128)(2,1)} %bitcast.11), calls=%async_computation | async-start | bytes 4194304 | tf_op jit(solution)/shard_map/all_to_all | solution.py:695
  38.6 1.3 copy-start
  95.8 40.5 %all-to-all-start.1 = ((bf16[64,128,128]{2,1,0:T(8,128)(2,1)}), bf16[64,128,128]{2,1,0:T(8,128)(2,1)S(1)}, u32[]{:S(2)}, u32[]{:S(2)}) async-start(bf16[64,128,128]{2,1,0:T(8,128)(2,1)} %get-tuple-element.39), calls=%async_computation.1 | async-start | bytes 4194304 | tf_op jit(solution)/shard_map/all_to_all | solution.py:700
  136.2 2.0 %collective-permute-start = (bf16[1600,128]{1,0:T(8,128)(2,1)}, bf16[1600,128]{1,0:T(8,128)(2,1)S(1)}, u32[]{:S(2)}, u32[]{:S(2)}) collective-permute-start(bf16[1600,128]{1,0:T(8,128)(2,1)} %get-tuple-element.57), channel_id=1, source_target_pairs={{0,4},{4,0},{8,12},{12,8},{16,20},{20,16},{24,28},{28,24},{32,36},... | collective-permute-start | bytes 1228808 | tf_op jit(solution)/shard_map/ppermute | solution.py:659
  139.5 7.7 %collective-permute-start.1 = (bf16[800,128]{1,0:T(8,128)(2,1)S(1)}, bf16[800,128]{1,0:T(8,128)(2,1)S(1)}, u32[]{:S(2)}, u32[]{:S(2)}) collective-permute-start(bf16[800,128]{1,0:T(8,128)(2,1)S(1)} %dynamic-slice_convert_fusion), channel_id=1, source_target_pairs={{0,3},{1,2},{2,1},{3,0},{4,7},{5,6},{6,5},{7,4},{8,11},{9,10},{10,... | collective-permute-start | bytes 614408 | tf_op jit(solution)/shard_map/ppermute | solution.py:659
  147.3 3.6 %collective-permute-start.2 = (bf16[400,128]{1,0:T(8,128)(2,1)S(1)}, bf16[400,128]{1,0:T(8,128)(2,1)S(1)}, u32[]{:S(2)}, u32[]{:S(2)}) collective-permute-start(bf16[400,128]{1,0:T(8,128)(2,1)S(1)} %dynamic-slice_convert_fusion.1), channel_id=1, source_target_pairs={{0,1},{1,0},{2,3},{3,2},{4,5},{5,4},{6,7},{7,6},{8,9},{9,8},{10,11... | collective-permute-start | bytes 307208 | tf_op jit(solution)/shard_map/ppermute | solution.py:659
  151.0 3.6 %collective-permute-start.3 = (bf16[400,128]{1,0:T(8,128)(2,1)S(1)}, bf16[400,128]{1,0:T(8,128)(2,1)S(1)}, u32[]{:S(2)}, u32[]{:S(2)}) collective-permute-start(bf16[400,128]{1,0:T(8,128)(2,1)S(1)} %fusion.2), channel_id=1, source_target_pairs={{0,8},{4,12},{8,0},{12,4},{16,24},{20,28},{24,16},{28,20},{32,40},... | collective-permute-start | bytes 307208 | tf_op jit(solution)/shard_map/ppermute | solution.py:659
  154.6 4.8 %collective-permute-start.4 = (bf16[400,128]{1,0:T(8,128)(2,1)S(1)}, bf16[400,128]{1,0:T(8,128)(2,1)S(1)}, u32[]{:S(2)}, u32[]{:S(2)}) collective-permute-start(bf16[400,128]{1,0:T(8,128)(2,1)S(1)} %fusion), channel_id=1, source_target_pairs={{0,24},{4,28},{8,16},{12,20},{16,8},{20,12},{24,0},{28,4},{32,56},... | collective-permute-start | bytes 307208 | tf_op jit(solution)/shard_map/ppermute | solution.py:659
  159.4 3.9 %collective-permute-start.5 = (bf16[400,128]{1,0:T(8,128)(2,1)S(1)}, bf16[400,128]{1,0:T(8,128)(2,1)S(1)}, u32[]{:S(2)}, u32[]{:S(2)}) collective-permute-start(bf16[400,128]{1,0:T(8,128)(2,1)S(1)} %get-tuple-element.66), channel_id=1, source_target_pairs={{0,32},{4,36},{8,40},{12,44},{16,48},{20,52},{24,56},{28,60},{32,0... | collective-permute-start | bytes 307208 | tf_op jit(solution)/shard_map/ppermute | solution.py:659
  163.4 4.8 %collective-permute-start.6 = (bf16[400,128]{1,0:T(8,128)(2,1)S(1)}, bf16[400,128]{1,0:T(8,128)(2,1)S(1)}, u32[]{:S(2)}, u32[]{:S(2)}) collective-permute-start(bf16[400,128]{1,0:T(8,128)(2,1)S(1)} %fusion.1), channel_id=1, source_target_pairs={{0,96},{4,100},{8,104},{12,108},{16,112},{20,116},{24,120},{28,124... | collective-permute-start | bytes 307208 | tf_op jit(solution)/shard_map/ppermute | solution.py:659
  168.2 3.6 %collective-permute-start.7 = (bf16[400,128]{1,0:T(8,128)(2,1)S(1)}, bf16[400,128]{1,0:T(8,128)(2,1)S(1)}, u32[]{:S(2)}, u32[]{:S(2)}) collective-permute-start(bf16[400,128]{1,0:T(8,128)(2,1)S(1)} %add_convert_fusion), channel_id=1, source_target_pairs={{0,1},{1,0},{2,3},{3,2},{4,5},{5,4},{6,7},{7,6},{8,9},{9,8},{10,11... | collective-permute-start | bytes 307208 | tf_op jit(solution)/shard_map/ppermute | solution.py:659
  171.9 5.9 %collective-permute-start.8 = (bf16[800,128]{1,0:T(8,128)(2,1)S(1)}, bf16[800,128]{1,0:T(8,128)(2,1)S(1)}, u32[]{:S(2)}, u32[]{:S(2)}) collective-permute-start(bf16[800,128]{1,0:T(8,128)(2,1)S(1)} %maximum_select_fusion.1), channel_id=1, source_target_pairs={{0,3},{1,2},{2,1},{3,0},{4,7},{5,6},{6,5},{7,4},{8,11},{9,10},{10,... | collective-permute-start | bytes 614408 | tf_op jit(solution)/shard_map/ppermute | solution.py:659
  177.9 10.3 %copy-start.1 = (bf16[1600,128]{1,0:T(8,128)(2,1)}, bf16[1600,128]{1,0:T(8,128)(2,1)S(1)}, u32[]{:S(2)}) copy-start(bf16[1600,128]{1,0:T(8,128)(2,1)S(1)} %maximum_select_fusion.mine) | copy-start | bytes 1228804
  177.9 10.3 %collective-permute-start.9 = (bf16[1600,128]{1,0:T(8,128)(2,1)S(1)}, bf16[1600,128]{1,0:T(8,128)(2,1)S(1)}, u32[]{:S(2)}, u32[]{:S(2)}) collective-permute-start(bf16[1600,128]{1,0:T(8,128)(2,1)S(1)} %maximum_select_fusion.mine), channel_id=1, source_target_pairs={{0,4},{4,0},{8,12},{12,8},{16,20},{20,16},{24,28},{28,24},{32,36},... | collective-permute-start | bytes 1228808 | tf_op jit(solution)/shard_map/ppermute | solution.py:659
  188.1 0.8 copy-start.2

commit v4 on v3

--- a/solution.py
+++ b/solution.py
@@ -78,6 +78,12 @@
     return jnp.concatenate([jnp.transpose(two[:, 0:S]), jnp.transpose(two[:, S:2 * S])], axis=1)
 
 
+def quad_lhs(one, two):
+    zero = jnp.zeros_like(one)
+    return jnp.concatenate(
+        [jnp.concatenate([one, zero], axis=1), jnp.concatenate([zero, two], axis=1)], axis=0)
+
+
 def pair_lhs(two):
     zero = jnp.zeros((HEAD, S), BF)
     return jnp.concatenate(
@@ -89,12 +95,14 @@
 
 def mix_values(sv, t, h):
     sl = slice(t * S, (t + 1) * S)
-    v = sv["p"][2 * D + HEAD * h:2 * D + HEAD * (h + 2), sl]
-    o = nn(jnp.concatenate([v, jnp.ones((HEAD, S), BF)], axis=0), sv["e"][t, :, h * S:(h + 2) * S])
+    v = [sv["p"][2 * D + HEAD * (h + 2 * q):2 * D + HEAD * (h + 2 * q + 2), sl] for q in range(2)]
+    ones = jnp.ones((HEAD // 2, S), BF)
+    left = jnp.concatenate([quad_lhs(*v), quad_lhs(ones, ones)], axis=0)
+    o = nn(left, jnp.concatenate([sv["e"][t, :, (h + 2 * q) * S:(h + 2 * q + 2) * S] for q in range(2)], axis=0))
     totals = []
-    for k in range(2):
-        kl = slice(k * S, (k + 1) * S)
-        totals.append(o[2 * HEAD:2 * HEAD + 8, kl])
+    for k in range(4):
+        kl = slice(k % 2 * S, (k % 2 + 1) * S)
+        totals.append(o[4 * HEAD + 8 * (k // 2):4 * HEAD + 8 * (k // 2) + 8, kl])
         inv = 1.0 / totals[k]
         sv["inv"][8 * (h + k):8 * (h + k) + 8, sl] = inv
         sv["o"][HEAD * (h + k):HEAD * (h + k + 1), sl] = (
@@ -118,7 +126,8 @@
                     part = scores[:, k * S:(k + 1) * S] + biases[t]
                     e = jnp.exp2(part - jnp.max(part, axis=0, keepdims=True))
                     sv["e"][t, :, (h + k) * S:(h + k + 1) * S] = e.astype(BF)
-                mix_values(sv, t, h)
+                if h % 4:
+                    mix_values(sv, t, h - 2)
             return carry
 
         lax.fori_loop(0, ng, one, 0)
@@ -145,7 +154,7 @@
             for k in range(2):
                 e = jnp.exp2(scores[:, k * S:(k + 1) * S] + biases[t])
                 sv["e"][t, :, (h + k) * S:(h + k + 1) * S] = e.astype(BF)
-        for t, h in UNITS[max(turn - per_turn, 0):turn]:
+        for t, h in UNITS[max(turn - per_turn, 0):turn:2]:
             for total in mix_values(sv, t, h):
                 share["low"] = total if share["low"] is None else jnp.minimum(share["low"], total)
                 share["high"] = total if share["high"] is None else jnp.maximum(share["high"], total)
@@ -192,12 +201,12 @@
     gz = g2.astype(BF)
     sv["gz"][...] = gz
     gu = None
-    for i in range(5):
+    for i in range(3):
         done = gu
-        if i < 4:
-            gu = nn(m2[i * D:(i + 1) * D, :], gz)
+        if i < 2:
+            gu = nn(m2[i * 2 * D:(i + 1) * 2 * D, :], gz)
         if i >= 1:
-            rows = slice((i - 1) * D, i * D)
+            rows = slice((i - 1) * 2 * D, i * 2 * D)
             sv["gh"][rows, :] = (done * sv["gp"][rows, :].astype(F32)).astype(BF)
         yield
     gb = nn(m1[...], sv["gh"][...])
@@ -239,15 +248,19 @@
                 kl = slice(k * S, (k + 1) * S)
                 e = sv["e"][t, :, (h + k) * S:(h + k + 1) * S].astype(F32)
                 sv["gs"][i, :, kl] = (e * (gf[:, kl] - rs[k])).astype(BF)
-        for i in range(max(turn - per_turn, 0), turn):
+        for i in range(max(turn - per_turn, 0), turn, 2):
             t, h = UNITS[i]
             sl = slice(t * S, (t + 1) * S)
-            pv = nn(gobs[i], flip_pair(sv["e"][t, :, h * S:(h + 2) * S]))
-            pq = nn(sv["p"][D + HEAD * h:D + HEAD * (h + 2), sl], sv["gs"][i])
-            pk = nn(sv["p"][HEAD * h:HEAD * (h + 2), sl], flip_pair(sv["gs"][i]))
-            for k in range(2):
+            gs2 = [sv["gs"][i], sv["gs"][i + 1]]
+            e2 = [sv["e"][t, :, (h + 2 * q) * S:(h + 2 * q + 2) * S] for q in range(2)]
+            pv = nn(quad_lhs(gobs[i], gobs[i + 1]), jnp.concatenate([flip_pair(v) for v in e2], axis=0))
+            pq = nn(quad_lhs(*[sv["p"][D + HEAD * (h + 2 * q):D + HEAD * (h + 2 * q + 2), sl] for q in range(2)]),
+                    jnp.concatenate(gs2, axis=0))
+            pk = nn(quad_lhs(*[sv["p"][HEAD * (h + 2 * q):HEAD * (h + 2 * q + 2), sl] for q in range(2)]),
+                    jnp.concatenate([flip_pair(v) for v in gs2], axis=0))
+            for k in range(4):
                 kr = slice(HEAD * k, HEAD * (k + 1))
-                kl = slice(k * S, (k + 1) * S)
+                kl = slice(k % 2 * S, (k % 2 + 1) * S)
                 at = HEAD * (h + k)
                 sv["gpk"][at:at + HEAD, sl] = (pq[kr, kl] * 0.25).astype(BF)
                 sv["gpk"][D + at:D + at + HEAD, sl] = (pk[kr, kl] * LN2).astype(BF)
@@ -655,8 +668,26 @@
     )(core.reshape(1).astype(jnp.int32), mine, other)
 
 
-def swap(value, axis, bits, size):
-    return lax.ppermute(value, axis, [(i, i ^ bits) for i in range(size)])
+def partner(i, first, second, n_group):
+    dp, x = i // n_group, i % n_group
+    y, z, core = dp // 8, dp % 8 // 2, dp % 2
+    axis, bits = second if core else first
+    if axis == "x":
+        x ^= bits
+    elif axis == "y":
+        y ^= bits
+    else:
+        z ^= bits
+    return (y * 8 + z * 2 + core) * n_group + x
+
+
+def swap(value, first, second, n_dp, n_group):
+    pairs = [(i, partner(i, first, second, n_group)) for i in range(n_dp * n_group)]
+    return lax.ppermute(value, ("dp", "group"), pairs)
+
+
+def swap_cores(value, n_dp):
+    return lax.ppermute(value, "dp", [(i, i ^ 1) for i in range(n_dp)])
 
 
 def split(value, bit):
@@ -670,19 +701,19 @@
     return jnp.where(bit == 0, jnp.concatenate([mine, other], axis=0), jnp.concatenate([other, mine], axis=0))
 
 
-def reduce_all(keep, send, n_dp, n_group):
-    x = lax.axis_index("group")
-    value = keep + swap(send, "dp", 1, n_dp).astype(F32)
-    for bits, bit in ((3, x // 2), (1, x % 2)):
+def reduce_all(core, keep, send, n_dp, n_group):
+    place = jnp.where(core == 0, lax.axis_index("group"), lax.axis_index("dp") // 8)
+    value = keep + swap_cores(send, n_dp).astype(F32)
+    for bits, bit in ((3, place // 2), (1, place % 2)):
         keep, send = split(value, bit)
-        value = keep + swap(send, "group", bits, n_group).astype(F32)
-    for bits in (2, 6, 8, 24):
-        value = value + swap(value.astype(BF), "dp", bits, n_dp).astype(F32)
+        value = keep + swap(send, ("x", bits), ("y", bits), n_dp, n_group).astype(F32)
+    for first, second in (("y", "z"), ("z", "x")):
+        for bits in (3, 1):
+            value = value + swap(value.astype(BF), (first, bits), (second, bits), n_dp, n_group).astype(F32)
     value = value.astype(BF)
-    for bits, bit in ((1, x % 2), (3, x // 2)):
-        value = join(value, swap(value, "group", bits, n_group), bit)
-    other = swap(value, "dp", 1, n_dp)
-    return value, other
+    for bits, bit in ((1, place % 2), (3, place // 2)):
+        value = join(value, swap(value, ("x", bits), ("y", bits), n_dp, n_group), bit)
+    return value, swap_cores(value, n_dp)
 
 
 def on_device(token_tiles, segment_ids, visible_flags, tile_order, mask_token, norm_gains, shift_terms,
@@ -703,7 +734,7 @@
     n_dp = lax.axis_size("dp")
     if n_dp == 32:
         decoded, send = lax.optimization_barrier((decoded, send))
-        mine, other = reduce_all(keep, send, n_dp, lax.axis_size("group"))
+        mine, other = reduce_all(core, keep, send, n_dp, lax.axis_size("group"))
     else:
         mine, other = keep.astype(BF), send
     g_m2, g_m1, g_wi, g_wo, g_gain, g_shift, g_hid, g_mask = unpack(core, mine, other)

time: 193 us -> 188 us (0.974)
  Pallas kernels: 119 us -> 116 us
  transfers between devices with their start and end apart: 12 -> 12, of which waited for: 11 -> 11; matrix products, arithmetic and copies ran while one was open for 0% -> 0% of each run, Pallas kernels for 32% -> 31%
where the time goes in v4:
time: 188 us
  Pallas kernels  116 us (62%)
  starting transfers between devices  37 us (20%)
  waiting for transfers between devices  28.7 us (15%)
  local copies, waits for them, and re-layouts  3.45 us (2%)
  other arithmetic  2.22 us (1%)
    pallas_call x1, Pallas kernels, run_decode(): pl.pallas_call(decode_kernel, grid_spec=pltpu.PrefetchScalarGridSpec(num_...  54.5 us
    pallas_call x1, Pallas kernels, run_back(): pl.pallas_call(back_kernel, grid_spec=pltpu.PrefetchScalarGridSpec(num_sc...  31.9 us
    pallas_call x1, Pallas kernels, run_encode(): pl.pallas_call(encode_kernel, grid=(steps,), in_specs=[step_spec((NT * NG...  26.7 us
    ppermute x8, waiting for transfers between devices, swap(): return lax.ppermute(value, ('dp', 'group'), pairs)  24.6 us
    ppermute x8, starting transfers between devices, swap(): return lax.ppermute(value, ('dp', 'group'), pairs)  11.4 us
    all_to_all x1, starting transfers between devices, on_device(): lax.all_to_all(cotangent.reshape(tiles, S, D), 'dp', split_axis=0, concat...  9.62 us
    ppermute x2, starting transfers between devices, swap_cores(): return lax.ppermute(value, 'dp', [(i, i ^ 1) for i in range(n_dp)])  9.54 us
    all_to_all x1, starting transfers between devices, on_device(): decoded = lax.all_to_all(dec, 'dp', split_axis=0, concat_axis=0, tiled=True)  6.49 us
  transfers between devices with their start and end apart: 12, of which 11 were waited for; matrix products, arithmetic and copies ran while one was open for 0% of the time, Pallas kernels for 31%

profile of v4, /device:TPU:1, one launch (start us, length us, event | category | flops | bytes accessed | tf_op | source)
XLA Modules:
  0.0 187.8 jit_solution(12788463245832153902)
XLA Ops:
  0.6 0.0 copy-start.3
  0.7 9.6 %all-to-all-start = ((bf16[64,128,128]{2,1,0:T(8,128)(2,1)}), bf16[64,128,128]{2,1,0:T(8,128)(2,1)S(1)}, u32[]{:S(2)}, u32[]{:S(2)}) async-start(bf16[64,128,128]{2,1,0:T(8,128)(2,1)} %bitcast.11), calls=%async_computation | async-start | bytes 4194304 | tf_op jit(solution)/shard_map/all_to_all | solution.py:726
  10.3 0.0 copy-done.3
  10.3 0.6 select_reduce_fusion.inv_order
  10.9 26.7 %shard_map.204 = (bf16[32,128,256]{2,1,0:T(8,128)(2,1)}, bf16[32,384,256]{2,1,0:T(8,128)(2,1)}, bf16[32,2,128,1024]{3,2,1,0:T(8,128)(2,1)}, f32[32,64,256]{2,1,0...) custom-call(bf16[64,128,128]{2,1,0:T(8,128)(2,1)} %bitcast.12, ...), custom_call_target="tpu_custom_call" | custom-call | flops 20000000000 | bytes 60000000 | tf_op jit(solution)/shard_map/pallas_call | solution.py:569
  37.6 1.0 all-to-all-done.rest_0_.rest_1_.rest_2_.rest_3_.rest_4_.rest_5_.rest_6_.rest_7_.rest_8_.rest_9_.rest_10_.rest_11_.rest_12_.rest_13_.rest_14_.rest_15_
  38.6 0.0 copy-start
  38.6 1.3 copy-done
  39.9 54.5 %shard_map.205 = (bf16[64,128,128]{2,1,0:T(8,128)(2,1)}, bf16[32,128,256]{2,1,0:T(8,128)(2,1)}, f32[1600,128]{1,0:T(8,128)}) custom-call(s32[64]{0:T(128)} %select_reduce_fusion.inv_order, bf16[32,128,256]{2,1,0:T(8,128)(2,1)} %get-tuple-element.38.enc_ref, bf16[64,128,128]{2,1,0:T(8,128)(2,1)} %copy-done, bf16[64,128,128]{2,1,0:T(8,128)(2,1)} %copy-done, ...), custom_call_target="tpu_custom_call" | custom-call | flops 40000000000 | bytes 10000000 | tf_op jit(solution)/shard_map/pallas_call | solution.py:587
  94.5 6.5 %all-to-all-start.1 = ((bf16[64,128,128]{2,1,0:T(8,128)(2,1)}), bf16[64,128,128]{2,1,0:T(8,128)(2,1)S(1)}, u32[]{:S(2)}, u32[]{:S(2)}) async-start(bf16[64,128,128]{2,1,0:T(8,128)(2,1)} %get-tuple-element.39), calls=%async_computation.1 | async-start | bytes 4194304 | tf_op jit(solution)/shard_map/all_to_all | solution.py:731
  101.0 31.9 %shard_map.206 = (f32[64,128,128]{2,1,0:T(8,128)}, f32[1600,128]{1,0:T(8,128)}, bf16[1600,128]{1,0:T(8,128)(2,1)}) custom-call(s32[1]{0:T(128)} %bitcast.6.core_ref, bf16[32,128,256]{2,1,0:T(8,128)(2,1)} %get-tuple-element.40.ge_ref, f32[1600,128]{1,0:T(8,128)} %get-tuple-element.41.other_ref, bf16[32,384,256]{2,1,0:T(8,128)(2,1)} %get-tuple-element.42.rest_0_, ...), custom_call_target="tpu_custom_call" | custom-call | flops 20000000000 | bytes 60000000 | tf_op jit(solution)/shard_map/pallas_call | solution.py:610
  132.9 0.0 all-to-all-done.1
  132.9 0.3 collective-permute-start
  133.2 1.7 collective-permute-done
  134.9 1.2 convert_add_fusion
  136.2 2.7 %collective-permute-start.1 = (bf16[800,128]{1,0:T(8,128)(2,1)S(1)}, bf16[800,128]{1,0:T(8,128)(2,1)S(1)}, u32[]{:S(2)}, u32[]{:S(2)}) collective-permute-start(bf16[800,128]{1,0:T(8,128)(2,1)S(1)} %dynamic-slice_convert_fusion), channel_id=1, source_target_pairs={{0,3},{1,2},{2,1},{3,0},{4,100},{5,101},{6,102},{7,103},{8,11},{9,... | collective-permute-start | bytes 614408 | tf_op jit(solution)/shard_map/ppermute | solution.py:686
  138.9 3.5 %collective-permute-done.1 = bf16[800,128]{1,0:T(8,128)(2,1)S(1)} collective-permute-done((bf16[800,128]{1,0:T(8,128)(2,1)S(1)}, bf16[800,128]{1,0:T(8,128)(2,1)S(1)}, u32[]{:S(2)}, u32[]{:S(2)}) %collective-permute-start.1) | collective-permute-done | bytes 204832 | tf_op jit(solution)/shard_map/ppermute | solution.py:686
  142.4 0.2 collective-permute-start.2
  142.7 3.3 %collective-permute-done.2 = bf16[400,128]{1,0:T(8,128)(2,1)S(1)} collective-permute-done((bf16[400,128]{1,0:T(8,128)(2,1)S(1)}, bf16[400,128]{1,0:T(8,128)(2,1)S(1)}, u32[]{:S(2)}, u32[]{:S(2)}) %collective-permute-start.2) | collective-permute-done | bytes 102432 | tf_op jit(solution)/shard_map/ppermute | solution.py:686
  146.1 2.7 %collective-permute-start.3 = (bf16[400,128]{1,0:T(8,128)(2,1)S(1)}, bf16[400,128]{1,0:T(8,128)(2,1)S(1)}, u32[]{:S(2)}, u32[]{:S(2)}) collective-permute-start(bf16[400,128]{1,0:T(8,128)(2,1)S(1)} %fusion.2), channel_id=1, source_target_pairs={{0,96},{1,97},{2,98},{3,99},{4,28},{5,29},{6,30},{7,31},{8,104},{9... | collective-permute-start | bytes 307208 | tf_op jit(solution)/shard_map/ppermute | solution.py:686
  148.7 2.1 %collective-permute-done.3 = bf16[400,128]{1,0:T(8,128)(2,1)S(1)} collective-permute-done((bf16[400,128]{1,0:T(8,128)(2,1)S(1)}, bf16[400,128]{1,0:T(8,128)(2,1)S(1)}, u32[]{:S(2)}, u32[]{:S(2)}) %collective-permute-start.3) | collective-permute-done | bytes 102432 | tf_op jit(solution)/shard_map/ppermute | solution.py:686
  150.9 0.3 collective-permute-start.4
  151.2 3.3 %collective-permute-done.4 = bf16[400,128]{1,0:T(8,128)(2,1)S(1)} collective-permute-done((bf16[400,128]{1,0:T(8,128)(2,1)S(1)}, bf16[400,128]{1,0:T(8,128)(2,1)S(1)}, u32[]{:S(2)}, u32[]{:S(2)}) %collective-permute-start.4) | collective-permute-done | bytes 102432 | tf_op jit(solution)/shard_map/ppermute | solution.py:686
  154.5 0.1 fusion.3
  154.6 2.5 %collective-permute-start.5 = (bf16[400,128]{1,0:T(8,128)(2,1)S(1)}, bf16[400,128]{1,0:T(8,128)(2,1)S(1)}, u32[]{:S(2)}, u32[]{:S(2)}) collective-permute-start(bf16[400,128]{1,0:T(8,128)(2,1)S(1)} %get-tuple-element.66), channel_id=1, source_target_pairs={{0,24},{1,25},{2,26},{3,27},{4,7},{5,6},{6,5},{7,4},{8,16},{9,17},... | collective-permute-start | bytes 307208 | tf_op jit(solution)/shard_map/ppermute | solution.py:686
  157.0 2.3 %collective-permute-done.5 = bf16[400,128]{1,0:T(8,128)(2,1)S(1)} collective-permute-done((bf16[400,128]{1,0:T(8,128)(2,1)S(1)}, bf16[400,128]{1,0:T(8,128)(2,1)S(1)}, u32[]{:S(2)}, u32[]{:S(2)}) %collective-permute-start.5) | collective-permute-done | bytes 102432 | tf_op jit(solution)/shard_map/ppermute | solution.py:686
  159.4 0.1 collective-permute-start.6
  159.5 3.5 %collective-permute-done.6 = bf16[400,128]{1,0:T(8,128)(2,1)S(1)} collective-permute-done((bf16[400,128]{1,0:T(8,128)(2,1)S(1)}, bf16[400,128]{1,0:T(8,128)(2,1)S(1)}, u32[]{:S(2)}, u32[]{:S(2)}) %collective-permute-start.6) | collective-permute-done | bytes 102432 | tf_op jit(solution)/shard_map/ppermute | solution.py:686
  163.0 0.2 collective-permute-start.7
  163.3 3.3 %collective-permute-done.7 = bf16[400,128]{1,0:T(8,128)(2,1)S(1)} collective-permute-done((bf16[400,128]{1,0:T(8,128)(2,1)S(1)}, bf16[400,128]{1,0:T(8,128)(2,1)S(1)}, u32[]{:S(2)}, u32[]{:S(2)}) %collective-permute-start.7) | collective-permute-done | bytes 102432 | tf_op jit(solution)/shard_map/ppermute | solution.py:686
  166.6 0.1 maximum_select_fusion.1
  166.7 2.7 %collective-permute-start.8 = (bf16[800,128]{1,0:T(8,128)(2,1)S(1)}, bf16[800,128]{1,0:T(8,128)(2,1)S(1)}, u32[]{:S(2)}, u32[]{:S(2)}) collective-permute-start(bf16[800,128]{1,0:T(8,128)(2,1)S(1)} %maximum_select_fusion.1), channel_id=1, source_target_pairs={{0,3},{1,2},{2,1},{3,0},{4,100},{5,101},{6,102},{7,103},{8,11},{9,... | collective-permute-start | bytes 614408 | tf_op jit(solution)/shard_map/ppermute | solution.py:686
  169.4 3.2 %collective-permute-done.8 = bf16[800,128]{1,0:T(8,128)(2,1)S(1)} collective-permute-done((bf16[800,128]{1,0:T(8,128)(2,1)S(1)}, bf16[800,128]{1,0:T(8,128)(2,1)S(1)}, u32[]{:S(2)}, u32[]{:S(2)}) %collective-permute-start.8) | collective-permute-done | bytes 204832 | tf_op jit(solution)/shard_map/ppermute | solution.py:686
  172.6 0.1 maximum_select_fusion.mine
  172.7 0.0 copy-start.1
  172.7 9.2 %collective-permute-start.9 = (bf16[1600,128]{1,0:T(8,128)(2,1)S(1)}, bf16[1600,128]{1,0:T(8,128)(2,1)S(1)}, u32[]{:S(2)}, u32[]{:S(2)}) collective-permute-start(bf16[1600,128]{1,0:T(8,128)(2,1)S(1)} %maximum_select_fusion.mine), channel_id=1, source_target_pairs={{0,4},{4,0},{8,12},{12,8},{16,20},{20,16},{24,28},{28,24},{32,36},... | collective-permute-start | bytes 1228808 | tf_op jit(solution)/shard_map/ppermute | solution.py:690
  181.9 1.4 collective-permute-done.9.other
  183.3 0.0 copy-done.1
  183.3 0.0 copy-start.2
  183.3 0.8 copy-done.2
  184.0 2.4 %shard_map.207 = (f32[2,512,128]{2,1,0:T(8,128)}, f32[2,128,512]{2,1,0:T(8,128)}, f32[2,128,384]{2,1,0:T(8,128)}, f32[2,128,128]{2,1,0:T(8,128)}, f32[2,2,128]{2...) custom-call(s32[1]{0:T(128)} %bitcast.6.core_ref, bf16[1600,128]{1,0:T(8,128)(2,1)} %copy-done.1, ...), custom_call_target="tpu_custom_call" | custom-call | tf_op jit(solution)/shard_map/pallas_call | solution.py:658
  186.4 1.3 copy.24
  (7 shorter events, 0.2 us)
Async XLA Ops:
  0.6 9.6 %copy-start.3 = (s32[1,1,64]{2,1,0:T(1,128)S(1)}, s32[1,1,64]{2,1,0:T(1,128)}, u32[]{:S(2)}) copy-start(s32[1,1,64]{2,1,0:T(1,128)} %param.16) | copy-start | bytes 772
  0.7 37.9 %all-to-all-start = ((bf16[64,128,128]{2,1,0:T(8,128)(2,1)}), bf16[64,128,128]{2,1,0:T(8,128)(2,1)S(1)}, u32[]{:S(2)}, u32[]{:S(2)}) async-start(bf16[64,128,128]{2,1,0:T(8,128)(2,1)} %bitcast.11), calls=%async_computation | async-start | bytes 4194304 | tf_op jit(solution)/shard_map/all_to_all | solution.py:726
  38.6 1.3 copy-start
  94.5 38.4 %all-to-all-start.1 = ((bf16[64,128,128]{2,1,0:T(8,128)(2,1)}), bf16[64,128,128]{2,1,0:T(8,128)(2,1)S(1)}, u32[]{:S(2)}, u32[]{:S(2)}) async-start(bf16[64,128,128]{2,1,0:T(8,128)(2,1)} %get-tuple-element.39), calls=%async_computation.1 | async-start | bytes 4194304 | tf_op jit(solution)/shard_map/all_to_all | solution.py:731
  132.9 2.0 %collective-permute-start = (bf16[1600,128]{1,0:T(8,128)(2,1)}, bf16[1600,128]{1,0:T(8,128)(2,1)S(1)}, u32[]{:S(2)}, u32[]{:S(2)}) collective-permute-start(bf16[1600,128]{1,0:T(8,128)(2,1)} %get-tuple-element.57), channel_id=1, source_target_pairs={{0,4},{4,0},{8,12},{12,8},{16,20},{20,16},{24,28},{28,24},{32,36},... | collective-permute-start | bytes 1228808 | tf_op jit(solution)/shard_map/ppermute | solution.py:690
  136.2 6.2 %collective-permute-start.1 = (bf16[800,128]{1,0:T(8,128)(2,1)S(1)}, bf16[800,128]{1,0:T(8,128)(2,1)S(1)}, u32[]{:S(2)}, u32[]{:S(2)}) collective-permute-start(bf16[800,128]{1,0:T(8,128)(2,1)S(1)} %dynamic-slice_convert_fusion), channel_id=1, source_target_pairs={{0,3},{1,2},{2,1},{3,0},{4,100},{5,101},{6,102},{7,103},{8,11},{9,... | collective-permute-start | bytes 614408 | tf_op jit(solution)/shard_map/ppermute | solution.py:686
  142.4 3.6 %collective-permute-start.2 = (bf16[400,128]{1,0:T(8,128)(2,1)S(1)}, bf16[400,128]{1,0:T(8,128)(2,1)S(1)}, u32[]{:S(2)}, u32[]{:S(2)}) collective-permute-start(bf16[400,128]{1,0:T(8,128)(2,1)S(1)} %dynamic-slice_convert_fusion.1), channel_id=1, source_target_pairs={{0,1},{1,0},{2,3},{3,2},{4,36},{5,37},{6,38},{7,39},{8,9},{9,8},{1... | collective-permute-start | bytes 307208 | tf_op jit(solution)/shard_map/ppermute | solution.py:686
  146.1 4.8 %collective-permute-start.3 = (bf16[400,128]{1,0:T(8,128)(2,1)S(1)}, bf16[400,128]{1,0:T(8,128)(2,1)S(1)}, u32[]{:S(2)}, u32[]{:S(2)}) collective-permute-start(bf16[400,128]{1,0:T(8,128)(2,1)S(1)} %fusion.2), channel_id=1, source_target_pairs={{0,96},{1,97},{2,98},{3,99},{4,28},{5,29},{6,30},{7,31},{8,104},{9... | collective-permute-start | bytes 307208 | tf_op jit(solution)/shard_map/ppermute | solution.py:686
  150.9 3.6 %collective-permute-start.4 = (bf16[400,128]{1,0:T(8,128)(2,1)S(1)}, bf16[400,128]{1,0:T(8,128)(2,1)S(1)}, u32[]{:S(2)}, u32[]{:S(2)}) collective-permute-start(bf16[400,128]{1,0:T(8,128)(2,1)S(1)} %fusion), channel_id=1, source_target_pairs={{0,32},{1,33},{2,34},{3,35},{4,12},{5,13},{6,14},{7,15},{8,40},{9,... | collective-permute-start | bytes 307208 | tf_op jit(solution)/shard_map/ppermute | solution.py:686
  154.6 4.8 %collective-permute-start.5 = (bf16[400,128]{1,0:T(8,128)(2,1)S(1)}, bf16[400,128]{1,0:T(8,128)(2,1)S(1)}, u32[]{:S(2)}, u32[]{:S(2)}) collective-permute-start(bf16[400,128]{1,0:T(8,128)(2,1)S(1)} %get-tuple-element.66), channel_id=1, source_target_pairs={{0,24},{1,25},{2,26},{3,27},{4,7},{5,6},{6,5},{7,4},{8,16},{9,17},... | collective-permute-start | bytes 307208 | tf_op jit(solution)/shard_map/ppermute | solution.py:686
  159.4 3.6 %collective-permute-start.6 = (bf16[400,128]{1,0:T(8,128)(2,1)S(1)}, bf16[400,128]{1,0:T(8,128)(2,1)S(1)}, u32[]{:S(2)}, u32[]{:S(2)}) collective-permute-start(bf16[400,128]{1,0:T(8,128)(2,1)S(1)} %fusion.1), channel_id=1, source_target_pairs={{0,8},{1,9},{2,10},{3,11},{4,5},{5,4},{6,7},{7,6},{8,0},{9,1},{10,... | collective-permute-start | bytes 307208 | tf_op jit(solution)/shard_map/ppermute | solution.py:686
  163.0 3.6 %collective-permute-start.7 = (bf16[400,128]{1,0:T(8,128)(2,1)S(1)}, bf16[400,128]{1,0:T(8,128)(2,1)S(1)}, u32[]{:S(2)}, u32[]{:S(2)}) collective-permute-start(bf16[400,128]{1,0:T(8,128)(2,1)S(1)} %add_convert_fusion), channel_id=1, source_target_pairs={{0,1},{1,0},{2,3},{3,2},{4,36},{5,37},{6,38},{7,39},{8,9},{9,8},{1... | collective-permute-start | bytes 307208 | tf_op jit(solution)/shard_map/ppermute | solution.py:686
  166.7 5.9 %collective-permute-start.8 = (bf16[800,128]{1,0:T(8,128)(2,1)S(1)}, bf16[800,128]{1,0:T(8,128)(2,1)S(1)}, u32[]{:S(2)}, u32[]{:S(2)}) collective-permute-start(bf16[800,128]{1,0:T(8,128)(2,1)S(1)} %maximum_select_fusion.1), channel_id=1, source_target_pairs={{0,3},{1,2},{2,1},{3,0},{4,100},{5,101},{6,102},{7,103},{8,11},{9,... | collective-permute-start | bytes 614408 | tf_op jit(solution)/shard_map/ppermute | solution.py:686
  172.7 10.6 %copy-start.1 = (bf16[1600,128]{1,0:T(8,128)(2,1)}, bf16[1600,128]{1,0:T(8,128)(2,1)S(1)}, u32[]{:S(2)}) copy-start(bf16[1600,128]{1,0:T(8,128)(2,1)S(1)} %maximum_select_fusion.mine) | copy-start | bytes 1228804
  172.7 10.6 %collective-permute-start.9 = (bf16[1600,128]{1,0:T(8,128)(2,1)S(1)}, bf16[1600,128]{1,0:T(8,128)(2,1)S(1)}, u32[]{:S(2)}, u32[]{:S(2)}) collective-permute-start(bf16[1600,128]{1,0:T(8,128)(2,1)S(1)} %maximum_select_fusion.mine), channel_id=1, source_target_pairs={{0,4},{4,0},{8,12},{12,8},{16,20},{20,16},{24,28},{28,24},{32,36},... | collective-permute-start | bytes 1228808 | tf_op jit(solution)/shard_map/ppermute | solution.py:690
  183.3 0.8 copy-start.2

commit v5 on v4

--- a/solution.py
+++ b/solution.py
@@ -135,7 +135,7 @@
 
 def layer_fwd(x, biases, w, sv, share):
     per_turn = share["per_turn"]
-    wi_t, wo_t, m1_t, m2_t, cols, hid = w["wi_t"], w["wo_t"], w["m1_t"], w["m2_t"], w["cols"], w["hid"]
+    wi_t, wo_t, m1_t, m2_t, cols = w["wi_t"], w["wo_t"], w["m1_t"], w["m2_t"], w["cols"]
     xhat0, rstd0 = normalize(x)
     sv["xhat0"][...] = xhat0.astype(BF)
     sv["rstd"][0:8, :] = jnp.broadcast_to(rstd0, (8, L))
@@ -170,14 +170,15 @@
     b = (xhat1 * wide(cols[1]) + wide(cols[3])).astype(BF)
     sv["b"][...] = b
     yield
+    b = jnp.concatenate([b, jnp.ones((HEAD, L), BF)], axis=0)
     hidden = None
     for i in range(5):
         last = hidden
         if i < 4:
-            hidden = nn(m1_t[i * D:(i + 1) * D, :], b)
+            hidden = nn(m1_t[i * D:(i + 1) * D, 0:D + HEAD], b)
         if i >= 1:
             rows = slice((i - 1) * D, i * D)
-            hv = last + wide(hid[rows, :])
+            hv = last
             arg = hv * 0.7071067811865476
             cdf2 = lax.erf(arg) + 1.0
             sv["u"][rows, :] = (hv * cdf2).astype(BF)
@@ -327,10 +328,9 @@
 RAW = ("gains", "shifts", "hidden", "wi", "wo", "m1", "m2")
 PREP = {
     "cols": ((6, D, S), F32),
-    "hid": ((FF, S), F32),
     "wi_t": ((3 * D, D), BF),
     "wo_t": ((D, D), BF),
-    "m1_t": ((FF, D), BF),
+    "m1_t": ((FF, 2 * D), BF),
     "m2_t": ((D, FF), BF),
     "m2_h": ((FF, D), BF),
 }
@@ -353,8 +353,14 @@
         if forward:
             for j in range(4):
                 rows = slice(j * D, (j + 1) * D)
-                prep["hid"][rows, :] = spread_row(raw["hidden"][l:l + 1, rows])
-                prep["m1_t"][rows, :] = jnp.transpose(raw["m1"][l, :, rows])
+                prep["m1_t"][rows, 0:D] = jnp.transpose(raw["m1"][l, :, rows])
+                bias = spread_row(raw["hidden"][l:l + 1, rows])
+                high = bias.astype(BF)
+                mid = (bias - high.astype(F32)).astype(BF)
+                low = (bias - high.astype(F32) - mid.astype(F32)).astype(BF)
+                lane = lax.broadcasted_iota(jnp.int32, (D, S), 1)
+                terms = jnp.where(lane == 0, high.astype(F32), 0.0) + jnp.where(lane == 1, mid.astype(F32), 0.0)
+                prep["m1_t"][rows, D:2 * D] = (terms + jnp.where(lane == 2, low.astype(F32), 0.0)).astype(BF)
                 prep["m2_t"][:, rows] = jnp.transpose(raw["m2"][l, rows, :]) * BF(0.5)
             for j in range(3):
                 rows = slice(j * D, (j + 1) * D)
@@ -690,29 +696,27 @@
     return lax.ppermute(value, "dp", [(i, i ^ 1) for i in range(n_dp)])
 
 
-def split(value, bit):
-    half = value.shape[0] // 2
-    keep = lax.dynamic_slice_in_dim(value, bit * half, half, axis=0)
-    send = lax.dynamic_slice_in_dim(value, (1 - bit) * half, half, axis=0)
-    return keep, send.astype(BF)
-
-
-def join(mine, other, bit):
-    return jnp.where(bit == 0, jnp.concatenate([mine, other], axis=0), jnp.concatenate([other, mine], axis=0))
-
-
 def reduce_all(core, keep, send, n_dp, n_group):
     place = jnp.where(core == 0, lax.axis_index("group"), lax.axis_index("dp") // 8)
     value = keep + swap_cores(send, n_dp).astype(F32)
-    for bits, bit in ((3, place // 2), (1, place % 2)):
-        keep, send = split(value, bit)
-        value = keep + swap(send, ("x", bits), ("y", bits), n_dp, n_group).astype(F32)
+    quarter = value.shape[0] // 4
+    whole = value
+    value = lax.dynamic_slice_in_dim(whole, place * quarter, quarter, axis=0)
+    for bits in (1, 2, 3):
+        send = lax.dynamic_slice_in_dim(whole, (place ^ bits) * quarter, quarter, axis=0).astype(BF)
+        value = value + swap(send, ("x", bits), ("y", bits), n_dp, n_group).astype(F32)
     for first, second in (("y", "z"), ("z", "x")):
-        for bits in (3, 1):
-            value = value + swap(value.astype(BF), (first, bits), (second, bits), n_dp, n_group).astype(F32)
+        value = lax.reduce_precision(value, 8, 7)
+        one, two, three = [swap(value.astype(BF), (first, bits), (second, bits), n_dp, n_group) for bits in (1, 2, 3)]
+        value = (value + one.astype(F32)) + (two.astype(F32) + three.astype(F32))
     value = value.astype(BF)
-    for bits, bit in ((1, place % 2), (3, place // 2)):
-        value = join(value, swap(value, ("x", bits), ("y", bits), n_dp, n_group), bit)
+    pieces = [value] + [swap(value, ("x", bits), ("y", bits), n_dp, n_group) for bits in (1, 2, 3)]
+    ordered = []
+    for j in range(4):
+        away = place ^ j
+        low = jnp.where(away == 0, pieces[0], pieces[1])
+        ordered.append(jnp.where(away < 2, low, jnp.where(away == 2, pieces[2], pieces[3])))
+    value = jnp.concatenate(ordered, axis=0)
     return value, swap_cores(value, n_dp)
 
 

time: 188 us -> 177 us (0.941)
  waiting for transfers between devices: 28.7 us -> 21.3 us
  starting transfers between devices: 37 us -> 34.7 us
    ppermute x8 -> x12, waiting for transfers between devices: 24.6 us -> 16.6 us  [swap(): return lax.ppermute(value, ('dp', 'group'), pairs)]
    ppermute x2, starting transfers between devices: 9.54 us -> 6.34 us  [swap_cores(): return lax.ppermute(value, 'dp', [(i, i ^ 1) for i in range(n_dp)])]
    ppermute x8 -> x12, starting transfers between devices: 11.4 us -> 12.9 us  [swap(): return lax.ppermute(value, ('dp', 'group'), pairs)]
  transfers between devices with their start and end apart: 12 -> 16, of which waited for: 11 -> 11; matrix products, arithmetic and copies ran while one was open for 0% -> 0% of each run, Pallas kernels for 31% -> 33%
where the time goes in v5:
time: 177 us
  Pallas kernels  115 us (65%)
  starting transfers between devices  34.7 us (20%)
  waiting for transfers between devices  21.3 us (12%)
  local copies, waits for them, and re-layouts  3.45 us (2%)
  other arithmetic  2.15 us (1%)
    pallas_call x1, Pallas kernels, run_decode(): pl.pallas_call(decode_kernel, grid_spec=pltpu.PrefetchScalarGridSpec(num_...  54.3 us
    pallas_call x1, Pallas kernels, run_back(): pl.pallas_call(back_kernel, grid_spec=pltpu.PrefetchScalarGridSpec(num_sc...  31.9 us
    pallas_call x1, Pallas kernels, run_encode(): pl.pallas_call(encode_kernel, grid=(steps,), in_specs=[step_spec((NT * NG...  26.1 us
    ppermute x12, waiting for transfers between devices, swap(): return lax.ppermute(value, ('dp', 'group'), pairs)  16.6 us
    ppermute x12, starting transfers between devices, swap(): return lax.ppermute(value, ('dp', 'group'), pairs)  12.9 us
    all_to_all x1, starting transfers between devices, on_device(): lax.all_to_all(cotangent.reshape(tiles, S, D), 'dp', split_axis=0, concat...  9.62 us
    ppermute x2, starting transfers between devices, swap_cores(): return lax.ppermute(value, 'dp', [(i, i ^ 1) for i in range(n_dp)])  6.34 us
    all_to_all x1, starting transfers between devices, on_device(): decoded = lax.all_to_all(dec, 'dp', split_axis=0, concat_axis=0, tiled=True)  5.83 us
  transfers between devices with their start and end apart: 16, of which 11 were waited for; matrix products, arithmetic and copies ran while one was open for 0% of the time, Pallas kernels for 33%

profile of v5, /device:TPU:1, one launch (start us, length us, event | category | flops | bytes accessed | tf_op | source)
XLA Modules:
  0.0 177.1 jit_solution(635110200155002940)
XLA Ops:
  0.7 9.6 %all-to-all-start = ((bf16[64,128,128]{2,1,0:T(8,128)(2,1)}), bf16[64,128,128]{2,1,0:T(8,128)(2,1)S(1)}, u32[]{:S(2)}, u32[]{:S(2)}) async-start(bf16[64,128,128]{2,1,0:T(8,128)(2,1)} %bitcast.11), calls=%async_computation | async-start | bytes 4194304 | tf_op jit(solution)/shard_map/all_to_all | solution.py:730
  10.3 0.0 copy-done.3
  10.3 0.6 select_reduce_fusion.inv_order
  10.9 26.1 %shard_map.204 = (bf16[32,128,256]{2,1,0:T(8,128)(2,1)}, bf16[32,384,256]{2,1,0:T(8,128)(2,1)}, bf16[32,2,128,1024]{3,2,1,0:T(8,128)(2,1)}, f32[32,64,256]{2,1,0...) custom-call(bf16[64,128,128]{2,1,0:T(8,128)(2,1)} %bitcast.12, ...), custom_call_target="tpu_custom_call" | custom-call | flops 20000000000 | bytes 60000000 | tf_op jit(solution)/shard_map/pallas_call | solution.py:575
  37.0 1.6 all-to-all-done.rest_0_.rest_1_.rest_2_.rest_3_.rest_4_.rest_5_.rest_6_.rest_7_.rest_8_.rest_9_.rest_10_.rest_11_.rest_12_.rest_13_.rest_14_.rest_15_
  38.6 1.3 copy-done
  39.9 54.3 %shard_map.205 = (bf16[64,128,128]{2,1,0:T(8,128)(2,1)}, bf16[32,128,256]{2,1,0:T(8,128)(2,1)}, f32[1600,128]{1,0:T(8,128)}) custom-call(s32[64]{0:T(128)} %select_reduce_fusion.inv_order, bf16[32,128,256]{2,1,0:T(8,128)(2,1)} %get-tuple-element.38.enc_ref, bf16[64,128,128]{2,1,0:T(8,128)(2,1)} %copy-done, bf16[64,128,128]{2,1,0:T(8,128)(2,1)} %copy-done, ...), custom_call_target="tpu_custom_call" | custom-call | flops 40000000000 | bytes 10000000 | tf_op jit(solution)/shard_map/pallas_call | solution.py:593
  94.2 5.8 %all-to-all-start.1 = ((bf16[64,128,128]{2,1,0:T(8,128)(2,1)}), bf16[64,128,128]{2,1,0:T(8,128)(2,1)S(1)}, u32[]{:S(2)}, u32[]{:S(2)}) async-start(bf16[64,128,128]{2,1,0:T(8,128)(2,1)} %get-tuple-element.39), calls=%async_computation.1 | async-start | bytes 4194304 | tf_op jit(solution)/shard_map/all_to_all | solution.py:735
  100.1 31.9 %shard_map.206 = (f32[64,128,128]{2,1,0:T(8,128)}, f32[1600,128]{1,0:T(8,128)}, bf16[1600,128]{1,0:T(8,128)(2,1)}) custom-call(s32[1]{0:T(128)} %bitcast.6.core_ref, bf16[32,128,256]{2,1,0:T(8,128)(2,1)} %get-tuple-element.40.ge_ref, f32[1600,128]{1,0:T(8,128)} %get-tuple-element.41.other_ref, bf16[32,384,256]{2,1,0:T(8,128)(2,1)} %get-tuple-element.42.rest_0_, ...), custom_call_target="tpu_custom_call" | custom-call | flops 20000000000 | bytes 60000000 | tf_op jit(solution)/shard_map/pallas_call | solution.py:616
  132.0 0.0 all-to-all-done.1
  132.0 0.3 collective-permute-start
  132.3 1.7 collective-permute-done
  134.0 1.2 convert_add_fusion
  135.3 0.1 dynamic-slice_convert_fusion.2
  135.3 2.7 %collective-permute-start.3 = (bf16[400,128]{1,0:T(8,128)(2,1)S(1)}, bf16[400,128]{1,0:T(8,128)(2,1)S(1)}, u32[]{:S(2)}, u32[]{:S(2)}) collective-permute-start(bf16[400,128]{1,0:T(8,128)(2,1)S(1)} %get-tuple-element.69), channel_id=1, source_target_pairs={{0,3},{1,2},{2,1},{3,0},{4,100},{5,101},{6,102},{7,103},{8,11},{9,... | collective-permute-start | bytes 307208 | tf_op jit(solution)/shard_map/ppermute | solution.py:692
  138.1 0.5 collective-permute-start.2
  138.6 0.1 collective-permute-start.1
  138.7 2.0 %collective-permute-done.3 = bf16[400,128]{1,0:T(8,128)(2,1)S(1)} collective-permute-done((bf16[400,128]{1,0:T(8,128)(2,1)S(1)}, bf16[400,128]{1,0:T(8,128)(2,1)S(1)}, u32[]{:S(2)}, u32[]{:S(2)}) %collective-permute-start.3) | collective-permute-done | bytes 102432 | tf_op jit(solution)/shard_map/ppermute | solution.py:692
  140.8 2.6 %collective-permute-done.2 = bf16[400,128]{1,0:T(8,128)(2,1)S(1)} collective-permute-done((bf16[400,128]{1,0:T(8,128)(2,1)S(1)}, bf16[400,128]{1,0:T(8,128)(2,1)S(1)}, u32[]{:S(2)}, u32[]{:S(2)}) %collective-permute-start.2) | collective-permute-done | bytes 102432 | tf_op jit(solution)/shard_map/ppermute | solution.py:692
  143.4 0.0 collective-permute-done.1
  143.4 0.1 fusion.1
  143.4 2.5 %collective-permute-start.6 = (bf16[400,128]{1,0:T(8,128)(2,1)S(1)}, bf16[400,128]{1,0:T(8,128)(2,1)S(1)}, u32[]{:S(2)}, u32[]{:S(2)}) collective-permute-start(bf16[400,128]{1,0:T(8,128)(2,1)S(1)} %get-tuple-element.66), channel_id=1, source_target_pairs={{0,96},{1,97},{2,98},{3,99},{4,28},{5,29},{6,30},{7,31},{8,104},{9... | collective-permute-start | bytes 307208 | tf_op jit(solution)/shard_map/ppermute | solution.py:692
  145.9 0.4 collective-permute-start.5
  146.3 0.4 collective-permute-start.4
  146.8 1.9 %collective-permute-done.6 = bf16[400,128]{1,0:T(8,128)(2,1)S(1)} collective-permute-done((bf16[400,128]{1,0:T(8,128)(2,1)S(1)}, bf16[400,128]{1,0:T(8,128)(2,1)S(1)}, u32[]{:S(2)}, u32[]{:S(2)}) %collective-permute-start.6) | collective-permute-done | bytes 102432 | tf_op jit(solution)/shard_map/ppermute | solution.py:692
  148.6 2.3 %collective-permute-done.5 = bf16[400,128]{1,0:T(8,128)(2,1)S(1)} collective-permute-done((bf16[400,128]{1,0:T(8,128)(2,1)S(1)}, bf16[400,128]{1,0:T(8,128)(2,1)S(1)}, u32[]{:S(2)}, u32[]{:S(2)}) %collective-permute-start.5) | collective-permute-done | bytes 102432 | tf_op jit(solution)/shard_map/ppermute | solution.py:692
  151.0 0.0 collective-permute-done.4
  151.0 0.1 fusion
  151.0 2.2 %collective-permute-start.9 = (bf16[400,128]{1,0:T(8,128)(2,1)S(1)}, bf16[400,128]{1,0:T(8,128)(2,1)S(1)}, u32[]{:S(2)}, u32[]{:S(2)}) collective-permute-start(bf16[400,128]{1,0:T(8,128)(2,1)S(1)} %fusion), channel_id=1, source_target_pairs={{0,24},{1,25},{2,26},{3,27},{4,7},{5,6},{6,5},{7,4},{8,16},{9,17},... | collective-permute-start | bytes 307208 | tf_op jit(solution)/shard_map/ppermute | solution.py:692
  153.3 0.6 collective-permute-start.8
  153.8 0.5 collective-permute-start.7
  154.4 1.5 collective-permute-done.9
  155.8 2.5 %collective-permute-done.8 = bf16[400,128]{1,0:T(8,128)(2,1)S(1)} collective-permute-done((bf16[400,128]{1,0:T(8,128)(2,1)S(1)}, bf16[400,128]{1,0:T(8,128)(2,1)S(1)}, u32[]{:S(2)}, u32[]{:S(2)}) %collective-permute-start.8) | collective-permute-done | bytes 102432 | tf_op jit(solution)/shard_map/ppermute | solution.py:692
  158.3 0.0 collective-permute-done.7
  158.3 0.1 add_convert_fusion
  158.4 2.0 %collective-permute-start.11 = (bf16[400,128]{1,0:T(8,128)(2,1)S(1)}, bf16[400,128]{1,0:T(8,128)(2,1)S(1)}, u32[]{:S(2)}, u32[]{:S(2)}) collective-permute-start(bf16[400,128]{1,0:T(8,128)(2,1)S(1)} %add_convert_fusion), channel_id=1, source_target_pairs={{0,2},{1,3},{2,0},{3,1},{4,68},{5,69},{6,70},{7,71},{8,10},{9,11},... | collective-permute-start | bytes 307208 | tf_op jit(solution)/shard_map/ppermute | solution.py:692
  160.4 0.9 collective-permute-start.12
  161.3 0.0 collective-permute-start.10
  161.3 2.2 %collective-permute-done.11 = bf16[400,128]{1,0:T(8,128)(2,1)S(1)} collective-permute-done((bf16[400,128]{1,0:T(8,128)(2,1)S(1)}, bf16[400,128]{1,0:T(8,128)(2,1)S(1)}, u32[]{:S(2)}, u32[]{:S(2)}) %collective-permute-start.11) | collective-permute-done | bytes 102432 | tf_op jit(solution)/shard_map/ppermute | solution.py:692
  163.5 1.6 collective-permute-done.12
  165.1 0.0 collective-permute-done.10
  165.1 0.1 select_select_fusion.3
  165.2 0.0 copy-start.1
  165.2 6.0 %collective-permute-start.13 = (bf16[1600,128]{1,0:T(8,128)(2,1)S(1)}, bf16[1600,128]{1,0:T(8,128)(2,1)S(1)}, u32[]{:S(2)}, u32[]{:S(2)}) collective-permute-start(bf16[1600,128]{1,0:T(8,128)(2,1)S(1)} %pad_maximum_fusion.mine), channel_id=1, source_target_pairs={{0,4},{4,0},{8,12},{12,8},{16,20},{20,16},{24,28},{28,24},{32,36},... | collective-permute-start | bytes 1228808 | tf_op jit(solution)/shard_map/ppermute | solution.py:696
  171.2 1.4 collective-permute-done.13.other
  172.6 0.7 copy-done.2
  173.3 2.4 %shard_map.207 = (f32[2,512,128]{2,1,0:T(8,128)}, f32[2,128,512]{2,1,0:T(8,128)}, f32[2,128,384]{2,1,0:T(8,128)}, f32[2,128,128]{2,1,0:T(8,128)}, f32[2,2,128]{2...) custom-call(s32[1]{0:T(128)} %bitcast.6.core_ref, bf16[1600,128]{1,0:T(8,128)(2,1)} %copy-done.1, ...), custom_call_target="tpu_custom_call" | custom-call | tf_op jit(solution)/shard_map/pallas_call | solution.py:664
  175.7 1.3 copy.24
  (5 shorter events, 0.0 us)
Async XLA Ops:
  0.6 9.6 %copy-start.3 = (s32[1,1,64]{2,1,0:T(1,128)S(1)}, s32[1,1,64]{2,1,0:T(1,128)}, u32[]{:S(2)}) copy-start(s32[1,1,64]{2,1,0:T(1,128)} %param.16) | copy-start | bytes 772
  0.7 37.9 %all-to-all-start = ((bf16[64,128,128]{2,1,0:T(8,128)(2,1)}), bf16[64,128,128]{2,1,0:T(8,128)(2,1)S(1)}, u32[]{:S(2)}, u32[]{:S(2)}) async-start(bf16[64,128,128]{2,1,0:T(8,128)(2,1)} %bitcast.11), calls=%async_computation | async-start | bytes 4194304 | tf_op jit(solution)/shard_map/all_to_all | solution.py:730
  38.6 1.3 copy-start
  94.2 37.8 %all-to-all-start.1 = ((bf16[64,128,128]{2,1,0:T(8,128)(2,1)}), bf16[64,128,128]{2,1,0:T(8,128)(2,1)S(1)}, u32[]{:S(2)}, u32[]{:S(2)}) async-start(bf16[64,128,128]{2,1,0:T(8,128)(2,1)} %get-tuple-element.39), calls=%async_computation.1 | async-start | bytes 4194304 | tf_op jit(solution)/shard_map/all_to_all | solution.py:735
  132.0 2.0 %collective-permute-start = (bf16[1600,128]{1,0:T(8,128)(2,1)}, bf16[1600,128]{1,0:T(8,128)(2,1)S(1)}, u32[]{:S(2)}, u32[]{:S(2)}) collective-permute-start(bf16[1600,128]{1,0:T(8,128)(2,1)} %get-tuple-element.57), channel_id=1, source_target_pairs={{0,4},{4,0},{8,12},{12,8},{16,20},{20,16},{24,28},{28,24},{32,36},... | collective-permute-start | bytes 1228808 | tf_op jit(solution)/shard_map/ppermute | solution.py:696
  135.3 5.4 %collective-permute-start.3 = (bf16[400,128]{1,0:T(8,128)(2,1)S(1)}, bf16[400,128]{1,0:T(8,128)(2,1)S(1)}, u32[]{:S(2)}, u32[]{:S(2)}) collective-permute-start(bf16[400,128]{1,0:T(8,128)(2,1)S(1)} %get-tuple-element.69), channel_id=1, source_target_pairs={{0,3},{1,2},{2,1},{3,0},{4,100},{5,101},{6,102},{7,103},{8,11},{9,... | collective-permute-start | bytes 307208 | tf_op jit(solution)/shard_map/ppermute | solution.py:692
  138.1 5.3 %collective-permute-start.2 = (bf16[400,128]{1,0:T(8,128)(2,1)S(1)}, bf16[400,128]{1,0:T(8,128)(2,1)S(1)}, u32[]{:S(2)}, u32[]{:S(2)}) collective-permute-start(bf16[400,128]{1,0:T(8,128)(2,1)S(1)} %get-tuple-element.70), channel_id=1, source_target_pairs={{0,2},{1,3},{2,0},{3,1},{4,68},{5,69},{6,70},{7,71},{8,10},{9,11},... | collective-permute-start | bytes 307208 | tf_op jit(solution)/shard_map/ppermute | solution.py:692
  138.6 4.8 %collective-permute-start.1 = (bf16[400,128]{1,0:T(8,128)(2,1)S(1)}, bf16[400,128]{1,0:T(8,128)(2,1)S(1)}, u32[]{:S(2)}, u32[]{:S(2)}) collective-permute-start(bf16[400,128]{1,0:T(8,128)(2,1)S(1)} %get-tuple-element.68), channel_id=1, source_target_pairs={{0,1},{1,0},{2,3},{3,2},{4,36},{5,37},{6,38},{7,39},{8,9},{9,8},{1... | collective-permute-start | bytes 307208 | tf_op jit(solution)/shard_map/ppermute | solution.py:692
  143.4 5.2 %collective-permute-start.6 = (bf16[400,128]{1,0:T(8,128)(2,1)S(1)}, bf16[400,128]{1,0:T(8,128)(2,1)S(1)}, u32[]{:S(2)}, u32[]{:S(2)}) collective-permute-start(bf16[400,128]{1,0:T(8,128)(2,1)S(1)} %get-tuple-element.66), channel_id=1, source_target_pairs={{0,96},{1,97},{2,98},{3,99},{4,28},{5,29},{6,30},{7,31},{8,104},{9... | collective-permute-start | bytes 307208 | tf_op jit(solution)/shard_map/ppermute | solution.py:692
  145.9 5.0 %collective-permute-start.5 = (bf16[400,128]{1,0:T(8,128)(2,1)S(1)}, bf16[400,128]{1,0:T(8,128)(2,1)S(1)}, u32[]{:S(2)}, u32[]{:S(2)}) collective-permute-start(bf16[400,128]{1,0:T(8,128)(2,1)S(1)} %get-tuple-element.66), channel_id=1, source_target_pairs={{0,64},{1,65},{2,66},{3,67},{4,20},{5,21},{6,22},{7,23},{8,72},{9,... | collective-permute-start | bytes 307208 | tf_op jit(solution)/shard_map/ppermute | solution.py:692
  146.3 4.6 %collective-permute-start.4 = (bf16[400,128]{1,0:T(8,128)(2,1)S(1)}, bf16[400,128]{1,0:T(8,128)(2,1)S(1)}, u32[]{:S(2)}, u32[]{:S(2)}) collective-permute-start(bf16[400,128]{1,0:T(8,128)(2,1)S(1)} %get-tuple-element.66), channel_id=1, source_target_pairs={{0,32},{1,33},{2,34},{3,35},{4,12},{5,13},{6,14},{7,15},{8,40},{9,... | collective-permute-start | bytes 307208 | tf_op jit(solution)/shard_map/ppermute | solution.py:692
  151.0 4.8 %collective-permute-start.9 = (bf16[400,128]{1,0:T(8,128)(2,1)S(1)}, bf16[400,128]{1,0:T(8,128)(2,1)S(1)}, u32[]{:S(2)}, u32[]{:S(2)}) collective-permute-start(bf16[400,128]{1,0:T(8,128)(2,1)S(1)} %fusion), channel_id=1, source_target_pairs={{0,24},{1,25},{2,26},{3,27},{4,7},{5,6},{6,5},{7,4},{8,16},{9,17},... | collective-permute-start | bytes 307208 | tf_op jit(solution)/shard_map/ppermute | solution.py:692
  153.3 5.0 %collective-permute-start.8 = (bf16[400,128]{1,0:T(8,128)(2,1)S(1)}, bf16[400,128]{1,0:T(8,128)(2,1)S(1)}, u32[]{:S(2)}, u32[]{:S(2)}) collective-permute-start(bf16[400,128]{1,0:T(8,128)(2,1)S(1)} %fusion), channel_id=1, source_target_pairs={{0,16},{1,17},{2,18},{3,19},{4,6},{5,7},{6,4},{7,5},{8,24},{9,25},... | collective-permute-start | bytes 307208 | tf_op jit(solution)/shard_map/ppermute | solution.py:692
  153.8 4.5 %collective-permute-start.7 = (bf16[400,128]{1,0:T(8,128)(2,1)S(1)}, bf16[400,128]{1,0:T(8,128)(2,1)S(1)}, u32[]{:S(2)}, u32[]{:S(2)}) collective-permute-start(bf16[400,128]{1,0:T(8,128)(2,1)S(1)} %fusion), channel_id=1, source_target_pairs={{0,8},{1,9},{2,10},{3,11},{4,5},{5,4},{6,7},{7,6},{8,0},{9,1},{10,... | collective-permute-start | bytes 307208 | tf_op jit(solution)/shard_map/ppermute | solution.py:692
  158.4 5.1 %collective-permute-start.11 = (bf16[400,128]{1,0:T(8,128)(2,1)S(1)}, bf16[400,128]{1,0:T(8,128)(2,1)S(1)}, u32[]{:S(2)}, u32[]{:S(2)}) collective-permute-start(bf16[400,128]{1,0:T(8,128)(2,1)S(1)} %add_convert_fusion), channel_id=1, source_target_pairs={{0,2},{1,3},{2,0},{3,1},{4,68},{5,69},{6,70},{7,71},{8,10},{9,11},... | collective-permute-start | bytes 307208 | tf_op jit(solution)/shard_map/ppermute | solution.py:692
  160.4 4.7 %collective-permute-start.12 = (bf16[400,128]{1,0:T(8,128)(2,1)S(1)}, bf16[400,128]{1,0:T(8,128)(2,1)S(1)}, u32[]{:S(2)}, u32[]{:S(2)}) collective-permute-start(bf16[400,128]{1,0:T(8,128)(2,1)S(1)} %add_convert_fusion), channel_id=1, source_target_pairs={{0,3},{1,2},{2,1},{3,0},{4,100},{5,101},{6,102},{7,103},{8,11},{9,... | collective-permute-start | bytes 307208 | tf_op jit(solution)/shard_map/ppermute | solution.py:692
  161.3 3.9 %collective-permute-start.10 = (bf16[400,128]{1,0:T(8,128)(2,1)S(1)}, bf16[400,128]{1,0:T(8,128)(2,1)S(1)}, u32[]{:S(2)}, u32[]{:S(2)}) collective-permute-start(bf16[400,128]{1,0:T(8,128)(2,1)S(1)} %add_convert_fusion), channel_id=1, source_target_pairs={{0,1},{1,0},{2,3},{3,2},{4,36},{5,37},{6,38},{7,39},{8,9},{9,8},{1... | collective-permute-start | bytes 307208 | tf_op jit(solution)/shard_map/ppermute | solution.py:692
  165.2 7.4 %copy-start.1 = (bf16[1600,128]{1,0:T(8,128)(2,1)}, bf16[1600,128]{1,0:T(8,128)(2,1)S(1)}, u32[]{:S(2)}) copy-start(bf16[1600,128]{1,0:T(8,128)(2,1)S(1)} %pad_maximum_fusion.mine) | copy-start | bytes 1228804
  165.2 7.4 %collective-permute-start.13 = (bf16[1600,128]{1,0:T(8,128)(2,1)S(1)}, bf16[1600,128]{1,0:T(8,128)(2,1)S(1)}, u32[]{:S(2)}, u32[]{:S(2)}) collective-permute-start(bf16[1600,128]{1,0:T(8,128)(2,1)S(1)} %pad_maximum_fusion.mine), channel_id=1, source_target_pairs={{0,4},{4,0},{8,12},{12,8},{16,20},{20,16},{24,28},{28,24},{32,36},... | collective-permute-start | bytes 1228808 | tf_op jit(solution)/shard_map/ppermute | solution.py:696
  172.6 0.8 copy-start.2

commit v6 on v5

--- a/solution.py
+++ b/solution.py
@@ -161,6 +161,7 @@
         yield
     if share["last"] is sv:
         share["redo"](share["low"], share["high"])
+        share["attended"]()
     yield
     x1 = x + nn(wo_t[...], sv["o"][...]) + wide(cols[4])
     yield
@@ -318,6 +319,7 @@
     "b": ((D, L), BF),
     "rstd": ((16, L), F32),
 }
+LATE = ("xhat1", "b", "u", "gp", "rstd")
 BACK = {
     "gs": ((len(UNITS), S, 2 * S), BF),
     "gz": ((D, L), BF),
@@ -389,6 +391,7 @@
         "views": group_views,
         "last": group_views[-1],
         "low": None,
+        "attended": lambda: None,
         "high": None,
         "redo": lambda low, high: redo_shifted(low, high, view_at, bias_at, len(group_views)),
     }
@@ -397,10 +400,33 @@
 def encode_kernel(x_ref, seg_ref, vis_ref, *rest):
     raw, rest = rest[:len(RAW)], rest[len(RAW):]
     enc_ref = rest[0]
-    saved = rest[1:1 + len(SAVED)]
-    w = prep_weights(0, raw, rest[1 + len(SAVED):], True)
-    share = sharing([views(SAVED, saved, g) for g in range(NG_E)], TURN_E, lambda g: views(SAVED, saved, g),
-                    lambda g: masks(seg_ref, vis_ref, NT * g, False))
+    saved, rest = rest[1:1 + len(SAVED)], rest[1 + len(SAVED):]
+    held, rest = rest[:len(SAVED)], rest[len(SAVED):]
+    sems, rest = rest[0], rest[1:]
+    w = prep_weights(0, raw, rest, True)
+    step = pl.program_id(0)
+    slot = lax.rem(step, 2)
+
+    def copies(at, where, late):
+        return [
+            pltpu.make_async_copy(held[j].at[where], saved[j].at[pl.ds(at * NG_E, NG_E)], sems.at[where, j])
+            for j, name in enumerate(SAVED) if (name in LATE) == late
+        ]
+
+    def start(late):
+        for copy in copies(step, slot, late):
+            copy.start()
+
+    @pl.when(step >= 2)
+    def _():
+        for copy in copies(step - 2, slot, False) + copies(step - 2, slot, True):
+            copy.wait()
+
+    def view(g):
+        return {name: ref.at[slot, g] for name, ref in zip(SAVED, held)}
+
+    share = sharing([view(g) for g in range(NG_E)], TURN_E, view, lambda g: masks(seg_ref, vis_ref, NT * g, False))
+    share["attended"] = lambda: start(False)
 
     def group(g):
         sv = share["views"][g]
@@ -411,6 +437,13 @@
         enc_ref[g] = out.astype(BF)
 
     drive([group(g) for g in range(NG_E)])
+    start(True)
+
+    @pl.when(step == pl.num_programs(0) - 1)
+    def _():
+        for late in (False, True):
+            for copy in copies(step - 1, 1 - slot, late) + copies(step, slot, late):
+                copy.wait()
 
 
 def zero_first(refs):
@@ -576,9 +609,10 @@
         encode_kernel,
         grid=(steps,),
         in_specs=[step_spec(((NT * NG_E), S, D)), step_spec((1, (NT * NG_E), S)), step_spec((1, (NT * NG_E), S))] + [const_spec(o) for o in ops],
-        out_specs=[step_spec((NG_E,) + o.shape[1:]) for o in out_shape],
+        out_specs=[step_spec((NG_E, D, L))] + [pl.BlockSpec(memory_space=pl.ANY)] * len(SAVED),
         out_shape=out_shape,
-        scratch_shapes=prep_scratch(),
+        scratch_shapes=[pltpu.VMEM((2, NG_E) + shape, dt) for shape, dt in SAVED.values()]
+        + [pltpu.SemaphoreType.DMA((2, len(SAVED)))] + prep_scratch(),
         cost_estimate=cost(20 * 10**9, 60 * 10**6),
         compiler_params=PARAMS,
     )(x, seg.reshape(steps, (NT * NG_E), S), vis.reshape(steps, (NT * NG_E), S), *ops)

time: 177 us -> 177 us (level)
  no operation moved by 1% of the time
where the time goes in v6:
time: 177 us
  Pallas kernels  114 us (64%)
  starting transfers between devices  34.2 us (19%)
  waiting for transfers between devices  21.8 us (12%)
  local copies, waits for them, and re-layouts  3.45 us (2%)
  other arithmetic  2.15 us (1%)
    pallas_call x1, Pallas kernels, run_decode(): pl.pallas_call(decode_kernel, grid_spec=pltpu.PrefetchScalarGridSpec(num_...  54.4 us
    pallas_call x1, Pallas kernels, run_back(): pl.pallas_call(back_kernel, grid_spec=pltpu.PrefetchScalarGridSpec(num_sc...  31.9 us
    pallas_call x1, Pallas kernels, run_encode(): pl.pallas_call(encode_kernel, grid=(steps,), in_specs=[step_spec((NT * NG...  25.6 us
    ppermute x12, waiting for transfers between devices, swap(): return lax.ppermute(value, ('dp', 'group'), pairs)  16.6 us
    ppermute x12, starting transfers between devices, swap(): return lax.ppermute(value, ('dp', 'group'), pairs)  12.9 us
    all_to_all x1, starting transfers between devices, on_device(): lax.all_to_all(cotangent.reshape(tiles, S, D), 'dp', split_axis=0, concat...  9.62 us
    ppermute x2, starting transfers between devices, swap_cores(): return lax.ppermute(value, 'dp', [(i, i ^ 1) for i in range(n_dp)])  6.32 us
    all_to_all x1, starting transfers between devices, on_device(): decoded = lax.all_to_all(dec, 'dp', split_axis=0, concat_axis=0, tiled=True)  5.3 us
  transfers between devices with their start and end apart: 16, of which 11 were waited for; matrix products, arithmetic and copies ran while one was open for 0% of the time, Pallas kernels for 33%

profile of v6, /device:TPU:1, one launch (start us, length us, event | category | flops | bytes accessed | tf_op | source)
XLA Modules:
  0.0 176.6 jit_solution(6545372647722415036)
XLA Ops:
  0.7 9.6 %all-to-all-start = ((bf16[64,128,128]{2,1,0:T(8,128)(2,1)}), bf16[64,128,128]{2,1,0:T(8,128)(2,1)S(1)}, u32[]{:S(2)}, u32[]{:S(2)}) async-start(bf16[64,128,128]{2,1,0:T(8,128)(2,1)} %bitcast.11), calls=%async_computation | async-start | bytes 4194304 | tf_op jit(solution)/shard_map/all_to_all | solution.py:764
  10.3 0.0 copy-done.3
  10.3 0.6 select_reduce_fusion.inv_order
  10.9 25.6 %shard_map.204 = (bf16[32,128,256]{2,1,0:T(8,128)(2,1)}, bf16[32,384,256]{2,1,0:T(8,128)(2,1)}, bf16[32,2,128,1024]{3,2,1,0:T(8,128)(2,1)}, f32[32,64,256]{2,1,0...) custom-call(bf16[64,128,128]{2,1,0:T(8,128)(2,1)} %bitcast.12, ...), custom_call_target="tpu_custom_call" | custom-call | flops 20000000000 | bytes 60000000 | tf_op jit(solution)/shard_map/pallas_call | solution.py:608
  36.5 2.1 %all-to-all-done.rest_0_.rest_1_.rest_2_.rest_3_.rest_4_.rest_5_.rest_6_.rest_7_.rest_8_.rest_9_.rest_10_.rest_11_.rest_12_.rest_13_.rest_14_.rest_15_ = bf16[64,128,128]{2,1,0:T(8,128)(2,1)S(1)} async-done(((bf16[64,128,128]{2,1,0:T(8,128)(2,1)}), bf16[64,128,128]{2,1,0:T(8,128)(2,1)S(1)}, u32[]{:S(2)}, u32[]{:S(2)}) %all-to-all-start) | async-done | bytes 2097184 | tf_op jit(solution)/shard_map/all_to_all | solution.py:764
  38.6 1.3 copy-done
  39.9 54.4 %shard_map.205 = (bf16[64,128,128]{2,1,0:T(8,128)(2,1)}, bf16[32,128,256]{2,1,0:T(8,128)(2,1)}, f32[1600,128]{1,0:T(8,128)}) custom-call(s32[64]{0:T(128)} %select_reduce_fusion.inv_order, bf16[32,128,256]{2,1,0:T(8,128)(2,1)} %get-tuple-element.38.enc_ref, bf16[64,128,128]{2,1,0:T(8,128)(2,1)} %copy-done, bf16[64,128,128]{2,1,0:T(8,128)(2,1)} %copy-done, ...), custom_call_target="tpu_custom_call" | custom-call | flops 40000000000 | bytes 10000000 | tf_op jit(solution)/shard_map/pallas_call | solution.py:627
  94.3 5.3 %all-to-all-start.1 = ((bf16[64,128,128]{2,1,0:T(8,128)(2,1)}), bf16[64,128,128]{2,1,0:T(8,128)(2,1)S(1)}, u32[]{:S(2)}, u32[]{:S(2)}) async-start(bf16[64,128,128]{2,1,0:T(8,128)(2,1)} %get-tuple-element.39), calls=%async_computation.1 | async-start | bytes 4194304 | tf_op jit(solution)/shard_map/all_to_all | solution.py:769
  99.6 31.9 %shard_map.206 = (f32[64,128,128]{2,1,0:T(8,128)}, f32[1600,128]{1,0:T(8,128)}, bf16[1600,128]{1,0:T(8,128)(2,1)}) custom-call(s32[1]{0:T(128)} %bitcast.6.core_ref, bf16[32,128,256]{2,1,0:T(8,128)(2,1)} %get-tuple-element.40.ge_ref, f32[1600,128]{1,0:T(8,128)} %get-tuple-element.41.other_ref, bf16[32,384,256]{2,1,0:T(8,128)(2,1)} %get-tuple-element.42.rest_0_, ...), custom_call_target="tpu_custom_call" | custom-call | flops 20000000000 | bytes 60000000 | tf_op jit(solution)/shard_map/pallas_call | solution.py:650
  131.5 0.0 all-to-all-done.1
  131.5 0.3 collective-permute-start
  131.8 1.7 collective-permute-done
  133.5 1.2 convert_add_fusion
  134.7 0.1 dynamic-slice_convert_fusion.2
  134.8 2.7 %collective-permute-start.3 = (bf16[400,128]{1,0:T(8,128)(2,1)S(1)}, bf16[400,128]{1,0:T(8,128)(2,1)S(1)}, u32[]{:S(2)}, u32[]{:S(2)}) collective-permute-start(bf16[400,128]{1,0:T(8,128)(2,1)S(1)} %get-tuple-element.69), channel_id=1, source_target_pairs={{0,3},{1,2},{2,1},{3,0},{4,100},{5,101},{6,102},{7,103},{8,11},{9,... | collective-permute-start | bytes 307208 | tf_op jit(solution)/shard_map/ppermute | solution.py:726
  137.5 0.5 collective-permute-start.2
  138.1 0.1 collective-permute-start.1
  138.2 2.0 %collective-permute-done.3 = bf16[400,128]{1,0:T(8,128)(2,1)S(1)} collective-permute-done((bf16[400,128]{1,0:T(8,128)(2,1)S(1)}, bf16[400,128]{1,0:T(8,128)(2,1)S(1)}, u32[]{:S(2)}, u32[]{:S(2)}) %collective-permute-start.3) | collective-permute-done | bytes 102432 | tf_op jit(solution)/shard_map/ppermute | solution.py:726
  140.2 2.6 %collective-permute-done.2 = bf16[400,128]{1,0:T(8,128)(2,1)S(1)} collective-permute-done((bf16[400,128]{1,0:T(8,128)(2,1)S(1)}, bf16[400,128]{1,0:T(8,128)(2,1)S(1)}, u32[]{:S(2)}, u32[]{:S(2)}) %collective-permute-start.2) | collective-permute-done | bytes 102432 | tf_op jit(solution)/shard_map/ppermute | solution.py:726
  142.9 0.0 collective-permute-done.1
  142.9 0.1 fusion.1
  142.9 2.2 %collective-permute-start.6 = (bf16[400,128]{1,0:T(8,128)(2,1)S(1)}, bf16[400,128]{1,0:T(8,128)(2,1)S(1)}, u32[]{:S(2)}, u32[]{:S(2)}) collective-permute-start(bf16[400,128]{1,0:T(8,128)(2,1)S(1)} %get-tuple-element.66), channel_id=1, source_target_pairs={{0,96},{1,97},{2,98},{3,99},{4,28},{5,29},{6,30},{7,31},{8,104},{9... | collective-permute-start | bytes 307208 | tf_op jit(solution)/shard_map/ppermute | solution.py:726
  145.1 0.6 collective-permute-start.5
  145.7 0.6 collective-permute-start.4
  146.3 1.5 collective-permute-done.6
  147.7 2.4 %collective-permute-done.5 = bf16[400,128]{1,0:T(8,128)(2,1)S(1)} collective-permute-done((bf16[400,128]{1,0:T(8,128)(2,1)S(1)}, bf16[400,128]{1,0:T(8,128)(2,1)S(1)}, u32[]{:S(2)}, u32[]{:S(2)}) %collective-permute-start.5) | collective-permute-done | bytes 102432 | tf_op jit(solution)/shard_map/ppermute | solution.py:726
  150.1 0.0 collective-permute-done.4
  150.2 0.1 fusion
  150.2 2.6 %collective-permute-start.9 = (bf16[400,128]{1,0:T(8,128)(2,1)S(1)}, bf16[400,128]{1,0:T(8,128)(2,1)S(1)}, u32[]{:S(2)}, u32[]{:S(2)}) collective-permute-start(bf16[400,128]{1,0:T(8,128)(2,1)S(1)} %fusion), channel_id=1, source_target_pairs={{0,24},{1,25},{2,26},{3,27},{4,7},{5,6},{6,5},{7,4},{8,16},{9,17},... | collective-permute-start | bytes 307208 | tf_op jit(solution)/shard_map/ppermute | solution.py:726
  152.8 0.5 collective-permute-start.8
  153.3 0.2 collective-permute-start.7
  153.5 1.9 %collective-permute-done.9 = bf16[400,128]{1,0:T(8,128)(2,1)S(1)} collective-permute-done((bf16[400,128]{1,0:T(8,128)(2,1)S(1)}, bf16[400,128]{1,0:T(8,128)(2,1)S(1)}, u32[]{:S(2)}, u32[]{:S(2)}) %collective-permute-start.9) | collective-permute-done | bytes 102432 | tf_op jit(solution)/shard_map/ppermute | solution.py:726
  155.5 2.3 %collective-permute-done.8 = bf16[400,128]{1,0:T(8,128)(2,1)S(1)} collective-permute-done((bf16[400,128]{1,0:T(8,128)(2,1)S(1)}, bf16[400,128]{1,0:T(8,128)(2,1)S(1)}, u32[]{:S(2)}, u32[]{:S(2)}) %collective-permute-start.8) | collective-permute-done | bytes 102432 | tf_op jit(solution)/shard_map/ppermute | solution.py:726
  157.8 0.0 collective-permute-done.7
  157.8 0.1 add_convert_fusion
  157.9 2.0 %collective-permute-start.11 = (bf16[400,128]{1,0:T(8,128)(2,1)S(1)}, bf16[400,128]{1,0:T(8,128)(2,1)S(1)}, u32[]{:S(2)}, u32[]{:S(2)}) collective-permute-start(bf16[400,128]{1,0:T(8,128)(2,1)S(1)} %add_convert_fusion), channel_id=1, source_target_pairs={{0,2},{1,3},{2,0},{3,1},{4,68},{5,69},{6,70},{7,71},{8,10},{9,11},... | collective-permute-start | bytes 307208 | tf_op jit(solution)/shard_map/ppermute | solution.py:726
  159.9 0.9 collective-permute-start.12
  160.8 0.0 collective-permute-start.10
  160.8 2.2 %collective-permute-done.11 = bf16[400,128]{1,0:T(8,128)(2,1)S(1)} collective-permute-done((bf16[400,128]{1,0:T(8,128)(2,1)S(1)}, bf16[400,128]{1,0:T(8,128)(2,1)S(1)}, u32[]{:S(2)}, u32[]{:S(2)}) %collective-permute-start.11) | collective-permute-done | bytes 102432 | tf_op jit(solution)/shard_map/ppermute | solution.py:726
  163.0 1.6 collective-permute-done.12
  164.6 0.0 collective-permute-done.10
  164.6 0.1 select_select_fusion.3
  164.7 0.0 copy-start.1
  164.7 6.0 %collective-permute-start.13 = (bf16[1600,128]{1,0:T(8,128)(2,1)S(1)}, bf16[1600,128]{1,0:T(8,128)(2,1)S(1)}, u32[]{:S(2)}, u32[]{:S(2)}) collective-permute-start(bf16[1600,128]{1,0:T(8,128)(2,1)S(1)} %pad_maximum_fusion.mine), channel_id=1, source_target_pairs={{0,4},{4,0},{8,12},{12,8},{16,20},{20,16},{24,28},{28,24},{32,36},... | collective-permute-start | bytes 1228808 | tf_op jit(solution)/shard_map/ppermute | solution.py:730
  170.7 1.4 collective-permute-done.13.other
  172.1 0.7 copy-done.2
  172.9 2.4 %shard_map.207 = (f32[2,512,128]{2,1,0:T(8,128)}, f32[2,128,512]{2,1,0:T(8,128)}, f32[2,128,384]{2,1,0:T(8,128)}, f32[2,128,128]{2,1,0:T(8,128)}, f32[2,2,128]{2...) custom-call(s32[1]{0:T(128)} %bitcast.6.core_ref, bf16[1600,128]{1,0:T(8,128)(2,1)} %copy-done.1, ...), custom_call_target="tpu_custom_call" | custom-call | tf_op jit(solution)/shard_map/pallas_call | solution.py:698
  175.3 1.3 copy.24
  (5 shorter events, 0.0 us)
Async XLA Ops:
  0.6 9.6 %copy-start.3 = (s32[1,1,64]{2,1,0:T(1,128)S(1)}, s32[1,1,64]{2,1,0:T(1,128)}, u32[]{:S(2)}) copy-start(s32[1,1,64]{2,1,0:T(1,128)} %param.16) | copy-start | bytes 772
  0.7 37.9 %all-to-all-start = ((bf16[64,128,128]{2,1,0:T(8,128)(2,1)}), bf16[64,128,128]{2,1,0:T(8,128)(2,1)S(1)}, u32[]{:S(2)}, u32[]{:S(2)}) async-start(bf16[64,128,128]{2,1,0:T(8,128)(2,1)} %bitcast.11), calls=%async_computation | async-start | bytes 4194304 | tf_op jit(solution)/shard_map/all_to_all | solution.py:764
  38.6 1.3 copy-start
  94.3 37.2 %all-to-all-start.1 = ((bf16[64,128,128]{2,1,0:T(8,128)(2,1)}), bf16[64,128,128]{2,1,0:T(8,128)(2,1)S(1)}, u32[]{:S(2)}, u32[]{:S(2)}) async-start(bf16[64,128,128]{2,1,0:T(8,128)(2,1)} %get-tuple-element.39), calls=%async_computation.1 | async-start | bytes 4194304 | tf_op jit(solution)/shard_map/all_to_all | solution.py:769
  131.5 2.0 %collective-permute-start = (bf16[1600,128]{1,0:T(8,128)(2,1)}, bf16[1600,128]{1,0:T(8,128)(2,1)S(1)}, u32[]{:S(2)}, u32[]{:S(2)}) collective-permute-start(bf16[1600,128]{1,0:T(8,128)(2,1)} %get-tuple-element.57), channel_id=1, source_target_pairs={{0,4},{4,0},{8,12},{12,8},{16,20},{20,16},{24,28},{28,24},{32,36},... | collective-permute-start | bytes 1228808 | tf_op jit(solution)/shard_map/ppermute | solution.py:730
  134.8 5.4 %collective-permute-start.3 = (bf16[400,128]{1,0:T(8,128)(2,1)S(1)}, bf16[400,128]{1,0:T(8,128)(2,1)S(1)}, u32[]{:S(2)}, u32[]{:S(2)}) collective-permute-start(bf16[400,128]{1,0:T(8,128)(2,1)S(1)} %get-tuple-element.69), channel_id=1, source_target_pairs={{0,3},{1,2},{2,1},{3,0},{4,100},{5,101},{6,102},{7,103},{8,11},{9,... | collective-permute-start | bytes 307208 | tf_op jit(solution)/shard_map/ppermute | solution.py:726
  137.5 5.3 %collective-permute-start.2 = (bf16[400,128]{1,0:T(8,128)(2,1)S(1)}, bf16[400,128]{1,0:T(8,128)(2,1)S(1)}, u32[]{:S(2)}, u32[]{:S(2)}) collective-permute-start(bf16[400,128]{1,0:T(8,128)(2,1)S(1)} %get-tuple-element.70), channel_id=1, source_target_pairs={{0,2},{1,3},{2,0},{3,1},{4,68},{5,69},{6,70},{7,71},{8,10},{9,11},... | collective-permute-start | bytes 307208 | tf_op jit(solution)/shard_map/ppermute | solution.py:726
  138.1 4.8 %collective-permute-start.1 = (bf16[400,128]{1,0:T(8,128)(2,1)S(1)}, bf16[400,128]{1,0:T(8,128)(2,1)S(1)}, u32[]{:S(2)}, u32[]{:S(2)}) collective-permute-start(bf16[400,128]{1,0:T(8,128)(2,1)S(1)} %get-tuple-element.68), channel_id=1, source_target_pairs={{0,1},{1,0},{2,3},{3,2},{4,36},{5,37},{6,38},{7,39},{8,9},{9,8},{1... | collective-permute-start | bytes 307208 | tf_op jit(solution)/shard_map/ppermute | solution.py:726
  142.9 4.8 %collective-permute-start.6 = (bf16[400,128]{1,0:T(8,128)(2,1)S(1)}, bf16[400,128]{1,0:T(8,128)(2,1)S(1)}, u32[]{:S(2)}, u32[]{:S(2)}) collective-permute-start(bf16[400,128]{1,0:T(8,128)(2,1)S(1)} %get-tuple-element.66), channel_id=1, source_target_pairs={{0,96},{1,97},{2,98},{3,99},{4,28},{5,29},{6,30},{7,31},{8,104},{9... | collective-permute-start | bytes 307208 | tf_op jit(solution)/shard_map/ppermute | solution.py:726
  145.1 5.0 %collective-permute-start.5 = (bf16[400,128]{1,0:T(8,128)(2,1)S(1)}, bf16[400,128]{1,0:T(8,128)(2,1)S(1)}, u32[]{:S(2)}, u32[]{:S(2)}) collective-permute-start(bf16[400,128]{1,0:T(8,128)(2,1)S(1)} %get-tuple-element.66), channel_id=1, source_target_pairs={{0,64},{1,65},{2,66},{3,67},{4,20},{5,21},{6,22},{7,23},{8,72},{9,... | collective-permute-start | bytes 307208 | tf_op jit(solution)/shard_map/ppermute | solution.py:726
  145.7 4.5 %collective-permute-start.4 = (bf16[400,128]{1,0:T(8,128)(2,1)S(1)}, bf16[400,128]{1,0:T(8,128)(2,1)S(1)}, u32[]{:S(2)}, u32[]{:S(2)}) collective-permute-start(bf16[400,128]{1,0:T(8,128)(2,1)S(1)} %get-tuple-element.66), channel_id=1, source_target_pairs={{0,32},{1,33},{2,34},{3,35},{4,12},{5,13},{6,14},{7,15},{8,40},{9,... | collective-permute-start | bytes 307208 | tf_op jit(solution)/shard_map/ppermute | solution.py:726
  150.2 5.3 %collective-permute-start.9 = (bf16[400,128]{1,0:T(8,128)(2,1)S(1)}, bf16[400,128]{1,0:T(8,128)(2,1)S(1)}, u32[]{:S(2)}, u32[]{:S(2)}) collective-permute-start(bf16[400,128]{1,0:T(8,128)(2,1)S(1)} %fusion), channel_id=1, source_target_pairs={{0,24},{1,25},{2,26},{3,27},{4,7},{5,6},{6,5},{7,4},{8,16},{9,17},... | collective-permute-start | bytes 307208 | tf_op jit(solution)/shard_map/ppermute | solution.py:726
  152.8 5.0 %collective-permute-start.8 = (bf16[400,128]{1,0:T(8,128)(2,1)S(1)}, bf16[400,128]{1,0:T(8,128)(2,1)S(1)}, u32[]{:S(2)}, u32[]{:S(2)}) collective-permute-start(bf16[400,128]{1,0:T(8,128)(2,1)S(1)} %fusion), channel_id=1, source_target_pairs={{0,16},{1,17},{2,18},{3,19},{4,6},{5,7},{6,4},{7,5},{8,24},{9,25},... | collective-permute-start | bytes 307208 | tf_op jit(solution)/shard_map/ppermute | solution.py:726
  153.3 4.5 %collective-permute-start.7 = (bf16[400,128]{1,0:T(8,128)(2,1)S(1)}, bf16[400,128]{1,0:T(8,128)(2,1)S(1)}, u32[]{:S(2)}, u32[]{:S(2)}) collective-permute-start(bf16[400,128]{1,0:T(8,128)(2,1)S(1)} %fusion), channel_id=1, source_target_pairs={{0,8},{1,9},{2,10},{3,11},{4,5},{5,4},{6,7},{7,6},{8,0},{9,1},{10,... | collective-permute-start | bytes 307208 | tf_op jit(solution)/shard_map/ppermute | solution.py:726
  157.9 5.1 %collective-permute-start.11 = (bf16[400,128]{1,0:T(8,128)(2,1)S(1)}, bf16[400,128]{1,0:T(8,128)(2,1)S(1)}, u32[]{:S(2)}, u32[]{:S(2)}) collective-permute-start(bf16[400,128]{1,0:T(8,128)(2,1)S(1)} %add_convert_fusion), channel_id=1, source_target_pairs={{0,2},{1,3},{2,0},{3,1},{4,68},{5,69},{6,70},{7,71},{8,10},{9,11},... | collective-permute-start | bytes 307208 | tf_op jit(solution)/shard_map/ppermute | solution.py:726
  159.9 4.7 %collective-permute-start.12 = (bf16[400,128]{1,0:T(8,128)(2,1)S(1)}, bf16[400,128]{1,0:T(8,128)(2,1)S(1)}, u32[]{:S(2)}, u32[]{:S(2)}) collective-permute-start(bf16[400,128]{1,0:T(8,128)(2,1)S(1)} %add_convert_fusion), channel_id=1, source_target_pairs={{0,3},{1,2},{2,1},{3,0},{4,100},{5,101},{6,102},{7,103},{8,11},{9,... | collective-permute-start | bytes 307208 | tf_op jit(solution)/shard_map/ppermute | solution.py:726
  160.8 3.9 %collective-permute-start.10 = (bf16[400,128]{1,0:T(8,128)(2,1)S(1)}, bf16[400,128]{1,0:T(8,128)(2,1)S(1)}, u32[]{:S(2)}, u32[]{:S(2)}) collective-permute-start(bf16[400,128]{1,0:T(8,128)(2,1)S(1)} %add_convert_fusion), channel_id=1, source_target_pairs={{0,1},{1,0},{2,3},{3,2},{4,36},{5,37},{6,38},{7,39},{8,9},{9,8},{1... | collective-permute-start | bytes 307208 | tf_op jit(solution)/shard_map/ppermute | solution.py:726
  164.7 7.4 %copy-start.1 = (bf16[1600,128]{1,0:T(8,128)(2,1)}, bf16[1600,128]{1,0:T(8,128)(2,1)S(1)}, u32[]{:S(2)}) copy-start(bf16[1600,128]{1,0:T(8,128)(2,1)S(1)} %pad_maximum_fusion.mine) | copy-start | bytes 1228804
  164.7 7.4 %collective-permute-start.13 = (bf16[1600,128]{1,0:T(8,128)(2,1)S(1)}, bf16[1600,128]{1,0:T(8,128)(2,1)S(1)}, u32[]{:S(2)}, u32[]{:S(2)}) collective-permute-start(bf16[1600,128]{1,0:T(8,128)(2,1)S(1)} %pad_maximum_fusion.mine), channel_id=1, source_target_pairs={{0,4},{4,0},{8,12},{12,8},{16,20},{20,16},{24,28},{28,24},{32,36},... | collective-permute-start | bytes 1228808 | tf_op jit(solution)/shard_map/ppermute | solution.py:730
  172.1 0.8 copy-start.2
